TPU v7x, 32 devices: a whole 2x2x4 slice. The times are simulated.
32 devices in a mesh: lon: 8 (over y, x, core), lat: 4 (over z).
Axes of the slice: x: 2, y: 2, z: 4, core: 2. Of those that a mesh axis runs over, the one named last changes fastest.
Arguments:
- queries: bfloat16 [32, 128, 1536], P('lat', 'lon'), may hold values from -24 to 24
- keys: bfloat16 [32, 128, 1536], P('lat', 'lon'), may hold values from -24 to 24
- values: bfloat16 [32, 128, 1536], P('lat', 'lon'), may hold values from -6 to 6
- out_grad: bfloat16 [32, 128, 1536], P('lat', 'lon'), may hold values from -6 to 6
- neighbours: int32 [32, 5], replicated, may hold values from -1 to 31, as said below
- partner: int32 [2, 8], replicated, may hold values from 0 to 7, as said below
Outputs:
- attended: bfloat16 [32, 128, 1536], P('lat', 'lon')
- grad_queries: bfloat16 [32, 128, 1536], P('lat', 'lon')
- grad_keys: bfloat16 [32, 128, 1536], P('lat', 'lon')
- grad_values: bfloat16 [32, 128, 1536], P('lat', 'lon')
Inputs may be any that keep to these rules, and one draw needn't show every extreme that they name: `neighbours`: row t = b * 8 + s lists, in some order and padded with -1, distinct tiles: t itself always, and any of b * 8 + (s - 1) mod 8, b * 8 + (s + 1) mod 8, t - 8 where b > 0 and t + 8 where b < 3. Rows of the first and the last band list all of those that exist. Each row is a permutation of the strips, and partner[j, s] - s - 4 is -1, 0 or 1 modulo 8.
All inputs are finite; a program needn't handle non-finite values.
Results may differ from a plain program's by a relative error of at most 0.022.
Values may be sent and summed in bfloat16 or wider, within the bound.
No kernel may reach another device: no remote copies, remote signals or barrier semaphores. Data moves between devices by JAX's collectives and lax.ppermute only.
A program may use at most 64 MiB of HBM per device.

v0:
```python
import jax
import jax.numpy as jnp
from jax import lax
from jax.sharding import PartitionSpec as P

DH = 128


def with_halo(cells, sides, width, closed):
    for axis, dim in sides:
        count = lax.axis_size(axis)
        ends = count if closed else count - 1
        head = lax.slice_in_dim(cells, 0, width, axis=dim)
        tail = lax.slice_in_dim(cells, cells.shape[dim] - width, cells.shape[dim], axis=dim)
        cells = jnp.concatenate(
            [
                lax.ppermute(tail, axis, [(i, (i + 1) % count) for i in range(ends)]),
                cells,
                lax.ppermute(head, axis, [((i + 1) % count, i) for i in range(ends)]),
            ],
            axis=dim,
        )
    return cells


def partner_2(x, axis, apart):
    return lax.ppermute(x, axis, [(i, i ^ 1 << apart) for i in range(lax.axis_size(axis))])


def body(queries, keys, values, out_grad, neighbours, partner):
    lat_count = lax.axis_size("lat")
    lon_count = lax.axis_size("lon")
    band_index = lax.axis_index("lat")
    strip_index = lax.axis_index("lon")
    tile_rows, tile_cols, feature_width = queries.shape
    tokens = tile_rows * tile_cols
    head_count = feature_width // DH
    scale = DH ** (-0.5)
    half_cycle = lon_count // 2
    top_bit = lon_count.bit_length() - 2
    query = queries.reshape(tokens, head_count, DH)
    cotan = out_grad.reshape(tokens, head_count, DH)
    polar_band = (band_index == 0) | (band_index == lat_count - 1)
    partner_row = jnp.where(band_index == 0, partner[0], partner[1])

    def tile_id(band_id, strip_id):
        return band_id * lon_count + strip_id

    west_strip = (strip_index - 1) % lon_count
    east_strip = (strip_index + 1) % lon_count
    opposite = (strip_index + half_cycle) % lon_count
    has_north = band_index > 0
    has_south = band_index < lat_count - 1
    my_id = tile_id(band_index, strip_index)
    west_id = tile_id(band_index, west_strip)
    east_id = tile_id(band_index, east_strip)
    north_id = jnp.where(has_north, my_id - lon_count, -7)
    south_id = jnp.where(has_south, my_id + lon_count, -7)
    candidates = jnp.stack([my_id, west_id, east_id, north_id, south_id])
    my_links = neighbours[my_id]
    present = jnp.any(candidates[:, None] == my_links[None, :], axis=1)
    present = jnp.concatenate([present, polar_band[None]])
    mask_bias = jnp.where(present, 0.0, -jnp.inf).astype(jnp.float32)
    pair_block = jnp.stack([keys, values]).reshape(1, 1, 2, tokens, feature_width)
    near = with_halo(pair_block, (("lon", 1), ("lat", 0)), 1, True)
    self_pair = near[1, 1]
    west_pair = near[1, 0]
    east_pair = near[1, 2]
    north_pair = near[0, 1]
    south_pair = near[2, 1]
    target = partner_row[opposite]
    differ = (target - opposite - half_cycle) % lon_count
    facing = jnp.where(differ == lon_count - 1, -1, differ)
    send_pair = jnp.where(facing == -1, west_pair, jnp.where(facing == 0, self_pair, east_pair))
    polar_pair = partner_2(send_pair, "lon", top_bit)
    stacked = jnp.stack([self_pair, west_pair, east_pair, north_pair, south_pair, polar_pair])
    near_keys = stacked[:, 0].reshape(6, tokens, head_count, DH)
    near_values = stacked[:, 1].reshape(6, tokens, head_count, DH)
    scores = (
        jnp.einsum("qhd,jkhd->hqjk", query, near_keys, preferred_element_type=jnp.float32) * scale
    )
    scores = scores + mask_bias[None, None, :, None]
    highest = jnp.max(scores, axis=(2, 3), keepdims=True)
    total = jnp.sum(jnp.exp(scores - highest), axis=(2, 3), keepdims=True)
    log_norm = highest + jnp.log(total)
    probability = jnp.exp(scores - log_norm)
    weights = probability.astype(jnp.bfloat16)
    attended = jnp.einsum(
        "hqjk,jkhd->qhd", weights, near_values, preferred_element_type=jnp.float32
    ).astype(jnp.bfloat16)
    delta = jnp.sum(cotan.astype(jnp.float32) * attended.astype(jnp.float32), axis=-1)
    dprob = jnp.einsum("qhd,jkhd->hqjk", cotan, near_values, preferred_element_type=jnp.float32)
    dscore = (probability * (dprob - delta.T[:, :, None, None])).astype(jnp.bfloat16)
    grad_query = (
        scale * jnp.einsum("hqjk,jkhd->qhd", dscore, near_keys, preferred_element_type=jnp.float32)
    ).astype(jnp.bfloat16)

    def tile_terms(first, count):
        score_part = lax.slice_in_dim(dscore, first, first + count, axis=2)
        weight_part = lax.slice_in_dim(weights, first, first + count, axis=2)
        key_part = jnp.einsum(
            "hqjk,qhd->jkhd", score_part, query, preferred_element_type=jnp.float32
        )
        value_part = jnp.einsum(
            "hqjk,qhd->jkhd", weight_part, cotan, preferred_element_type=jnp.float32
        )
        return jnp.stack([key_part, value_part], axis=1)

    polar_terms = tile_terms(5, 1)[0]
    returned = partner_2(polar_terms.astype(jnp.bfloat16), "lon", top_bit).astype(polar_terms.dtype)
    zeros_like = jnp.zeros_like(returned)
    self_term = tile_terms(0, 1)[0] + jnp.where(facing == 0, returned, zeros_like)
    cycle_terms = tile_terms(1, 2)
    west_term = cycle_terms[0] + jnp.where(facing == -1, returned, zeros_like)
    east_term = cycle_terms[1] + jnp.where(facing == 1, returned, zeros_like)
    cycle_block = jnp.stack([west_term, east_term])[None]
    cycle_back = with_halo(cycle_block.astype(jnp.bfloat16), (("lon", 1),), 1, True).astype(
        cycle_block.dtype
    )
    band_block = tile_terms(3, 2)[:, None]
    band_back = with_halo(band_block.astype(jnp.bfloat16), (("lat", 0),), 1, False).astype(
        band_block.dtype
    )
    summed = self_term + cycle_back[0, 0] + cycle_back[0, 3] + band_back[0, 0] + band_back[3, 0]
    key_sum = summed[0]
    value_sum = summed[1]
    grad_keys = (scale * key_sum).astype(jnp.bfloat16)
    grad_values = value_sum.astype(jnp.bfloat16)
    out_shape = (tile_rows, tile_cols, feature_width)
    return (
        attended.reshape(out_shape),
        grad_query.reshape(out_shape),
        grad_keys.reshape(out_shape),
        grad_values.reshape(out_shape),
    )


def solution(mesh):
    return jax.shard_map(
        body,
        mesh=mesh,
        in_specs=(
            P("lat", "lon", None),
            P("lat", "lon", None),
            P("lat", "lon", None),
            P("lat", "lon", None),
            P(),
            P(),
        ),
        out_specs=(
            P("lat", "lon", None),
            P("lat", "lon", None),
            P("lat", "lon", None),
            P("lat", "lon", None),
        ),
        check_vma=False,
    )
```

profile of v0, /device:TPU:0, one launch (start us, length us, event | category | flops | bytes accessed | tf_op | source)
XLA Modules:
  0.0 203.4 jit_solution(3077519336964575243)
XLA Ops:
  0.6 1.2 pad_maximum_fusion.7
  1.9 0.5 collective-permute-start
  2.4 2.9 %collective-permute-start.1 = (bf16[1,1,2,128,1536]{4,3,2,1,0:T(8,128)(2,1)S(1)}, bf16[1,1,2,128,1536]{4,3,2,1,0:T(8,128)(2,1)S(1)}, u32[]{:S(2)}, u32[]{:S(2)}) collective-permute-start(bf16[1,1,2,128,1536]{4,3,2,1,0:T(8,128)(2,1)S(1)} %pad_maximum_fusion.7), channel_id=1, source_target_pairs={{4,0},{8,4},{12,8},{16,12},{20,16},{24,20},{28,24},{0,28},{5,1},{9... | collective-permute-start | bytes 2359304 | tf_op jit(solution)/shard_map/ppermute | solution.py:19
  5.3 15.4 %collective-permute-done = bf16[1,1,2,128,1536]{4,3,2,1,0:T(8,128)(2,1)S(1)} collective-permute-done((bf16[1,1,2,128,1536]{4,3,2,1,0:T(8,128)(2,1)S(1)}, bf16[1,1,2,128,1536]{4,3,2,1,0:T(8,128)(2,1)S(1)}, u32[]{:S(2)}, u32[]{:S(2)}) %collective-permute-start) | collective-permute-done | bytes 786464 | tf_op jit(solution)/shard_map/ppermute | solution.py:17
  20.7 1.5 collective-permute-done.1
  22.2 2.8 %pad_maximum_fusion = bf16[1,3,2,128,1536]{4,3,2,1,0:T(8,128)(2,1)} fusion(bf16[1,1,2,128,1536]{4,3,2,1,0:T(8,128)(2,1)S(1)} %collective-permute-done.1, bf16[1,1,1,128,1536]{4,3,2,1,0:T(8,128)(2,1)} %bitcast.195, bf16[1,1,1,128,1536]{4,3,2,1,0:T(8,128)(2,1)} %bitcast.199, bf16[1,1,2,128,1536]{4,3,2,1,0:T(8,128)(2,1)S(1)} %collective-permute-done), kind=kLoop, calls=%fused_computation.15 | loop fusion | flops 3538944 | bytes 4718592 | tf_op jit(solution)/shard_map/concatenate | solution.py:15
  25.0 1.6 collective-permute-start.2
  26.6 0.6 constant_dynamic-slice_fusion
  27.9 0.3 reshape.293
  28.2 1.1 copy.105
  29.3 1.3 reshape.291
  30.6 0.2 dynamic-slice_reduce_fusion
  30.8 0.1 stack.119
  30.9 0.2 compare_reduce_fusion
  31.1 2.3 %collective-permute-start.3 = (bf16[1,3,2,128,1536]{4,3,2,1,0:T(8,128)(2,1)}, bf16[1,3,2,128,1536]{4,3,2,1,0:T(8,128)(2,1)S(1)}, u32[]{:S(2)}, u32[]{:S(2)}) collective-permute-start(bf16[1,3,2,128,1536]{4,3,2,1,0:T(8,128)(2,1)} %pad_maximum_fusion), channel_id=1, source_target_pairs={{1,0},{2,1},{3,2},{0,3},{5,4},{6,5},{7,6},{4,7},{9,8},{10,9},{11,1... | collective-permute-start | bytes 7077896 | tf_op jit(solution)/shard_map/ppermute | solution.py:19
  33.4 0.1 add_select_fusion
  33.5 0.1 fusion.54
  33.6 2.7 %collective-permute-start.4 = (bf16[2,128,1536]{2,1,0:T(8,128)(2,1)S(1)}, bf16[2,128,1536]{2,1,0:T(8,128)(2,1)S(1)}, u32[]{:S(2)}, u32[]{:S(2)}) collective-permute-start(bf16[2,128,1536]{2,1,0:T(8,128)(2,1)S(1)} %fusion.54), channel_id=1, source_target_pairs={{0,16},{4,20},{8,24},{12,28},{16,0},{20,4},{24,8},{28,12},{1,17},{... | collective-permute-start | bytes 2359304 | tf_op jit(solution)/shard_map/ppermute | solution.py:27
  36.4 0.1 bitcast_dynamic-update-slice_fusion.1
  36.4 44.1 %collective-permute-done.2 = bf16[1,3,2,128,1536]{4,3,2,1,0:T(8,128)(2,1)} collective-permute-done((bf16[1,3,2,128,1536]{4,3,2,1,0:T(8,128)(2,1)}, bf16[1,3,2,128,1536]{4,3,2,1,0:T(8,128)(2,1)}, u32[]{:S(2)}, u32[]{:S(2)}) %collective-permute-start.2) | collective-permute-done | bytes 2359328 | tf_op jit(solution)/shard_map/ppermute | solution.py:17
  80.6 1.2 fusion.53
  81.8 49.9 %collective-permute-done.3 = bf16[1,3,2,128,1536]{4,3,2,1,0:T(8,128)(2,1)S(1)} collective-permute-done((bf16[1,3,2,128,1536]{4,3,2,1,0:T(8,128)(2,1)}, bf16[1,3,2,128,1536]{4,3,2,1,0:T(8,128)(2,1)S(1)}, u32[]{:S(2)}, u32[]{:S(2)}) %collective-permute-start.3) | collective-permute-done | bytes 2359328 | tf_op jit(solution)/shard_map/ppermute | solution.py:19
  131.7 0.1 bitcast_dynamic-update-slice_fusion
  131.8 1.9 fusion.73
  133.7 2.4 %copy.97 = bf16[6,1,128,1536]{2,3,0,1:T(8,128)(2,1)} copy(bf16[6,1,128,1536]{3,2,1,0:T(8,128)(2,1)S(1)} %get-tuple-element.9) | data formatting | bytes 4718592 | tf_op jit(solution)/shard_map/slice | solution.py:78
  136.1 3.0 %copy.98 = bf16[6,1,128,1536]{2,3,0,1:T(8,128)(2,1)S(1)} copy(bf16[6,1,128,1536]{3,2,1,0:T(8,128)(2,1)} %get-tuple-element.8) | data formatting | bytes 4718592 | tf_op jit(solution)/shard_map/slice | solution.py:77
  139.2 1.2 bitcast_reduce_fusion
  140.3 1.0 fusion.2
  141.4 1.0 fusion.4
  142.4 1.3 fusion.43
  143.7 1.5 multiply_reduce_fusion
  145.2 1.9 fusion
  147.1 1.3 fusion.42
  148.4 1.4 fusion.74
  149.7 1.3 fusion.75
  151.0 2.2 %copy.102 = bf16[128,12,128]{2,1,0:T(8,128)(2,1)} copy(bf16[128,12,128]{0,2,1:T(8,128)(2,1)} %get-tuple-element.21) | data formatting | bytes 786432 | tf_op jit(solution)/shard_map/convert_element_type | solution.py:90
  153.1 2.1 %reshape.292 = bf16[8,16,1536]{2,1,0:T(8,128)(2,1)} reshape(bf16[128,12,128]{2,1,0:T(8,128)(2,1)} %copy.102) | data formatting | bytes 786432 | tf_op jit(solution)/shard_map/reshape | solution.py:131
  155.2 1.3 maximum_bitcast_fusion.3
  156.5 1.8 collective-permute-start.5
  158.3 1.5 convolution_convert_fusion.1
  159.8 0.4 convolution_convert_fusion
  160.2 1.3 fusion.50
  161.4 1.5 collective-permute-start.9
  162.9 5.4 %collective-permute-start.8 = (bf16[1,1,2,128,12,128]{5,3,4,2,1,0:T(8,128)(2,1)}, bf16[1,1,2,128,12,128]{5,3,4,2,1,0:T(8,128)(2,1)}, u32[]{:S(2)}, u32[]{:S(2)}) collective-permute-start(bf16[1,1,2,128,12,128]{5,3,4,2,1,0:T(8,128)(2,1)} %get-tuple-element.16), channel_id=1, source_target_pairs={{0,1},{1,2},{2,3},{4,5},{5,6},{6,7},{8,9},{9,10},{10,11},{12,13},{... | collective-permute-start | bytes 2359304 | tf_op jit(solution)/shard_map/ppermute | solution.py:17
  168.4 0.4 convolution_bitcast_fusion.1
  168.7 0.4 convolution_bitcast_fusion
  169.1 7.0 %collective-permute-done.5 = bf16[2,128,12,128]{3,1,2,0:T(8,128)(2,1)S(1)} collective-permute-done((bf16[2,128,12,128]{3,1,2,0:T(8,128)(2,1)S(1)}, bf16[2,128,12,128]{3,1,2,0:T(8,128)(2,1)S(1)}, u32[]{:S(2)}, u32[]{:S(2)}) %collective-permute-start.5) | collective-permute-done | bytes 786464 | tf_op jit(solution)/shard_map/ppermute | solution.py:27
  176.1 1.7 fusion.21
  177.8 0.7 collective-permute-start.7
  178.4 1.5 fusion.44
  180.0 1.4 copy.107
  181.4 1.0 reshape.294
  182.4 1.3 convolution_bitcast_fusion.2
  183.7 1.4 convolution_bitcast_fusion.3
  185.1 1.5 maximum_bitcast_fusion.1
  186.7 9.7 %collective-permute-done.7 = bf16[1,1,2,128,12,128]{5,3,4,2,1,0:T(8,128)(2,1)} collective-permute-done((bf16[1,1,2,128,12,128]{5,3,4,2,1,0:T(8,128)(2,1)}, bf16[1,1,2,128,12,128]{5,3,4,2,1,0:T(8,128)(2,1)}, u32[]{:S(2)}, u32[]{:S(2)}) %collective-permute-start.7) | collective-permute-done | bytes 786464 | tf_op jit(solution)/shard_map/ppermute | solution.py:19
  196.4 2.0 collective-permute-done.6
  198.4 2.2 %fusion.19 = f32[2,128,12,128]{3,1,2,0:T(8,128)S(1)} fusion(bf16[2,128,12,128]{3,1,2,0:T(8,128)(2,1)S(1)} %copy-done.9, f32[1,1,128,12,128]{4,2,3,1,0:T(8,128)S(1)} %convolution_bitcast_fusion.2, f32[1,1,128,12,128]{4,2,3,1,0:T(8,128)S(1)} %convolution_bitcast_fusion.3, bf16[1,1,2,128,12,128]{5,3,4,2,1,0:T(8,128)(2,1)} %collective-permute-done.9, ...), kind=kLoop, calls=%fused_computation.28 | loop fusion | flops 13369344 | bytes 10223617 | tf_op jit(solution)/shard_map/add | solution.py:124
  200.6 0.1 fusion.51
  200.7 0.1 slice.153
  200.8 0.3 copy.122
  201.1 1.0 convert_element_type.110
  202.1 0.3 copy.123
  202.4 1.0 convert_element_type.111
  (47 shorter events, 0.3 us)
Async XLA Ops:
  0.6 30.0 %copy-start = (s32[32,5]{0,1:T(8,128)S(1)}, s32[32,5]{0,1:T(8,128)}, u32[]{:S(2)}) copy-start(s32[32,5]{0,1:T(8,128)} %param.10) | copy-start | bytes 1924
  1.8 24.8 %copy-start.18 = (s32[2,8]{1,0:T(2,128)S(1)}, s32[2,8]{1,0:T(2,128)}, u32[]{:S(2)}) copy-start(s32[2,8]{1,0:T(2,128)} %param.11) | copy-start | bytes 196
  1.9 26.1 %copy-start.16 = (bf16[8,16,1536]{2,1,0:T(8,128)(2,1)S(1)}, bf16[8,16,1536]{2,1,0:T(8,128)(2,1)}, u32[]{:S(2)}) copy-start(bf16[8,16,1536]{2,1,0:T(8,128)(2,1)} %param.9) | copy-start | bytes 1179652
  1.9 18.8 %collective-permute-start = (bf16[1,1,2,128,1536]{4,3,2,1,0:T(8,128)(2,1)S(1)}, bf16[1,1,2,128,1536]{4,3,2,1,0:T(8,128)(2,1)S(1)}, u32[]{:S(2)}, u32[]{:S(2)}) collective-permute-start(bf16[1,1,2,128,1536]{4,3,2,1,0:T(8,128)(2,1)S(1)} %pad_maximum_fusion.7), channel_id=1, source_target_pairs={{0,4},{4,8},{8,12},{12,16},{16,20},{20,24},{24,28},{28,0},{1,5},{5... | collective-permute-start | bytes 2359304 | tf_op jit(solution)/shard_map/ppermute | solution.py:17
  2.4 19.8 %collective-permute-start.1 = (bf16[1,1,2,128,1536]{4,3,2,1,0:T(8,128)(2,1)S(1)}, bf16[1,1,2,128,1536]{4,3,2,1,0:T(8,128)(2,1)S(1)}, u32[]{:S(2)}, u32[]{:S(2)}) collective-permute-start(bf16[1,1,2,128,1536]{4,3,2,1,0:T(8,128)(2,1)S(1)} %pad_maximum_fusion.7), channel_id=1, source_target_pairs={{4,0},{8,4},{12,8},{16,12},{20,16},{24,20},{28,24},{0,28},{5,1},{9... | collective-permute-start | bytes 2359304 | tf_op jit(solution)/shard_map/ppermute | solution.py:19
  25.0 8.4 %copy-start.6 = (bf16[8,16,1536]{2,1,0:T(8,128)(2,1)S(1)}, bf16[8,16,1536]{2,1,0:T(8,128)(2,1)}, u32[]{:S(2)}) copy-start(bf16[8,16,1536]{2,1,0:T(8,128)(2,1)} %param.8) | copy-start | bytes 1179652
  25.0 8.4 %copy-start.7 = (bf16[8,16,1536]{2,1,0:T(8,128)(2,1)S(1)}, bf16[8,16,1536]{2,1,0:T(8,128)(2,1)}, u32[]{:S(2)}) copy-start(bf16[8,16,1536]{2,1,0:T(8,128)(2,1)} %param.7) | copy-start | bytes 1179652
  25.0 55.6 %collective-permute-start.2 = (bf16[1,3,2,128,1536]{4,3,2,1,0:T(8,128)(2,1)}, bf16[1,3,2,128,1536]{4,3,2,1,0:T(8,128)(2,1)}, u32[]{:S(2)}, u32[]{:S(2)}) collective-permute-start(bf16[1,3,2,128,1536]{4,3,2,1,0:T(8,128)(2,1)} %pad_maximum_fusion), channel_id=1, source_target_pairs={{0,1},{1,2},{2,3},{3,0},{4,5},{5,6},{6,7},{7,4},{8,9},{9,10},{10,1... | collective-permute-start | bytes 7077896 | tf_op jit(solution)/shard_map/ppermute | solution.py:17
  31.1 100.6 %collective-permute-start.3 = (bf16[1,3,2,128,1536]{4,3,2,1,0:T(8,128)(2,1)}, bf16[1,3,2,128,1536]{4,3,2,1,0:T(8,128)(2,1)S(1)}, u32[]{:S(2)}, u32[]{:S(2)}) collective-permute-start(bf16[1,3,2,128,1536]{4,3,2,1,0:T(8,128)(2,1)} %pad_maximum_fusion), channel_id=1, source_target_pairs={{1,0},{2,1},{3,2},{0,3},{5,4},{6,5},{7,6},{4,7},{9,8},{10,9},{11,1... | collective-permute-start | bytes 7077896 | tf_op jit(solution)/shard_map/ppermute | solution.py:19
  33.6 98.1 %collective-permute-start.4 = (bf16[2,128,1536]{2,1,0:T(8,128)(2,1)S(1)}, bf16[2,128,1536]{2,1,0:T(8,128)(2,1)S(1)}, u32[]{:S(2)}, u32[]{:S(2)}) collective-permute-start(bf16[2,128,1536]{2,1,0:T(8,128)(2,1)S(1)} %fusion.54), channel_id=1, source_target_pairs={{0,16},{4,20},{8,24},{12,28},{16,0},{20,4},{24,8},{28,12},{1,17},{... | collective-permute-start | bytes 2359304 | tf_op jit(solution)/shard_map/ppermute | solution.py:27
  141.3 2.3 %copy-start.15 = (bf16[6,1,128,1536]{2,3,0,1:T(8,128)(2,1)S(1)}, bf16[6,1,128,1536]{2,3,0,1:T(8,128)(2,1)}, u32[]{:S(2)}) copy-start(bf16[6,1,128,1536]{2,3,0,1:T(8,128)(2,1)} %copy.97) | copy-start | bytes 7077892
  141.3 2.3 %copy-start.17 = (bf16[128,12,128]{0,2,1:T(8,128)(2,1)S(1)}, bf16[128,12,128]{0,2,1:T(8,128)(2,1)}, u32[]{:S(2)}) copy-start(bf16[128,12,128]{0,2,1:T(8,128)(2,1)} %copy.105) | copy-start | bytes 1179652
  142.4 7.3 %copy-start.1 = (bf16[12,128,6,128]{1,3,2,0:T(8,128)(2,1)}, bf16[12,128,6,128]{1,3,2,0:T(8,128)(2,1)S(1)}, u32[]{:S(2)}) copy-start(bf16[12,128,6,128]{1,3,2,0:T(8,128)(2,1)S(1)} %fusion.4) | copy-start | bytes 7077892
  147.1 3.9 %copy-start.13 = (bf16[12,128,6,128]{1,3,2,0:T(8,128)(2,1)}, bf16[12,128,6,128]{1,3,2,0:T(8,128)(2,1)S(1)}, u32[]{:S(2)}) copy-start(bf16[12,128,6,128]{1,3,2,0:T(8,128)(2,1)S(1)} %fusion) | copy-start | bytes 7077892
  155.2 4.6 %copy-start.12 = (bf16[12,128,2,128]{1,3,2,0:T(8,128)(2,1)S(1)}, bf16[12,128,2,128]{1,3,2,0:T(8,128)(2,1)}, u32[]{:S(2)}) copy-start(bf16[12,128,2,128]{1,3,2,0:T(8,128)(2,1)} %get-tuple-element.15) | copy-start | bytes 2359300
  156.5 19.6 %collective-permute-start.5 = (bf16[2,128,12,128]{3,1,2,0:T(8,128)(2,1)S(1)}, bf16[2,128,12,128]{3,1,2,0:T(8,128)(2,1)S(1)}, u32[]{:S(2)}, u32[]{:S(2)}) collective-permute-start(bf16[2,128,12,128]{3,1,2,0:T(8,128)(2,1)S(1)} %maximum_bitcast_fusion.3), channel_id=1, source_target_pairs={{0,16},{4,20},{8,24},{12,28},{16,0},{20,4},{24,8},{28,12},{1,17},{... | collective-permute-start | bytes 2359304 | tf_op jit(solution)/shard_map/ppermute | solution.py:27
  159.7 1.7 copy-start.2
  159.8 8.6 %copy-start.10 = (bf16[12,128,2,128]{1,3,2,0:T(8,128)(2,1)S(1)}, bf16[12,128,2,128]{1,3,2,0:T(8,128)(2,1)}, u32[]{:S(2)}) copy-start(bf16[12,128,2,128]{1,3,2,0:T(8,128)(2,1)} %get-tuple-element.12) | copy-start | bytes 2359300
  160.1 8.6 %copy-start.4 = (bf16[12,2,128,128]{3,2,0,1:T(8,128)(2,1)}, bf16[12,2,128,128]{3,2,0,1:T(8,128)(2,1)S(1)}, u32[]{:S(2)}) copy-start(bf16[12,2,128,128]{3,2,0,1:T(8,128)(2,1)S(1)} %convolution_convert_fusion) | copy-start | bytes 2359300
  160.2 8.6 %copy-start.11 = (bf16[12,128,2,128]{1,3,2,0:T(8,128)(2,1)S(1)}, bf16[12,128,2,128]{1,3,2,0:T(8,128)(2,1)}, u32[]{:S(2)}) copy-start(bf16[12,128,2,128]{1,3,2,0:T(8,128)(2,1)} %get-tuple-element.14) | copy-start | bytes 2359300
  161.4 25.2 %collective-permute-start.9 = (bf16[1,1,2,128,12,128]{5,3,4,2,1,0:T(8,128)(2,1)}, bf16[1,1,2,128,12,128]{5,3,4,2,1,0:T(8,128)(2,1)}, u32[]{:S(2)}, u32[]{:S(2)}) collective-permute-start(bf16[1,1,2,128,12,128]{5,3,4,2,1,0:T(8,128)(2,1)} %get-tuple-element.17), channel_id=1, source_target_pairs={{1,0},{2,1},{3,2},{5,4},{6,5},{7,6},{9,8},{10,9},{11,10},{13,12},{... | collective-permute-start | bytes 2359304 | tf_op jit(solution)/shard_map/ppermute | solution.py:19
  162.9 23.8 %collective-permute-start.8 = (bf16[1,1,2,128,12,128]{5,3,4,2,1,0:T(8,128)(2,1)}, bf16[1,1,2,128,12,128]{5,3,4,2,1,0:T(8,128)(2,1)}, u32[]{:S(2)}, u32[]{:S(2)}) collective-permute-start(bf16[1,1,2,128,12,128]{5,3,4,2,1,0:T(8,128)(2,1)} %get-tuple-element.16), channel_id=1, source_target_pairs={{0,1},{1,2},{2,3},{4,5},{5,6},{6,7},{8,9},{9,10},{10,11},{12,13},{... | collective-permute-start | bytes 2359304 | tf_op jit(solution)/shard_map/ppermute | solution.py:17
  169.1 9.3 %copy-start.14 = (bf16[12,128,6,128]{1,3,2,0:T(8,128)(2,1)S(1)}, bf16[12,128,6,128]{1,3,2,0:T(8,128)(2,1)}, u32[]{:S(2)}) copy-start(bf16[12,128,6,128]{1,3,2,0:T(8,128)(2,1)} %copy-done.13) | copy-start | bytes 7077892
  176.1 1.7 copy-start.8
  177.8 18.6 %collective-permute-start.7 = (bf16[1,1,2,128,12,128]{5,3,4,2,1,0:T(8,128)(2,1)}, bf16[1,1,2,128,12,128]{5,3,4,2,1,0:T(8,128)(2,1)}, u32[]{:S(2)}, u32[]{:S(2)}) collective-permute-start(bf16[1,1,2,128,12,128]{5,3,4,2,1,0:T(8,128)(2,1)} %bitcast.65), channel_id=1, source_target_pairs={{4,0},{8,4},{12,8},{16,12},{20,16},{24,20},{28,24},{0,28},{5,1},{9... | collective-permute-start | bytes 2359304 | tf_op jit(solution)/shard_map/ppermute | solution.py:19
  178.4 20.0 %collective-permute-start.6 = (bf16[1,1,2,128,12,128]{5,3,4,2,1,0:T(8,128)(2,1)}, bf16[1,1,2,128,12,128]{5,3,4,2,1,0:T(8,128)(2,1)}, u32[]{:S(2)}, u32[]{:S(2)}) collective-permute-start(bf16[1,1,2,128,12,128]{5,3,4,2,1,0:T(8,128)(2,1)} %bitcast.60), channel_id=1, source_target_pairs={{0,4},{4,8},{8,12},{12,16},{16,20},{20,24},{24,28},{28,0},{1,5},{5... | collective-permute-start | bytes 2359304 | tf_op jit(solution)/shard_map/ppermute | solution.py:17
  183.7 14.7 %copy-start.3 = (bf16[12,2,128,128]{3,2,0,1:T(8,128)(2,1)S(1)}, bf16[12,2,128,128]{3,2,0,1:T(8,128)(2,1)}, u32[]{:S(2)}) copy-start(bf16[12,2,128,128]{3,2,0,1:T(8,128)(2,1)} %copy-done.2) | copy-start | bytes 2359300
  183.7 14.7 %copy-start.5 = (bf16[12,2,128,128]{3,2,0,1:T(8,128)(2,1)S(1)}, bf16[12,2,128,128]{3,2,0,1:T(8,128)(2,1)}, u32[]{:S(2)}) copy-start(bf16[12,2,128,128]{3,2,0,1:T(8,128)(2,1)} %copy-done.4) | copy-start | bytes 2359300
  183.7 14.7 %copy-start.9 = (bf16[2,128,12,128]{3,1,2,0:T(8,128)(2,1)S(1)}, bf16[2,128,12,128]{3,1,2,0:T(8,128)(2,1)}, u32[]{:S(2)}) copy-start(bf16[2,128,12,128]{3,1,2,0:T(8,128)(2,1)} %copy-done.8) | copy-start | bytes 2359300
where the time goes:
time: 204 us; the launch traced here: 203 us
  waiting for transfers between devices  130 us (64%)
  local copies, waits for them, and re-layouts  24.3 us (12%)
  starting transfers between devices  19.4 us (10%)
  other arithmetic  14.5 us (7%)
  matrix products  13.9 us (7%)
    ppermute x4, waiting for transfers between devices, with_halo(): lax.ppermute(tail, axis, [(i, (i + 1) % count) for i in range(ends)])  61.5 us
    ppermute x4, waiting for transfers between devices, with_halo(): lax.ppermute(head, axis, [((i + 1) % count, i) for i in range(ends)])  61.2 us
    ppermute x4, starting transfers between devices, with_halo(): lax.ppermute(tail, axis, [(i, (i + 1) % count) for i in range(ends)])  7.53 us
    ppermute x4, starting transfers between devices, with_halo(): lax.ppermute(head, axis, [((i + 1) % count, i) for i in range(ends)])  7.36 us
    ppermute x2, waiting for transfers between devices, partner_2(): lax.ppermute(x, axis, [(i, i ^ 1 << apart) for i in range(lax.axis_size(a...  6.97 us
    slice x2, local copies, waits for them, and re-layouts, body(): near_keys = stacked[:, 0].reshape(6, tokens, head_count, DH)  4.91 us
    dot_general x4, matrix products, tile_terms(): jnp.einsum('hqjk,qhd->jkhd', score_part, query, preferred_element_type=jn...  4.51 us
    ppermute x2, starting transfers between devices, partner_2(): lax.ppermute(x, axis, [(i, i ^ 1 << apart) for i in range(lax.axis_size(a...  4.46 us
  transfers between devices with their start and end apart: 10, of which 7 were waited for; matrix products, arithmetic and copies ran while one was open for 9% of the time, Pallas kernels for 0%

commit v1 on v0

v1 whole, which is shorter than its diff:
```python
import functools
import math

import jax
import jax.numpy as jnp
from jax import lax
from jax.experimental import pallas as pl
from jax.experimental.pallas import tpu as pltpu
from jax.sharding import PartitionSpec as P

DH = 128
CHUNKS = 1
STEP_HEADS = 2
LOW = -1e30
F32 = jnp.float32
BF16 = jnp.bfloat16


def dot_nt(a, b):
    return lax.dot_general(a, b, (((1,), (1,)), ((), ())), preferred_element_type=F32)


def dot_nn(a, b):
    return lax.dot_general(a, b, (((1,), (0,)), ((), ())), preferred_element_type=F32)


def dot_tn(a, b):
    return lax.dot_general(a, b, (((0,), (0,)), ((), ())), preferred_element_type=F32)


def rows(*parts):
    return jnp.concatenate(parts, axis=0)


def block_bias(flags, slot, tokens, both):
    own = jnp.where(flags[slot] > 0, 0.0, LOW).astype(F32)
    if not both:
        return jnp.full((1, tokens), own, F32)
    other = jnp.where(flags[8 + slot] > 0, 0.0, LOW).astype(F32)
    lane = lax.broadcasted_iota(jnp.int32, (1, 2 * tokens), 1)
    return jnp.where(lane < tokens, own, other)


def gathered(j, polar, q, k, v, g, near):
    cols = pl.ds(j * DH, DH)
    slots = near[:3] if polar else near
    kk = rows(k[:, cols], *[r[0, :, cols] for r in slots])
    vv = rows(v[:, cols], *[r[1, :, cols] for r in slots])
    qq, gg = q[:, cols], g[:, cols]
    if polar:
        qq = rows(qq, near[3][0, :, cols])
        gg = rows(gg, near[3][1, :, cols])
    return qq, gg, kk, vv


def stats_kernel(factor, heads, tokens, flags, q, k, v, g, n1, n2, n3, n4, out):
    near = (n1, n2, n3, n4)

    def work(polar):
        width = 2 * tokens if polar else tokens
        count = 4 if polar else 5
        bias = [block_bias(flags, b, tokens, polar) for b in range(count)]
        tops, sums, deltas = [], [], []
        for j in range(heads):
            qq, gg, kk, vv = gathered(j, polar, q, k, v, g, near)
            s = dot_nt(kk, qq)
            dp = dot_nt(vv, gg)
            parts = [s[b * tokens : (b + 1) * tokens] * factor + bias[b] for b in range(count)]
            top = functools.reduce(jnp.maximum, [jnp.max(x, axis=0, keepdims=True) for x in parts])
            total = jnp.zeros((1, width), F32)
            delta = jnp.zeros((1, width), F32)
            for b in range(count):
                e = jnp.exp2(parts[b] - top)
                total += jnp.sum(e, axis=0, keepdims=True)
                delta += jnp.sum(e * dp[b * tokens : (b + 1) * tokens], axis=0, keepdims=True)
            tops.append(top)
            sums.append(total)
            deltas.append(delta)
        stat = rows(*tops, *sums, *deltas)
        for r in range(3 * heads):
            out[0, r : r + 1, :width] = stat[r : r + 1]
        if out.shape[1] > 3 * heads:
            out[0, 3 * heads :, :] = jnp.zeros((out.shape[1] - 3 * heads, 2 * tokens), F32)
        if not polar:
            out[0, : 3 * heads, tokens:] = jnp.zeros((3 * heads, tokens), F32)

    pl.when(flags[7] > 0)(lambda: work(True))
    pl.when(flags[7] == 0)(lambda: work(False))


def grads_kernel(factor, heads, tokens, flags, mine, theirs, q, k, v, g, n1, n2, n3, n4, att, dq, dk, dv, r1, r2, r3, r4):
    near = (n1, n2, n3, n4)
    back = (r1, r2, r3, r4)

    def work(polar):
        width = 2 * tokens if polar else tokens
        count = 4 if polar else 5
        bias = [block_bias(flags, b, tokens, polar) for b in range(count)]
        for j in range(heads):
            cols = pl.ds(j * DH, DH)
            top, total, delta = [mine[0, r * heads + j : r * heads + j + 1, :width] for r in range(3)]
            if polar:
                top2, total2, delta2 = [
                    jnp.concatenate(
                        [
                            theirs[0, r * heads + j : r * heads + j + 1, tokens:],
                            theirs[0, r * heads + j : r * heads + j + 1, :tokens],
                        ],
                        axis=1,
                    )
                    for r in range(3)
                ]
                high = jnp.maximum(top, top2)
                a1, a2 = jnp.exp2(top - high), jnp.exp2(top2 - high)
                total = total * a1 + total2 * a2
                delta = delta * a1 + delta2 * a2
                top = high
            lse = top + jnp.log2(total)
            delta = delta / total
            qq, gg, kk, vv = gathered(j, polar, q, k, v, g, near)
            s = dot_nt(kk, qq)
            dp = dot_nt(vv, gg)
            ps = []
            for b in range(count):
                ps.append(jnp.exp2(s[b * tokens : (b + 1) * tokens] * factor + (bias[b] - lse)))
            p = rows(*ps)
            w = p.astype(BF16)
            ds = (p * (dp - delta)).astype(BF16)
            dkk = dot_nn(ds, qq)
            dvv = dot_nn(w, gg)
            o = dot_tn(vv, w).T
            dqq = dot_tn(kk, ds).T
            att[:, cols] = o[:tokens]
            dq[:, cols] = dqq[:tokens]
            dk[:, cols] = dkk[:tokens]
            dv[:, cols] = dvv[:tokens]
            for b in range(1, count):
                back[b - 1][0, :, cols] = dkk[b * tokens : (b + 1) * tokens].astype(BF16)
                back[b - 1][1, :, cols] = dvv[b * tokens : (b + 1) * tokens].astype(BF16)
            if polar:
                r4[0, :, cols] = o[tokens:].astype(BF16)
                r4[1, :, cols] = dqq[tokens:].astype(BF16)

    pl.when(flags[7] > 0)(lambda: work(True))
    pl.when(flags[7] == 0)(lambda: work(False))


def exchange_plan(lon_count, lat_count):
    half = lon_count // 2

    def polar(b):
        return b == 0 or b == lat_count - 1

    def second(b, s):
        ring, base = (half, s // half * half) if polar(b) else (lon_count, 0)
        place = s - base
        return base + (place - 1 if place % 2 == 0 else place + 1) % ring

    def fourth(b, s):
        if polar(b):
            return b, (s + half) % lon_count
        return (b - 1 if b % 2 == 0 else b + 1), s

    cells = [(b, s) for b in range(lat_count) for s in range(lon_count)]

    def pairs(move, chosen=cells):
        return [(s * lat_count + b, move(b, s)[1] * lat_count + move(b, s)[0]) for b, s in chosen]

    return (
        pairs(lambda b, s: (b, s ^ 1)),
        pairs(lambda b, s: (b, second(b, s))),
        pairs(lambda b, s: (b ^ 1, s)),
        pairs(fourth),
        pairs(fourth, [(b, s) for b, s in cells if polar(b)]),
    )


def link_flags(neighbours, partner, lon_count, lat_count):
    half = lon_count // 2
    b, s = lax.axis_index("lat"), lax.axis_index("lon")
    polar = (b == 0) | (b == lat_count - 1)
    first = s ^ 1
    ring = jnp.where(polar, half, lon_count)
    base = jnp.where(polar, s // half * half, 0)
    place = s - base
    second = base + (place + jnp.where(place % 2 == 0, ring - 1, 1)) % ring
    inner = jnp.where(b % 2 == 0, b - 1, b + 1)
    held = jnp.stack([
        b * lon_count + s,
        b * lon_count + first,
        b * lon_count + second,
        (b ^ 1) * lon_count + s,
        jnp.where(polar, -7, inner * lon_count + s),
    ])
    across = (s + half) % lon_count
    pole = jnp.where(b == 0, partner[0], partner[1])

    def links(strip):
        tile = b * lon_count + strip
        extra = jnp.where(polar, b * lon_count + pole[strip], -9)
        return jnp.concatenate([neighbours[tile], extra[None]])

    own = jnp.any(held[:, None] == links(s)[None, :], axis=1)
    other = jnp.any(held[:3, None] == links(across)[None, :], axis=1)
    parts = [own, jnp.zeros((2,), bool), polar[None], other, jnp.zeros((5,), bool)]
    return jnp.concatenate(parts).astype(jnp.int32), polar


def body(queries, keys, values, out_grad, neighbours, partner):
    lat_count, lon_count = lax.axis_size("lat"), lax.axis_size("lon")
    tile_rows, tile_cols, features = queries.shape
    tokens = tile_rows * tile_cols
    heads = features // DH
    scale = DH**-0.5
    factor = scale * math.log2(math.e)
    q, k, v, g = [x.reshape(tokens, features) for x in (queries, keys, values, out_grad)]
    p1, p2, p3, p4, swap = exchange_plan(lon_count, lat_count)
    axes = ("lon", "lat")
    flags, polar = link_flags(neighbours, partner, lon_count, lat_count)

    chunk_heads = heads // CHUNKS
    step_heads = STEP_HEADS
    steps = chunk_heads // step_heads
    wide = chunk_heads * DH
    block = step_heads * DH
    stat_rows = -(-3 * step_heads // 8) * 8
    params = pltpu.CompilerParams(vmem_limit_bytes=48 * 1024 * 1024)

    def compute(c, near):
        own = pl.BlockSpec((tokens, block), lambda i, f: (0, c * steps + i))
        pair = pl.BlockSpec((2, tokens, block), lambda i, f: (0, 0, i))
        flat = pl.BlockSpec((tokens, block), lambda i, f: (0, i))
        stat = pl.BlockSpec((1, stat_rows, 2 * tokens), lambda i, f: (i, 0, 0))
        stats = pl.pallas_call(
            functools.partial(stats_kernel, factor, step_heads, tokens),
            grid_spec=pltpu.PrefetchScalarGridSpec(
                num_scalar_prefetch=1,
                grid=(steps,),
                in_specs=[own] * 4 + [pair] * 4,
                out_specs=stat,
            ),
            out_shape=jax.ShapeDtypeStruct((steps, stat_rows, 2 * tokens), F32),
            compiler_params=params,
            name="stats",
        )(flags, q, k, v, g, *near)
        swapped = lax.ppermute(stats, axes, swap)
        whole = jax.ShapeDtypeStruct((tokens, wide), F32)
        term = jax.ShapeDtypeStruct((2, tokens, wide), BF16)
        return pl.pallas_call(
            functools.partial(grads_kernel, factor, step_heads, tokens),
            grid_spec=pltpu.PrefetchScalarGridSpec(
                num_scalar_prefetch=1,
                grid=(steps,),
                in_specs=[stat] * 2 + [own] * 4 + [pair] * 4,
                out_specs=[flat] * 4 + [pair] * 4,
            ),
            out_shape=[whole] * 4 + [term] * 4,
            compiler_params=params,
            name="grads",
        )(flags, stats, swapped, q, k, v, g, *near)

    outs = []
    for c in range(CHUNKS):
        cut = slice(c * wide, (c + 1) * wide)
        kv = jnp.stack([k[:, cut], v[:, cut]])
        qg = jnp.stack([q[:, cut], g[:, cut]])
        n1, n2, n3 = [lax.ppermute(kv, axes, p) for p in (p1, p2, p3)]
        n4 = lax.ppermute(jnp.where(polar, qg, kv), axes, p4)
        att, dq, dk, dv, t1, t2, t3, t4 = compute(c, (n1, n2, n3, n4))
        b1, b2, b3, b4 = [lax.ppermute(t, axes, p).astype(F32) for t, p in zip((t1, t2, t3, t4), (p1, p2, p3, p4))]
        fourth_q = jnp.where(polar, b4, 0.0)
        fourth_k = jnp.where(polar, 0.0, b4)
        outs.append((
            (att + fourth_q[0]).astype(BF16),
            (scale * (dq + fourth_q[1])).astype(BF16),
            (scale * (dk + b1[0] + b2[0] + b3[0] + fourth_k[0])).astype(BF16),
            (dv + b1[1] + b2[1] + b3[1] + fourth_k[1]).astype(BF16),
        ))
    shape = (tile_rows, tile_cols, features)
    return tuple(
        (parts[0] if CHUNKS == 1 else jnp.concatenate(parts, axis=1)).reshape(shape) for parts in zip(*outs)
    )


def solution(mesh):
    spec = P("lat", "lon", None)
    return jax.shard_map(
        body,
        mesh=mesh,
        in_specs=(spec,) * 4 + (P(),) * 2,
        out_specs=(spec,) * 4,
        check_vma=False,
    )
```

time: 204 us -> 73.1 us (0.36)
  waiting for transfers between devices: 130 us -> 35.7 us
  local copies, waits for them, and re-layouts: 24.3 us -> 1.03 us
  Pallas kernels: 0 us -> 15.4 us
  matrix products: 13.9 us -> 0 us
  starting transfers between devices: 19.4 us -> 11.6 us
  other arithmetic: 14.5 us -> 6.78 us
    ppermute x10 -> x9, waiting for transfers between devices: 130 us -> 35.7 us  [the longest x4 18.1 us: body(): lax.ppermute(t, axes, p).astype(F32)]
    pallas_call x0 -> x2, Pallas kernels: none -> 15.4 us  [the longest x1 9.13 us: compute(): pl.pallas_call(functools.partial(grads_kernel, factor, step_heads, tokens...]
    dot_general x12 -> x0, matrix products: 13.9 us -> none  [the longest x4 4.51 us: tile_terms(): jnp.einsum('hqjk,qhd->jkhd', score_part, query, preferred_element_type=jn...]
    slice x7 -> x0, local copies, waits for them, and re-layouts: 10.3 us -> none  [the longest x2 4.91 us: body(): near_keys = stacked[:, 0].reshape(6, tokens, head_count, DH)]
    ppermute x10 -> x9, starting transfers between devices: 19.4 us -> 11.6 us  [the longest x3 5.59 us: body(): n1, n2, n3 = [lax.ppermute(kv, axes, p) for p in (p1, p2, p3)]]
    convert_element_type x5 -> x0, local copies, waits for them, and re-layouts: 5.89 us -> none  [the longest x1 2.17 us: body(): attended = jnp.einsum('hqjk,jkhd->qhd', weights, near_values, preferred_e...]
    reshape x5 -> x0, local copies, waits for them, and re-layouts: 5.74 us -> none  [the longest x1 2.06 us: body(): attended.reshape(out_shape)]
    concatenate x2 -> x1, other arithmetic: 4.32 us -> 0.08 us  [links(): return jnp.concatenate([neighbours[tile], extra[None]])]
  transfers between devices with their start and end apart: 10 -> 9, of which waited for: 7 -> 7; matrix products, arithmetic and copies ran while one was open for 9% -> 4% of each run, Pallas kernels for 0% -> 0%
where the time goes in v1:
time: 73.1 us; the launch traced here: 72.7 us
  waiting for transfers between devices  35.7 us (49%)
  Pallas kernels  15.4 us (21%)
  starting transfers between devices  11.6 us (16%)
  other arithmetic  6.78 us (9%)
  between operations  2.16 us (3%)
  local copies, waits for them, and re-layouts  1.03 us (1%)
    ppermute x4, waiting for transfers between devices, body(): lax.ppermute(t, axes, p).astype(F32)  18.1 us
    ppermute x3, waiting for transfers between devices, body(): n1, n2, n3 = [lax.ppermute(kv, axes, p) for p in (p1, p2, p3)]  13.8 us
    pallas_call x1, Pallas kernels, compute(): pl.pallas_call(functools.partial(grads_kernel, factor, step_heads, tokens...  9.13 us
    pallas_call x1, Pallas kernels, compute(): pl.pallas_call(functools.partial(stats_kernel, factor, step_heads, tokens...  6.25 us
    ppermute x3, starting transfers between devices, body(): n1, n2, n3 = [lax.ppermute(kv, axes, p) for p in (p1, p2, p3)]  5.59 us
    ppermute x1, starting transfers between devices, compute(): swapped = lax.ppermute(stats, axes, swap)  3.43 us
    select_n x1, other arithmetic, body(): n4 = lax.ppermute(jnp.where(polar, qg, kv), axes, p4)  2.73 us
    ppermute x1, waiting for transfers between devices, compute(): swapped = lax.ppermute(stats, axes, swap)  2.55 us
  transfers between devices with their start and end apart: 9, of which 7 were waited for; matrix products, arithmetic and copies ran while one was open for 4% of the time, Pallas kernels for 0%

profile of v1, /device:TPU:0, one launch (start us, length us, event | category | flops | bytes accessed | tf_op | source)
XLA Modules:
  0.0 72.7 jit_solution(1286254089815693371)
XLA Ops:
  0.6 0.0 copy-start.7
  0.7 0.0 copy-start.6
  0.7 0.0 copy-start
  0.7 0.0 copy-start.1
  0.7 0.0 copy-start.2
  0.7 0.0 copy-start.3
  0.7 2.7 %maximum_select_fusion = (bf16[2,128,1536]{2,1,0:T(8,128)(2,1)}, bf16[2,128,1536]{2,1,0:T(8,128)(2,1)}) fusion(bf16[1,128,1536]{2,1,0:T(8,128)(2,1)} %bitcast.95, bf16[1,128,1536]{2,1,0:T(8,128)(2,1)} %bitcast.86, pred[]{:T(512)} %or.3, bf16[1,128,1536]{2,1,0:T(8,128)(2,1)} %bitcast.92, bf16[1,128,1536]{2,1,0:T(8,128)(2,1)} %bitcast.89), kind=kLoop, calls=%fused_computation.29 | loop fusion | flops 1179648 | bytes 3145729 | tf_op jit(solution)/shard_map/jit(_where)/select_n | solution.py:268
  3.4 0.5 collective-permute-start
  3.9 2.6 %collective-permute-start.1 = (bf16[2,128,1536]{2,1,0:T(8,128)(2,1)}, bf16[2,128,1536]{2,1,0:T(8,128)(2,1)S(1)}, u32[]{:S(2)}, u32[]{:S(2)}) collective-permute-start(bf16[2,128,1536]{2,1,0:T(8,128)(2,1)} %get-tuple-element.29), channel_id=1, source_target_pairs={{0,12},{4,8},{8,4},{12,0},{16,28},{20,24},{24,20},{28,16},{1,29},{... | collective-permute-start | bytes 2359304 | tf_op jit(solution)/shard_map/ppermute | solution.py:267
  6.5 2.5 %collective-permute-start.2 = (bf16[2,128,1536]{2,1,0:T(8,128)(2,1)}, bf16[2,128,1536]{2,1,0:T(8,128)(2,1)}, u32[]{:S(2)}, u32[]{:S(2)}) collective-permute-start(bf16[2,128,1536]{2,1,0:T(8,128)(2,1)} %get-tuple-element.29), channel_id=1, source_target_pairs={{0,1},{4,5},{8,9},{12,13},{16,17},{20,21},{24,25},{28,29},{1,0},{5... | collective-permute-start | bytes 2359304 | tf_op jit(solution)/shard_map/ppermute | solution.py:267
  9.0 0.5 collective-permute-start.3
  9.5 0.0 copy-done.7
  9.5 0.6 constant_dynamic-slice_fusion
  11.5 0.1 stack.31
  11.6 0.0 copy-done.6
  11.6 0.2 dynamic-slice_reduce_fusion
  11.8 0.1 pad_add_fusion.1
  11.9 0.1 pad_add_fusion
  11.9 0.2 compare_reduce_fusion
  12.1 0.2 compare_reduce_fusion.1
  12.3 0.1 concatenate.12
  12.4 0.0 collective-permute-done.n1
  12.5 0.0 copy-start.4
  12.5 12.2 %collective-permute-done.1.n2 = bf16[2,128,1536]{2,1,0:T(8,128)(2,1)S(1)} collective-permute-done((bf16[2,128,1536]{2,1,0:T(8,128)(2,1)}, bf16[2,128,1536]{2,1,0:T(8,128)(2,1)S(1)}, u32[]{:S(2)}, u32[]{:S(2)}) %collective-permute-start.1) | collective-permute-done | bytes 786464 | tf_op jit(solution)/shard_map/ppermute | solution.py:267
  24.6 0.0 copy-start.5
  24.6 1.6 %collective-permute-done.2.n3 = bf16[2,128,1536]{2,1,0:T(8,128)(2,1)} collective-permute-done((bf16[2,128,1536]{2,1,0:T(8,128)(2,1)}, bf16[2,128,1536]{2,1,0:T(8,128)(2,1)}, u32[]{:S(2)}, u32[]{:S(2)}) %collective-permute-start.2) | collective-permute-done | bytes 786464 | tf_op jit(solution)/shard_map/ppermute | solution.py:267
  26.3 1.3 %collective-permute-done.3.n4 = bf16[2,128,1536]{2,1,0:T(8,128)(2,1)} collective-permute-done((bf16[2,128,1536]{2,1,0:T(8,128)(2,1)}, bf16[2,128,1536]{2,1,0:T(8,128)(2,1)}, u32[]{:S(2)}, u32[]{:S(2)}) %collective-permute-start.3) | collective-permute-done | bytes 786464 | tf_op jit(solution)/shard_map/ppermute | solution.py:268
  27.6 0.0 copy-done
  27.6 0.0 copy-done.1
  27.6 0.0 copy-done.2
  27.6 0.0 copy-done.3
  27.6 6.2 %stats.1.mine = f32[6,8,256]{2,1,0:T(8,128)S(1)} custom-call(s32[16]{0:T(128)S(1)} %convert_element_type.27.flags, bf16[128,1536]{1,0:T(8,128)(2,1)S(1)} %bitcast.87, bf16[128,1536]{1,0:T(8,128)(2,1)S(1)} %bitcast.90, bf16[128,1536]{1,0:T(8,128)(2,1)S(1)} %bitcast.93, bf16[128,1536]{1,0:T(8,128)(2,1)S(1)} %bitcast.96, ...), custom_call_target="tpu_custom_call" | custom-call | tf_op jit(solution)/shard_map/stats/pallas_call | solution.py:234
  33.8 0.0 copy-done.4
  33.8 0.0 copy-done.5
  33.9 3.4 %collective-permute-start.4 = (f32[6,8,256]{2,1,0:T(8,128)S(1)}, f32[6,8,256]{2,1,0:T(8,128)S(1)}, u32[]{:S(2)}, u32[]{:S(2)}) collective-permute-start(f32[6,8,256]{2,1,0:T(8,128)S(1)} %stats.1.mine), channel_id=1, source_target_pairs={{0,16},{4,20},{8,24},{12,28},{16,0},{20,4},{24,8},{28,12},{3,19},{... | collective-permute-start | bytes 147464 | tf_op jit(solution)/shard_map/ppermute | solution.py:246
  37.3 2.5 %collective-permute-done.4.theirs = f32[6,8,256]{2,1,0:T(8,128)S(1)} collective-permute-done((f32[6,8,256]{2,1,0:T(8,128)S(1)}, f32[6,8,256]{2,1,0:T(8,128)S(1)}, u32[]{:S(2)}, u32[]{:S(2)}) %collective-permute-start.4) | collective-permute-done | bytes 49184 | tf_op jit(solution)/shard_map/ppermute | solution.py:246
  39.8 9.1 %grads.1 = (f32[128,1536]{1,0:T(8,128)S(1)}, f32[128,1536]{1,0:T(8,128)S(1)}, f32[128,1536]{1,0:T(8,128)S(1)}, f32[128,1536]{1,0:T(8,128)S(1)}, bf16[2,128,1536]...) custom-call(s32[16]{0:T(128)S(1)} %convert_element_type.27.flags, ...), custom_call_target="tpu_custom_call" | custom-call | tf_op jit(solution)/shard_map/grads/pallas_call | solution.py:249
  49.0 1.5 %collective-permute-start.5 = (bf16[2,128,1536]{2,1,0:T(8,128)(2,1)}, bf16[2,128,1536]{2,1,0:T(8,128)(2,1)S(1)}, u32[]{:S(2)}, u32[]{:S(2)}) collective-permute-start(bf16[2,128,1536]{2,1,0:T(8,128)(2,1)} %get-tuple-element.13), channel_id=1, source_target_pairs={{0,16},{4,20},{8,24},{12,28},{16,0},{20,4},{24,8},{28,12},{1,2},{5... | collective-permute-start | bytes 2359304 | tf_op jit(solution)/shard_map/ppermute | solution.py:270
  50.5 0.0 collective-permute-start.8
  50.5 0.0 collective-permute-start.7
  50.5 0.6 collective-permute-start.6
  51.1 15.1 %collective-permute-done.5 = bf16[2,128,1536]{2,1,0:T(8,128)(2,1)S(1)} collective-permute-done((bf16[2,128,1536]{2,1,0:T(8,128)(2,1)}, bf16[2,128,1536]{2,1,0:T(8,128)(2,1)S(1)}, u32[]{:S(2)}, u32[]{:S(2)}) %collective-permute-start.5) | collective-permute-done | bytes 786464 | tf_op jit(solution)/shard_map/ppermute | solution.py:270
  66.2 0.2 convert_select_fusion
  66.4 1.2 %collective-permute-done.8 = bf16[2,128,1536]{2,1,0:T(8,128)(2,1)S(1)} collective-permute-done((bf16[2,128,1536]{2,1,0:T(8,128)(2,1)}, bf16[2,128,1536]{2,1,0:T(8,128)(2,1)S(1)}, u32[]{:S(2)}, u32[]{:S(2)}) %collective-permute-start.8) | collective-permute-done | bytes 786464 | tf_op jit(solution)/shard_map/ppermute | solution.py:270
  67.6 0.2 convert_element_type.33
  67.8 1.8 %collective-permute-done.7 = bf16[2,128,1536]{2,1,0:T(8,128)(2,1)S(1)} collective-permute-done((bf16[2,128,1536]{2,1,0:T(8,128)(2,1)}, bf16[2,128,1536]{2,1,0:T(8,128)(2,1)S(1)}, u32[]{:S(2)}, u32[]{:S(2)}) %collective-permute-start.7) | collective-permute-done | bytes 786464 | tf_op jit(solution)/shard_map/ppermute | solution.py:270
  69.6 0.2 convert_element_type.32
  69.8 1.1 %fusion.13 = (bf16[128,1536]{1,0:T(8,128)(2,1)}, bf16[128,1536]{1,0:T(8,128)(2,1)}) fusion(f32[128,1536]{1,0:T(8,128)S(1)} %get-tuple-element.14, f32[2,128,1536]{2,1,0:T(8,128)S(1)} %get-tuple-element.27, f32[128,1536]{1,0:T(8,128)S(1)} %get-tuple-element.12), kind=kLoop, calls=%fused_computation.24 | loop fusion | flops 983040 | bytes 3932160 | tf_op jit(solution)/shard_map/convert_element_type | solution.py:275
  70.9 0.0 collective-permute-done.6
  70.9 0.2 convert_element_type.31
  71.1 1.7 %fusion.1 = (bf16[128,1536]{1,0:T(8,128)(2,1)}, bf16[128,1536]{1,0:T(8,128)(2,1)}) fusion(f32[2,128,1536]{2,1,0:T(8,128)S(1)} %get-tuple-element.26, f32[2,128,1536]{2,1,0:T(8,128)S(1)} %convert_element_type.33, f32[2,128,1536]{2,1,0:T(8,128)S(1)} %convert_element_type.32, f32[128,1536]{1,0:T(8,128)S(1)} %get-tuple-element.19, ...), kind=kLoop, calls=%fused_computation.4 | loop fusion | flops 2162688 | bytes 8650752 | tf_op jit(solution)/shard_map/convert_element_type | solution.py:277
  (4 shorter events, 0.0 us)
Async XLA Ops:
  0.6 8.9 %copy-start.7 = (s32[2,8]{1,0:T(2,128)S(1)}, s32[2,8]{1,0:T(2,128)}, u32[]{:S(2)}) copy-start(s32[2,8]{1,0:T(2,128)} %param.11) | copy-start | bytes 196
  0.7 10.9 %copy-start.6 = (s32[32,5]{0,1:T(8,128)S(1)}, s32[32,5]{0,1:T(8,128)}, u32[]{:S(2)}) copy-start(s32[32,5]{0,1:T(8,128)} %param.10) | copy-start | bytes 1924
  0.7 26.9 %copy-start = (bf16[8,16,1536]{2,1,0:T(8,128)(2,1)S(1)}, bf16[8,16,1536]{2,1,0:T(8,128)(2,1)}, u32[]{:S(2)}) copy-start(bf16[8,16,1536]{2,1,0:T(8,128)(2,1)} %param.6) | copy-start | bytes 1179652
  0.7 26.9 %copy-start.1 = (bf16[8,16,1536]{2,1,0:T(8,128)(2,1)S(1)}, bf16[8,16,1536]{2,1,0:T(8,128)(2,1)}, u32[]{:S(2)}) copy-start(bf16[8,16,1536]{2,1,0:T(8,128)(2,1)} %param.7) | copy-start | bytes 1179652
  0.7 26.9 %copy-start.2 = (bf16[8,16,1536]{2,1,0:T(8,128)(2,1)S(1)}, bf16[8,16,1536]{2,1,0:T(8,128)(2,1)}, u32[]{:S(2)}) copy-start(bf16[8,16,1536]{2,1,0:T(8,128)(2,1)} %param.8) | copy-start | bytes 1179652
  0.7 26.9 %copy-start.3 = (bf16[8,16,1536]{2,1,0:T(8,128)(2,1)S(1)}, bf16[8,16,1536]{2,1,0:T(8,128)(2,1)}, u32[]{:S(2)}) copy-start(bf16[8,16,1536]{2,1,0:T(8,128)(2,1)} %param.9) | copy-start | bytes 1179652
  3.4 9.0 %collective-permute-start = (bf16[2,128,1536]{2,1,0:T(8,128)(2,1)}, bf16[2,128,1536]{2,1,0:T(8,128)(2,1)S(1)}, u32[]{:S(2)}, u32[]{:S(2)}) collective-permute-start(bf16[2,128,1536]{2,1,0:T(8,128)(2,1)} %get-tuple-element.29), channel_id=1, source_target_pairs={{0,4},{4,0},{8,12},{12,8},{16,20},{20,16},{24,28},{28,24},{1,5},{5... | collective-permute-start | bytes 2359304 | tf_op jit(solution)/shard_map/ppermute | solution.py:267
  3.9 20.7 %collective-permute-start.1 = (bf16[2,128,1536]{2,1,0:T(8,128)(2,1)}, bf16[2,128,1536]{2,1,0:T(8,128)(2,1)S(1)}, u32[]{:S(2)}, u32[]{:S(2)}) collective-permute-start(bf16[2,128,1536]{2,1,0:T(8,128)(2,1)} %get-tuple-element.29), channel_id=1, source_target_pairs={{0,12},{4,8},{8,4},{12,0},{16,28},{20,24},{24,20},{28,16},{1,29},{... | collective-permute-start | bytes 2359304 | tf_op jit(solution)/shard_map/ppermute | solution.py:267
  6.5 19.8 %collective-permute-start.2 = (bf16[2,128,1536]{2,1,0:T(8,128)(2,1)}, bf16[2,128,1536]{2,1,0:T(8,128)(2,1)}, u32[]{:S(2)}, u32[]{:S(2)}) collective-permute-start(bf16[2,128,1536]{2,1,0:T(8,128)(2,1)} %get-tuple-element.29), channel_id=1, source_target_pairs={{0,1},{4,5},{8,9},{12,13},{16,17},{20,21},{24,25},{28,29},{1,0},{5... | collective-permute-start | bytes 2359304 | tf_op jit(solution)/shard_map/ppermute | solution.py:267
  9.0 18.5 %collective-permute-start.3 = (bf16[2,128,1536]{2,1,0:T(8,128)(2,1)}, bf16[2,128,1536]{2,1,0:T(8,128)(2,1)}, u32[]{:S(2)}, u32[]{:S(2)}) collective-permute-start(bf16[2,128,1536]{2,1,0:T(8,128)(2,1)} %get-tuple-element.28), channel_id=1, source_target_pairs={{0,16},{4,20},{8,24},{12,28},{16,0},{20,4},{24,8},{28,12},{1,2},{5... | collective-permute-start | bytes 2359304 | tf_op jit(solution)/shard_map/ppermute | solution.py:268
  12.5 21.4 %copy-start.4 = (bf16[2,128,1536]{2,1,0:T(8,128)(2,1)}, bf16[2,128,1536]{2,1,0:T(8,128)(2,1)S(1)}, u32[]{:S(2)}) copy-start(bf16[2,128,1536]{2,1,0:T(8,128)(2,1)S(1)} %collective-permute-done.n1) | copy-start | bytes 2359300
  24.6 9.2 %copy-start.5 = (bf16[2,128,1536]{2,1,0:T(8,128)(2,1)}, bf16[2,128,1536]{2,1,0:T(8,128)(2,1)S(1)}, u32[]{:S(2)}) copy-start(bf16[2,128,1536]{2,1,0:T(8,128)(2,1)S(1)} %collective-permute-done.1.n2) | copy-start | bytes 2359300
  33.9 6.0 %collective-permute-start.4 = (f32[6,8,256]{2,1,0:T(8,128)S(1)}, f32[6,8,256]{2,1,0:T(8,128)S(1)}, u32[]{:S(2)}, u32[]{:S(2)}) collective-permute-start(f32[6,8,256]{2,1,0:T(8,128)S(1)} %stats.1.mine), channel_id=1, source_target_pairs={{0,16},{4,20},{8,24},{12,28},{16,0},{20,4},{24,8},{28,12},{3,19},{... | collective-permute-start | bytes 147464 | tf_op jit(solution)/shard_map/ppermute | solution.py:246
  49.0 17.2 %collective-permute-start.5 = (bf16[2,128,1536]{2,1,0:T(8,128)(2,1)}, bf16[2,128,1536]{2,1,0:T(8,128)(2,1)S(1)}, u32[]{:S(2)}, u32[]{:S(2)}) collective-permute-start(bf16[2,128,1536]{2,1,0:T(8,128)(2,1)} %get-tuple-element.13), channel_id=1, source_target_pairs={{0,16},{4,20},{8,24},{12,28},{16,0},{20,4},{24,8},{28,12},{1,2},{5... | collective-permute-start | bytes 2359304 | tf_op jit(solution)/shard_map/ppermute | solution.py:270
  50.5 17.1 %collective-permute-start.8 = (bf16[2,128,1536]{2,1,0:T(8,128)(2,1)}, bf16[2,128,1536]{2,1,0:T(8,128)(2,1)S(1)}, u32[]{:S(2)}, u32[]{:S(2)}) collective-permute-start(bf16[2,128,1536]{2,1,0:T(8,128)(2,1)} %get-tuple-element.18), channel_id=1, source_target_pairs={{0,1},{4,5},{8,9},{12,13},{16,17},{20,21},{24,25},{28,29},{1,0},{5... | collective-permute-start | bytes 2359304 | tf_op jit(solution)/shard_map/ppermute | solution.py:270
  50.5 19.1 %collective-permute-start.7 = (bf16[2,128,1536]{2,1,0:T(8,128)(2,1)}, bf16[2,128,1536]{2,1,0:T(8,128)(2,1)S(1)}, u32[]{:S(2)}, u32[]{:S(2)}) collective-permute-start(bf16[2,128,1536]{2,1,0:T(8,128)(2,1)} %get-tuple-element.17), channel_id=1, source_target_pairs={{0,12},{4,8},{8,4},{12,0},{16,28},{20,24},{24,20},{28,16},{1,29},{... | collective-permute-start | bytes 2359304 | tf_op jit(solution)/shard_map/ppermute | solution.py:270
  50.5 20.4 %collective-permute-start.6 = (bf16[2,128,1536]{2,1,0:T(8,128)(2,1)S(1)}, bf16[2,128,1536]{2,1,0:T(8,128)(2,1)S(1)}, u32[]{:S(2)}, u32[]{:S(2)}) collective-permute-start(bf16[2,128,1536]{2,1,0:T(8,128)(2,1)S(1)} %get-tuple-element.16), channel_id=1, source_target_pairs={{0,4},{4,0},{8,12},{12,8},{16,20},{20,16},{24,28},{28,24},{1,5},{5... | collective-permute-start | bytes 2359304 | tf_op jit(solution)/shard_map/ppermute | solution.py:270

commit v2 on v1

v2 whole, which is shorter than its diff:
```python
import functools
import math

import jax
import jax.numpy as jnp
from jax import lax
from jax.experimental import pallas as pl
from jax.experimental.pallas import tpu as pltpu
from jax.sharding import PartitionSpec as P

DH = 128
SHARES = (0, 6, 12)
FINISH_WIDTH = 0
AHEAD = True
ORDER = (3, 1, 2, 0)
TIES = ((3,), (0,), (3,), (0,))
LATE = (0, 1, 2)
LAST = ((2,), (), (), ())
VMEM_BYTES = 16 * 1024 * 1024
SCALE = DH**-0.5
FACTOR = SCALE * math.log2(math.e)
LOW = -1e30
F32 = jnp.float32
BF16 = jnp.bfloat16


def dot_nt(a, b):
    return lax.dot_general(a, b, (((1,), (1,)), ((), ())), preferred_element_type=F32)


def dot_nn(a, b):
    return lax.dot_general(a, b, (((1,), (0,)), ((), ())), preferred_element_type=F32)


def dot_tn(a, b):
    return lax.dot_general(a, b, (((0,), (0,)), ((), ())), preferred_element_type=F32)


def rows(*parts):
    return jnp.concatenate(parts, axis=0)


def block_bias(flags, slot, tokens, both):
    own = jnp.where(flags[slot] > 0, 0.0, LOW).astype(F32)
    if not both:
        return jnp.full((1, tokens), own, F32)
    other = jnp.where(flags[8 + slot] > 0, 0.0, LOW).astype(F32)
    lane = lax.broadcasted_iota(jnp.int32, (1, 2 * tokens), 1)
    return jnp.where(lane < tokens, own, other)


def gathered(j, polar, qg, kv, near):
    cols = pl.ds(j * DH, DH)
    slots = (kv,) + (near[:3] if polar else near)
    kk, vv = [rows(*[r[i, :, cols] for r in slots]) for i in range(2)]
    qq, gg = [rows(qg[i, :, cols], near[3][i, :, cols]) if polar else qg[i, :, cols] for i in range(2)]
    return qq, gg, kk, vv


def stats_kernel(heads, tokens, flags, n4, n2, n3, n1, qg, kv, out):
    near = (n1, n2, n3, n4)

    def work(polar):
        width = 2 * tokens if polar else tokens
        count = 4 if polar else 5
        bias = [block_bias(flags, b, tokens, polar) for b in range(count)]
        tops, sums, deltas = [], [], []
        for j in range(heads):
            qq, gg, kk, vv = gathered(j, polar, qg, kv, near)
            s = dot_nt(kk, qq)
            dp = dot_nt(vv, gg)
            parts = [s[b * tokens : (b + 1) * tokens] * FACTOR + bias[b] for b in range(count)]
            top = functools.reduce(jnp.maximum, [jnp.max(x, axis=0, keepdims=True) for x in parts])
            total = jnp.zeros((1, width), F32)
            delta = jnp.zeros((1, width), F32)
            for b in range(count):
                e = jnp.exp2(parts[b] - top)
                total += jnp.sum(e, axis=0, keepdims=True)
                delta += jnp.sum(e * dp[b * tokens : (b + 1) * tokens], axis=0, keepdims=True)
            tops.append(top)
            sums.append(total)
            deltas.append(delta)
        stat = rows(*tops, *sums, *deltas)
        for r in range(3 * heads):
            out[r : r + 1, :width] = stat[r : r + 1]
        if out.shape[0] > 3 * heads:
            out[3 * heads :, :] = jnp.zeros((out.shape[0] - 3 * heads, 2 * tokens), F32)
        if not polar:
            out[: 3 * heads, tokens:] = jnp.zeros((3 * heads, tokens), F32)

    pl.when(flags[7] > 0)(lambda: work(True))
    pl.when(flags[7] == 0)(lambda: work(False))


def grads_kernel(heads, tokens, flags, n4, n2, n3, n1, mine, theirs, qg, kv, att, dq, dk, dv, r1, r2, r3, r4):
    near = (n1, n2, n3, n4)
    back = (r1, r2, r3, r4)

    def work(polar):
        width = 2 * tokens if polar else tokens
        count = 4 if polar else 5
        bias = [block_bias(flags, b, tokens, polar) for b in range(count)]
        for j in range(heads):
            cols = pl.ds(j * DH, DH)
            top, total, delta = [mine[r * heads + j : r * heads + j + 1, :width] for r in range(3)]
            if polar:
                top2, total2, delta2 = [
                    jnp.concatenate(
                        [
                            theirs[r * heads + j : r * heads + j + 1, tokens:],
                            theirs[r * heads + j : r * heads + j + 1, :tokens],
                        ],
                        axis=1,
                    )
                    for r in range(3)
                ]
                high = jnp.maximum(top, top2)
                a1, a2 = jnp.exp2(top - high), jnp.exp2(top2 - high)
                total = total * a1 + total2 * a2
                delta = delta * a1 + delta2 * a2
                top = high
            lse = top + jnp.log2(total)
            delta = delta / total
            qq, gg, kk, vv = gathered(j, polar, qg, kv, near)
            s = dot_nt(kk, qq)
            dp = dot_nt(vv, gg)
            ps = []
            for b in range(count):
                ps.append(jnp.exp2(s[b * tokens : (b + 1) * tokens] * FACTOR + (bias[b] - lse)))
            p = rows(*ps)
            w = p.astype(BF16)
            ds = (p * (dp - delta)).astype(BF16)
            dkk = dot_nn(ds, qq)
            dvv = dot_nn(w, gg)
            o = dot_tn(vv, w).T
            dqq = dot_tn(kk, ds).T
            att[:, cols] = o[:tokens]
            dq[:, cols] = dqq[:tokens]
            dk[:, cols] = dkk[:tokens]
            dv[:, cols] = dvv[:tokens]
            for b in range(1, count):
                back[b - 1][0, :, cols] = dkk[b * tokens : (b + 1) * tokens].astype(BF16)
                back[b - 1][1, :, cols] = dvv[b * tokens : (b + 1) * tokens].astype(BF16)
            if polar:
                r4[0, :, cols] = o[tokens:].astype(BF16)
                r4[1, :, cols] = dqq[tokens:].astype(BF16)

    pl.when(flags[7] > 0)(lambda: work(True))
    pl.when(flags[7] == 0)(lambda: work(False))


def exchange_plan(lon_count, lat_count):
    half = lon_count // 2

    def polar(b):
        return b == 0 or b == lat_count - 1

    def second(b, s):
        ring, base = (half, s // half * half) if polar(b) else (lon_count, 0)
        place = s - base
        return base + (place - 1 if place % 2 == 0 else place + 1) % ring

    def fourth(b, s):
        if polar(b):
            return b, (s + half) % lon_count
        return (b - 1 if b % 2 == 0 else b + 1), s

    cells = [(b, s) for b in range(lat_count) for s in range(lon_count)]

    def pairs(move):
        return [(s * lat_count + b, move(b, s)[1] * lat_count + move(b, s)[0]) for b, s in cells]

    return (
        pairs(lambda b, s: (b, s ^ 1)),
        pairs(lambda b, s: (b, second(b, s))),
        pairs(lambda b, s: (b ^ 1, s)),
        pairs(fourth),
    )


def held(x):
    return pltpu.with_memory_space_constraint(x, pltpu.VMEM)


def call(kernel, name, outs, *operands):
    whole = pl.BlockSpec(memory_space=pltpu.VMEM)
    flags = pl.BlockSpec(memory_space=pltpu.SMEM)
    return pl.pallas_call(
        kernel,
        in_specs=[flags] + [whole] * (len(operands) - 1),
        out_specs=[whole] * len(outs),
        out_shape=[pltpu.VMEM(shape, dtype) for shape, dtype in outs],
        compiler_params=pltpu.CompilerParams(vmem_limit_bytes=VMEM_BYTES),
        name=name,
    )(operands[0], *[held(x) for x in operands[1:]])


def start_all(copies):
    for copy in copies:
        copy.start()


def wait_all(copies):
    for copy in copies:
        copy.wait()


def cut_copies(first, one, two, out, sem, at):
    cut = pl.ds(first, out.shape[2])
    return [pltpu.make_async_copy(x.at[:, cut], out.at[i], sem.at[at + i]) for i, x in enumerate((one, two))]


def start_sends(first, polar, q, k, v, g, kv, chosen, sem):
    start_all(cut_copies(first, k, v, kv, sem, 0))
    pl.when(polar)(lambda: start_all(cut_copies(first, q, g, chosen, sem, 2)))
    pl.when(jnp.logical_not(polar))(lambda: start_all(cut_copies(first, k, v, chosen, sem, 2)))
    return cut_copies(first, k, v, kv, sem, 0) + cut_copies(first, k, v, chosen, sem, 2)


def is_polar(lat_count):
    b = lax.axis_index("lat")
    return (b == 0) | (b == lat_count - 1)


def first_pack_kernel(lat_count, q, k, v, g, kv, chosen, sem):
    wait_all(start_sends(0, is_polar(lat_count), q, k, v, g, kv, chosen, sem))


def later_pack_kernel(firsts, lat_count, lon_count, neighbours_in, partner_in, q, k, v, g, flags, *rest):
    *outs, sem, neighbours, partner = rest
    b, s = lax.axis_index("lat"), lax.axis_index("lon")
    polar = is_polar(lat_count)
    count = len(firsts)
    tables = [
        pltpu.make_async_copy(neighbours_in, neighbours, sem.at[0, 4]),
        pltpu.make_async_copy(partner_in, partner, sem.at[0, 5]),
    ]
    start_all(tables)
    copies = []
    for c in range(1, count):
        pair = outs[count + 2 * c - 2 : count + 2 * c]
        copies += start_sends(firsts[c], polar, q, k, v, g, *pair, sem.at[c])
    for c in range(count):
        more = cut_copies(firsts[c], q, g, outs[c], sem.at[c], 6)
        start_all(more)
        copies += more
    wait_all(tables)

    half = lon_count // 2
    ring = jnp.where(polar, half, lon_count)
    base = jnp.where(polar & (s >= half), half, 0)
    place = s - base
    second = base + lax.rem(place + jnp.where(lax.rem(place, 2) == 0, ring - 1, 1), ring)
    first = jnp.where(lax.rem(s, 2) == 0, s + 1, s - 1)
    even = lax.rem(b, 2) == 0
    third = jnp.where(even, b + 1, b - 1)
    fourth = jnp.where(even, b - 1, b + 1)
    slots = [
        b * lon_count + s,
        b * lon_count + first,
        b * lon_count + second,
        third * lon_count + s,
        jnp.where(polar, -7, fourth * lon_count + s),
    ]
    across = jnp.where(s >= half, s - half, s + half)
    pole = jnp.where(b == 0, 0, 1)

    def mark(strip, at, tiles):
        tile = b * lon_count + strip
        links = [neighbours[i, tile] for i in range(neighbours.shape[0])]
        links.append(jnp.where(polar, b * lon_count + partner[pole, strip], -9))
        for i, one in enumerate(tiles):
            flags[at + i] = functools.reduce(jnp.logical_or, [one == link for link in links]).astype(jnp.int32)

    mark(s, 0, slots)
    mark(across, 8, slots[:3])
    flags[7] = polar.astype(jnp.int32)
    for i in (5, 6, 11, 12, 13, 14, 15):
        flags[i] = 0
    wait_all(copies)


def pack(firsts, widths, lat_count, lon_count, neighbours, partner, q, k, v, g):
    tokens = q.shape[0]
    pairs = [pltpu.VMEM((2, tokens, wide), BF16) for wide in widths]
    smem, vmem, anywhere = [pl.BlockSpec(memory_space=m) for m in (pltpu.SMEM, pltpu.VMEM, pl.ANY)]
    far = [pltpu.with_memory_space_constraint(x, pltpu.HBM) for x in (neighbours, partner, q, k, v, g)]
    params = pltpu.CompilerParams(vmem_limit_bytes=VMEM_BYTES)
    kv, chosen = pl.pallas_call(
        functools.partial(first_pack_kernel, lat_count),
        in_specs=[anywhere] * 4,
        out_specs=[vmem] * 2,
        out_shape=[pairs[0]] * 2,
        scratch_shapes=[pltpu.SemaphoreType.DMA((4,))],
        compiler_params=params,
        name="first_pack",
    )(*far[2:])
    count = len(widths)
    later = [pair for pair in pairs[1:] for _ in range(2)]
    flags, *outs = pl.pallas_call(
        functools.partial(later_pack_kernel, firsts, lat_count, lon_count),
        in_specs=[anywhere] * 6,
        out_specs=[smem] + [vmem] * (count + len(later)),
        out_shape=[jax.ShapeDtypeStruct((16,), jnp.int32)] + pairs + later,
        scratch_shapes=[
            pltpu.SemaphoreType.DMA((count, 8)),
            pltpu.SMEM(neighbours.shape, jnp.int32),
            pltpu.SMEM(partner.shape, jnp.int32),
        ],
        compiler_params=params,
        name="later_pack",
    )(*far)
    sends = [(kv, chosen)] + [outs[count + 2 * c - 2 : count + 2 * c] for c in range(1, count)]
    return flags, [(sends[c][0], outs[c], sends[c][1]) for c in range(count)]


def after(x, *others):
    return lax.optimization_barrier((x, *others))[0]


def finish_kernel(flags, b4, b2, b3, b1, att, dq, dk, dv, *rest):
    o_att, o_dq, o_dk, o_dv = rest[-4:]
    inner = jnp.where(flags[7] > 0, 0.0, 1.0).astype(F32)
    fourth = [b4[i].astype(F32) for i in range(2)]
    o_att[...] = (att[...] + (1.0 - inner) * fourth[0]).astype(BF16)
    o_dq[...] = (SCALE * (dq[...] + (1.0 - inner) * fourth[1])).astype(BF16)
    terms = [b1[i].astype(F32) + b2[i].astype(F32) + b3[i].astype(F32) + inner * fourth[i] for i in range(2)]
    o_dk[...] = (SCALE * (dk[...] + terms[0])).astype(BF16)
    o_dv[...] = (dv[...] + terms[1]).astype(BF16)


def finish(first, features, flags, parts, returned, before):
    tokens, wide = parts[0].shape
    block = math.gcd(first, wide) if FINISH_WIDTH == 0 else math.gcd(FINISH_WIDTH * DH, math.gcd(first, wide))
    flat = pl.BlockSpec((tokens, block), lambda i: (0, i))
    pair = pl.BlockSpec((2, tokens, block), lambda i: (0, 0, i))
    place = pl.BlockSpec((tokens, block), lambda i: (0, first // block + i))
    kept = [pl.BlockSpec(memory_space=pl.ANY)] * len(before)
    return pl.pallas_call(
        finish_kernel,
        grid=(wide // block,),
        in_specs=[pl.BlockSpec(memory_space=pltpu.SMEM)] + [pair] * 4 + [flat] * 4 + kept,
        out_specs=[place] * 4,
        out_shape=[jax.ShapeDtypeStruct((tokens, features), BF16)] * 4,
        input_output_aliases={9 + i: i for i in range(len(before))},
        compiler_params=pltpu.CompilerParams(vmem_limit_bytes=VMEM_BYTES),
        name="finish",
    )(flags, *[returned[i] for i in (3, 1, 2, 0)], *parts, *before)


def body(queries, keys, values, out_grad, neighbours, partner):
    lat_count, lon_count = lax.axis_size("lat"), lax.axis_size("lon")
    tile_rows, tile_cols, features = queries.shape
    tokens = tile_rows * tile_cols
    heads = features // DH
    cuts = [heads * part // SHARES[-1] for part in SHARES]
    counts = [b - a for a, b in zip(cuts, cuts[1:])]
    firsts, widths = [a * DH for a in cuts[:-1]], [n * DH for n in counts]
    chunks = len(counts)
    q, k, v, g = [x.reshape(tokens, features) for x in (queries, keys, values, out_grad)]
    plan = exchange_plan(lon_count, lat_count)
    axes = ("lon", "lat")
    def exchange(operands, ties):
        out = [None] * 4
        for i in ORDER:
            out[i] = lax.ppermute(after(operands[i], *ties[i]) if ties[i] else operands[i], axes, plan[i])
        return out

    flags, packed = pack(firsts, widths, lat_count, lon_count, neighbours.T, partner, q, k, v, g)

    near = []
    for c in range(chunks):
        kv, qg, chosen = packed[c]
        ties = [[]] * 4 if c == 0 else [[near[-1][i] for i in tie] for tie in TIES]
        near.append(exchange((kv, kv, kv, chosen), ties))

    mine, theirs = [], []
    for c in range(chunks):
        kv, qg, chosen = packed[c]
        kernel = functools.partial(stats_kernel, counts[c], tokens)
        mine += call(kernel, "stats", [((-(-3 * counts[c] // 8) * 8, 2 * tokens), F32)], flags, *[near[c][i] for i in (3, 1, 2, 0)], qg, kv)
        theirs.append(lax.ppermute(mine[c], axes, plan[3]))
    done = []
    for c in range(chunks):
        kv, qg, chosen = packed[c]
        other = after(theirs[c], mine[c + 1]) if AHEAD and c + 1 < chunks else theirs[c]
        kernel = functools.partial(grads_kernel, counts[c], tokens)
        outs = [((tokens, widths[c]), F32)] * 4 + [((2, tokens, widths[c]), BF16)] * 4
        results = call(kernel, "grads", outs, flags, *[near[c][i] for i in (3, 1, 2, 0)], mine[c], other, qg, kv)
        if c + 1 < chunks:
            ties = [[theirs[c + 1]] if i in LATE else [] for i in range(4)]
        else:
            ties = [[done[-1][1][i] for i in tie] for tie in LAST]
        done.append((results[:4], exchange(results[4:], ties)))
    outs = []
    for c in range(chunks):
        outs = finish(firsts[c], features, flags, *done[c], outs)
    return tuple(x.reshape(tile_rows, tile_cols, features) for x in outs)


def solution(mesh):
    spec = P("lat", "lon", None)
    return jax.shard_map(
        body,
        mesh=mesh,
        in_specs=(spec,) * 4 + (P(),) * 2,
        out_specs=(spec,) * 4,
        check_vma=False,
    )
```

time: 73.1 us -> 56.2 us (0.77)
  waiting for transfers between devices: 35.7 us -> 19.8 us
  starting transfers between devices: 11.6 us -> 18.6 us
  other arithmetic: 6.78 us -> 0 us
  between operations: 2.16 us -> 0.71 us
  local copies, waits for them, and re-layouts: 1.03 us -> 0 us
  Pallas kernels: 15.4 us -> 16.4 us
    ppermute x9 -> x18, waiting for transfers between devices: 35.7 us -> 19.8 us  [the longest x16 19.8 us: exchange(): lax.ppermute(after(operands[i], *ties[i]) if ties[i] else operands[i], ax...]
    ppermute x9 -> x18, starting transfers between devices: 11.6 us -> 18.6 us  [the longest x16 15.8 us: exchange(): lax.ppermute(after(operands[i], *ties[i]) if ties[i] else operands[i], ax...]
    convert_element_type x6 -> x0, other arithmetic: 3.32 us -> none  [the longest x1 1.66 us: body(): (dv + b1[1] + b2[1] + b3[1] + fourth_k[1]).astype(BF16)]
    select_n x3 -> x0, other arithmetic: 2.94 us -> none  [the longest x1 2.73 us: body(): n4 = lax.ppermute(jnp.where(polar, qg, kv), axes, p4)]
    pallas_call x2 -> x8, Pallas kernels: 15.4 us -> 16.4 us  [the longest x4 9.8 us: call(): pl.pallas_call(kernel, in_specs=[flags] + [whole] * (len(operands) - 1),...]
    dynamic_slice x2 -> x0, local copies, waits for them, and re-layouts: 0.8 us -> none  [the longest x1 0.59 us: links(): extra = jnp.where(polar, b * lon_count + pole[strip], -9)]
  transfers between devices with their start and end apart: 9 -> 18, of which waited for: 7 -> 9; matrix products, arithmetic and copies ran while one was open for 4% -> 0% of each run, Pallas kernels for 0% -> 24%
where the time goes in v2:
time: 56.2 us; the launch traced here: 55.5 us
  waiting for transfers between devices  19.8 us (35%)
  starting transfers between devices  18.6 us (33%)
  Pallas kernels  16.4 us (29%)
  between operations  0.71 us (1%)
    ppermute x16, waiting for transfers between devices, exchange(): lax.ppermute(after(operands[i], *ties[i]) if ties[i] else operands[i], ax...  19.8 us
    ppermute x16, starting transfers between devices, exchange(): lax.ppermute(after(operands[i], *ties[i]) if ties[i] else operands[i], ax...  15.8 us
    pallas_call x4, Pallas kernels, call(): pl.pallas_call(kernel, in_specs=[flags] + [whole] * (len(operands) - 1),...  9.8 us
    pallas_call x2, Pallas kernels, finish(): pl.pallas_call(finish_kernel, grid=(wide // block,), in_specs=[pl.BlockSp...  3.17 us
    ppermute x2, starting transfers between devices, body(): theirs.append(lax.ppermute(mine[c], axes, plan[3]))  2.83 us
    pallas_call x1, Pallas kernels, pack(): pl.pallas_call(functools.partial(later_pack_kernel, firsts, lat_count, lo...  2.19 us
    pallas_call x1, Pallas kernels, pack(): pl.pallas_call(functools.partial(first_pack_kernel, lat_count), in_specs=...  1.26 us
  transfers between devices with their start and end apart: 18, of which 9 were waited for; matrix products, arithmetic and copies ran while one was open for 0% of the time, Pallas kernels for 24%

profile of v2, /device:TPU:0, one launch (start us, length us, event | category | flops | bytes accessed | tf_op | source)
XLA Modules:
  0.0 55.5 jit_solution(12204346071663699442)
XLA Ops:
  0.6 1.3 %first_pack.1 = (bf16[2,128,768]{2,1,0:T(8,128)(2,1)S(1)}, bf16[2,128,768]{2,1,0:T(8,128)(2,1)S(1)}) custom-call(bf16[128,1536]{1,0:T(8,128)(2,1)} %bitcast.9, bf16[128,1536]{1,0:T(8,128)(2,1)} %bitcast.11, bf16[128,1536]{1,0:T(8,128)(2,1)} %bitcast.13, bf16[128,1536]{1,0:T(8,128)(2,1)} %bitcast.15), custom_call_target="tpu_custom_call" | custom-call | tf_op jit(solution)/shard_map/first_pack/pallas_call | solution.py:289
  1.9 0.5 collective-permute-start
  2.4 2.6 %collective-permute-start.3 = (bf16[2,128,768]{2,1,0:T(8,128)(2,1)S(1)}, bf16[2,128,768]{2,1,0:T(8,128)(2,1)S(1)}, u32[]{:S(2)}, u32[]{:S(2)}) collective-permute-start(bf16[2,128,768]{2,1,0:T(8,128)(2,1)S(1)} %get-tuple-element.49), channel_id=1, source_target_pairs={{0,16},{4,20},{8,24},{12,28},{16,0},{20,4},{24,8},{28,12},{1,2},{5... | collective-permute-start | bytes 1179656 | tf_op jit(solution)/shard_map/ppermute | solution.py:366
  5.0 1.3 %collective-permute-start.10 = (bf16[2,128,768]{2,1,0:T(8,128)(2,1)S(1)}, bf16[2,128,768]{2,1,0:T(8,128)(2,1)S(1)}, u32[]{:S(2)}, u32[]{:S(2)}) collective-permute-start(bf16[2,128,768]{2,1,0:T(8,128)(2,1)S(1)} %get-tuple-element.45.kv), channel_id=1, source_target_pairs={{0,12},{4,8},{8,4},{12,0},{16,28},{20,24},{24,20},{28,16},{1,29},{... | collective-permute-start | bytes 1179656 | tf_op jit(solution)/shard_map/ppermute | solution.py:366
  6.3 2.6 %collective-permute-start.11 = (bf16[2,128,768]{2,1,0:T(8,128)(2,1)S(1)}, bf16[2,128,768]{2,1,0:T(8,128)(2,1)S(1)}, u32[]{:S(2)}, u32[]{:S(2)}) collective-permute-start(bf16[2,128,768]{2,1,0:T(8,128)(2,1)S(1)} %get-tuple-element.45.kv), channel_id=1, source_target_pairs={{0,1},{4,5},{8,9},{12,13},{16,17},{20,21},{24,25},{28,29},{1,0},{5... | collective-permute-start | bytes 1179656 | tf_op jit(solution)/shard_map/ppermute | solution.py:366
  8.9 2.2 %later_pack.1 = (s32[16]{0:T(128)S(1)}, bf16[2,128,768]{2,1,0:T(8,128)(2,1)S(1)}, bf16[2,128,768]{2,1,0:T(8,128)(2,1)S(1)}, bf16[2,128,768]{2,1,0:T(8,128)(2,1)S(1)}, bf16[2,128,768]{2,1,0:T(8,128)(2,1)S(1)}) custom-call(s32[5,32]{1,0:T(8,128)} %bitcast.21, s32[2,8]{1,0:T(2,128)} %partner_in.1, bf16[128,1536]{1,0:T(8,128)(2,1)} %bitcast.10, ...), custom_call_target="tpu_custom_call" | custom-call | tf_op jit(solution)/shard_map/later_pack/pallas_call | solution.py:300
  11.1 0.0 collective-permute-done.n1
  11.1 0.3 collective-permute-start.2
  11.3 0.5 collective-permute-start.1
  11.8 3.1 %collective-permute-done.3.n4 = bf16[2,128,768]{2,1,0:T(8,128)(2,1)S(1)} collective-permute-done((bf16[2,128,768]{2,1,0:T(8,128)(2,1)S(1)}, bf16[2,128,768]{2,1,0:T(8,128)(2,1)S(1)}, u32[]{:S(2)}, u32[]{:S(2)}) %collective-permute-start.3) | collective-permute-done | bytes 393248 | tf_op jit(solution)/shard_map/ppermute | solution.py:366
  15.0 2.0 %collective-permute-start.4 = (bf16[2,128,768]{2,1,0:T(8,128)(2,1)S(1)}, bf16[2,128,768]{2,1,0:T(8,128)(2,1)S(1)}, u32[]{:S(2)}, u32[]{:S(2)}) collective-permute-start(bf16[2,128,768]{2,1,0:T(8,128)(2,1)S(1)} %get-tuple-element.50.kv), channel_id=1, source_target_pairs={{0,1},{4,5},{8,9},{12,13},{16,17},{20,21},{24,25},{28,29},{1,0},{5... | collective-permute-start | bytes 1179656 | tf_op jit(solution)/shard_map/ppermute | solution.py:366
  17.0 0.0 collective-permute-done.10.n2
  17.0 0.0 collective-permute-start.5
  17.0 1.1 %collective-permute-done.11.n3 = bf16[2,128,768]{2,1,0:T(8,128)(2,1)S(1)} collective-permute-done((bf16[2,128,768]{2,1,0:T(8,128)(2,1)S(1)}, bf16[2,128,768]{2,1,0:T(8,128)(2,1)S(1)}, u32[]{:S(2)}, u32[]{:S(2)}) %collective-permute-start.11) | collective-permute-done | bytes 393248 | tf_op jit(solution)/shard_map/ppermute | solution.py:366
  18.0 1.9 %stats.3.mine = f32[24,256]{1,0:T(8,128)S(1)} custom-call(s32[16]{0:T(128)S(1)} %get-tuple-element.43.flags, bf16[2,128,768]{2,1,0:T(8,128)(2,1)S(1)} %collective-permute-done.3.n4, bf16[2,128,768]{2,1,0:T(8,128)(2,1)S(1)} %collective-permute-done.10.n2, bf16[2,128,768]{2,1,0:T(8,128)(2,1)S(1)} %collective-permute-done.11.n3, ...), custom_call_target="tpu_custom_call" | custom-call | tf_op jit(solution)/shard_map/stats/pallas_call | solution.py:188
  20.0 1.4 %collective-permute-start.12 = (f32[24,256]{1,0:T(8,128)S(1)}, f32[24,256]{1,0:T(8,128)S(1)}, u32[]{:S(2)}, u32[]{:S(2)}) collective-permute-start(f32[24,256]{1,0:T(8,128)S(1)} %stats.3.mine), channel_id=1, source_target_pairs={{0,16},{4,20},{8,24},{12,28},{16,0},{20,4},{24,8},{28,12},{1,2},{5... | collective-permute-start | bytes 73736 | tf_op jit(solution)/shard_map/ppermute | solution.py:382
  21.3 3.2 %collective-permute-done.2.n2 = bf16[2,128,768]{2,1,0:T(8,128)(2,1)S(1)} collective-permute-done((bf16[2,128,768]{2,1,0:T(8,128)(2,1)S(1)}, bf16[2,128,768]{2,1,0:T(8,128)(2,1)S(1)}, u32[]{:S(2)}, u32[]{:S(2)}) %collective-permute-start.2) | collective-permute-done | bytes 393248 | tf_op jit(solution)/shard_map/ppermute | solution.py:366
  24.5 0.0 collective-permute-done.1.n4
  24.5 1.6 %collective-permute-done.4.n3 = bf16[2,128,768]{2,1,0:T(8,128)(2,1)S(1)} collective-permute-done((bf16[2,128,768]{2,1,0:T(8,128)(2,1)S(1)}, bf16[2,128,768]{2,1,0:T(8,128)(2,1)S(1)}, u32[]{:S(2)}, u32[]{:S(2)}) %collective-permute-start.4) | collective-permute-done | bytes 393248 | tf_op jit(solution)/shard_map/ppermute | solution.py:366
  26.1 0.0 collective-permute-done.5.n1
  26.1 1.9 %stats.2.mine = f32[24,256]{1,0:T(8,128)S(1)} custom-call(s32[16]{0:T(128)S(1)} %get-tuple-element.43.flags, bf16[2,128,768]{2,1,0:T(8,128)(2,1)S(1)} %collective-permute-done.1.n4, bf16[2,128,768]{2,1,0:T(8,128)(2,1)S(1)} %collective-permute-done.2.n2, bf16[2,128,768]{2,1,0:T(8,128)(2,1)S(1)} %collective-permute-done.4.n3, ...), custom_call_target="tpu_custom_call" | custom-call | tf_op jit(solution)/shard_map/stats/pallas_call | solution.py:188
  28.0 1.5 %collective-permute-start.6 = (f32[24,256]{1,0:T(8,128)S(1)}, f32[24,256]{1,0:T(8,128)S(1)}, u32[]{:S(2)}, u32[]{:S(2)}) collective-permute-start(f32[24,256]{1,0:T(8,128)S(1)} %stats.2.mine), channel_id=1, source_target_pairs={{0,16},{4,20},{8,24},{12,28},{16,0},{20,4},{24,8},{28,12},{1,2},{5... | collective-permute-start | bytes 73736 | tf_op jit(solution)/shard_map/ppermute | solution.py:382
  29.5 0.0 collective-permute-done.12.theirs
  29.5 2.9 %grads.3 = (f32[128,768]{1,0:T(8,128)S(1)}, f32[128,768]{1,0:T(8,128)S(1)}, f32[128,768]{1,0:T(8,128)S(1)}, f32[128,768]{1,0:T(8,128)S(1)}, bf16[2,128,768]{2,1,...) custom-call(s32[16]{0:T(128)S(1)} %get-tuple-element.43.flags, ...), custom_call_target="tpu_custom_call" | custom-call | tf_op jit(solution)/shard_map/grads/pallas_call | solution.py:188
  32.4 0.0 collective-permute-done.6.theirs
  32.4 1.1 %collective-permute-start.13 = (bf16[2,128,768]{2,1,0:T(8,128)(2,1)S(1)}, bf16[2,128,768]{2,1,0:T(8,128)(2,1)S(1)}, u32[]{:S(2)}, u32[]{:S(2)}) collective-permute-start(bf16[2,128,768]{2,1,0:T(8,128)(2,1)S(1)} %get-tuple-element.59), channel_id=1, source_target_pairs={{0,1},{4,5},{8,9},{12,13},{16,17},{20,21},{24,25},{28,29},{1,0},{5... | collective-permute-start | bytes 1179656 | tf_op jit(solution)/shard_map/ppermute | solution.py:366
  33.5 1.3 %collective-permute-start.15 = (bf16[2,128,768]{2,1,0:T(8,128)(2,1)S(1)}, bf16[2,128,768]{2,1,0:T(8,128)(2,1)S(1)}, u32[]{:S(2)}, u32[]{:S(2)}) collective-permute-start(bf16[2,128,768]{2,1,0:T(8,128)(2,1)S(1)} %get-tuple-element.65), channel_id=1, source_target_pairs={{0,16},{4,20},{8,24},{12,28},{16,0},{20,4},{24,8},{28,12},{1,2},{5... | collective-permute-start | bytes 1179656 | tf_op jit(solution)/shard_map/ppermute | solution.py:366
  34.8 0.0 collective-permute-start.17
  34.8 1.6 %collective-permute-start.16 = (bf16[2,128,768]{2,1,0:T(8,128)(2,1)S(1)}, bf16[2,128,768]{2,1,0:T(8,128)(2,1)S(1)}, u32[]{:S(2)}, u32[]{:S(2)}) collective-permute-start(bf16[2,128,768]{2,1,0:T(8,128)(2,1)S(1)} %get-tuple-element.67), channel_id=1, source_target_pairs={{0,12},{4,8},{8,4},{12,0},{16,28},{20,24},{24,20},{28,16},{1,29},{... | collective-permute-start | bytes 1179656 | tf_op jit(solution)/shard_map/ppermute | solution.py:366
  36.4 3.1 %grads.2 = (f32[128,768]{1,0:T(8,128)S(1)}, f32[128,768]{1,0:T(8,128)S(1)}, f32[128,768]{1,0:T(8,128)S(1)}, f32[128,768]{1,0:T(8,128)S(1)}, bf16[2,128,768]{2,1,...) custom-call(s32[16]{0:T(128)S(1)} %get-tuple-element.43.flags, ...), custom_call_target="tpu_custom_call" | custom-call | tf_op jit(solution)/shard_map/grads/pallas_call | solution.py:188
  39.4 0.6 %collective-permute-start.7 = (bf16[2,128,768]{2,1,0:T(8,128)(2,1)S(1)}, bf16[2,128,768]{2,1,0:T(8,128)(2,1)S(1)}, u32[]{:S(2)}, u32[]{:S(2)}) collective-permute-start(bf16[2,128,768]{2,1,0:T(8,128)(2,1)S(1)} %get-tuple-element.52), channel_id=1, source_target_pairs={{0,16},{4,20},{8,24},{12,28},{16,0},{20,4},{24,8},{28,12},{1,2},{5... | collective-permute-start | bytes 1179656 | tf_op jit(solution)/shard_map/ppermute | solution.py:366
  40.0 1.8 %collective-permute-done.13.b3 = bf16[2,128,768]{2,1,0:T(8,128)(2,1)S(1)} collective-permute-done((bf16[2,128,768]{2,1,0:T(8,128)(2,1)S(1)}, bf16[2,128,768]{2,1,0:T(8,128)(2,1)S(1)}, u32[]{:S(2)}, u32[]{:S(2)}) %collective-permute-start.13) | collective-permute-done | bytes 393248 | tf_op jit(solution)/shard_map/ppermute | solution.py:366
  41.8 0.0 collective-permute-start.8
  41.8 1.1 %collective-permute-done.15.b4 = bf16[2,128,768]{2,1,0:T(8,128)(2,1)S(1)} collective-permute-done((bf16[2,128,768]{2,1,0:T(8,128)(2,1)S(1)}, bf16[2,128,768]{2,1,0:T(8,128)(2,1)S(1)}, u32[]{:S(2)}, u32[]{:S(2)}) %collective-permute-start.15) | collective-permute-done | bytes 393248 | tf_op jit(solution)/shard_map/ppermute | solution.py:366
  42.8 1.5 %collective-permute-start.9 = (bf16[2,128,768]{2,1,0:T(8,128)(2,1)S(1)}, bf16[2,128,768]{2,1,0:T(8,128)(2,1)S(1)}, u32[]{:S(2)}, u32[]{:S(2)}) collective-permute-start(bf16[2,128,768]{2,1,0:T(8,128)(2,1)S(1)} %get-tuple-element.54), channel_id=1, source_target_pairs={{0,1},{4,5},{8,9},{12,13},{16,17},{20,21},{24,25},{28,29},{1,0},{5... | collective-permute-start | bytes 1179656 | tf_op jit(solution)/shard_map/ppermute | solution.py:366
  44.3 0.0 collective-permute-done.17.b1
  44.3 0.0 collective-permute-start.14
  44.4 1.5 %collective-permute-done.16.b2 = bf16[2,128,768]{2,1,0:T(8,128)(2,1)S(1)} collective-permute-done((bf16[2,128,768]{2,1,0:T(8,128)(2,1)S(1)}, bf16[2,128,768]{2,1,0:T(8,128)(2,1)S(1)}, u32[]{:S(2)}, u32[]{:S(2)}) %collective-permute-start.16) | collective-permute-done | bytes 393248 | tf_op jit(solution)/shard_map/ppermute | solution.py:366
  45.8 1.6 %finish.2 = (bf16[128,1536]{1,0:T(8,128)(2,1)}, bf16[128,1536]{1,0:T(8,128)(2,1)}, bf16[128,1536]{1,0:T(8,128)(2,1)}, bf16[128,1536]{1,0:T(8,128)(2,1)}) custom-call(s32[16]{0:T(128)S(1)} %get-tuple-element.43.flags, bf16[2,128,768]{2,1,0:T(8,128)(2,1)S(1)} %collective-permute-done.15.b4, bf16[2,128,768]{2,1,0:T(8,128)(2,1)S(1)} %collective-permute-done.16.b2, ...), custom_call_target="tpu_custom_call" | custom-call | tf_op jit(solution)/shard_map/finish/pallas_call | solution.py:339
  47.4 3.5 %collective-permute-done.7.b4 = bf16[2,128,768]{2,1,0:T(8,128)(2,1)S(1)} collective-permute-done((bf16[2,128,768]{2,1,0:T(8,128)(2,1)S(1)}, bf16[2,128,768]{2,1,0:T(8,128)(2,1)S(1)}, u32[]{:S(2)}, u32[]{:S(2)}) %collective-permute-start.7) | collective-permute-done | bytes 393248 | tf_op jit(solution)/shard_map/ppermute | solution.py:366
  50.9 3.0 %collective-permute-done.8.b2 = bf16[2,128,768]{2,1,0:T(8,128)(2,1)S(1)} collective-permute-done((bf16[2,128,768]{2,1,0:T(8,128)(2,1)S(1)}, bf16[2,128,768]{2,1,0:T(8,128)(2,1)S(1)}, u32[]{:S(2)}, u32[]{:S(2)}) %collective-permute-start.8) | collective-permute-done | bytes 393248 | tf_op jit(solution)/shard_map/ppermute | solution.py:366
  53.9 0.0 collective-permute-done.9.b3
  54.0 0.0 collective-permute-done.14.b1
  54.0 1.6 %finish.3 = (bf16[128,1536]{1,0:T(8,128)(2,1)}, bf16[128,1536]{1,0:T(8,128)(2,1)}, bf16[128,1536]{1,0:T(8,128)(2,1)}, bf16[128,1536]{1,0:T(8,128)(2,1)}) custom-call(s32[16]{0:T(128)S(1)} %get-tuple-element.43.flags, bf16[2,128,768]{2,1,0:T(8,128)(2,1)S(1)} %collective-permute-done.7.b4, ...), custom_call_target="tpu_custom_call", output_to_operand_aliasing={{0}: (9, {}), {1}: (10, {}), {2}: (11, {}), {3}: (12, {})} | custom-call | tf_op jit(solution)/shard_map/finish/pallas_call | solution.py:339
Async XLA Ops:
  1.9 9.2 %collective-permute-start = (bf16[2,128,768]{2,1,0:T(8,128)(2,1)S(1)}, bf16[2,128,768]{2,1,0:T(8,128)(2,1)S(1)}, u32[]{:S(2)}, u32[]{:S(2)}) collective-permute-start(bf16[2,128,768]{2,1,0:T(8,128)(2,1)S(1)} %get-tuple-element.45.kv), channel_id=1, source_target_pairs={{0,4},{4,0},{8,12},{12,8},{16,20},{20,16},{24,28},{28,24},{1,5},{5... | collective-permute-start | bytes 1179656 | tf_op jit(solution)/shard_map/ppermute | solution.py:366
  2.4 12.6 %collective-permute-start.3 = (bf16[2,128,768]{2,1,0:T(8,128)(2,1)S(1)}, bf16[2,128,768]{2,1,0:T(8,128)(2,1)S(1)}, u32[]{:S(2)}, u32[]{:S(2)}) collective-permute-start(bf16[2,128,768]{2,1,0:T(8,128)(2,1)S(1)} %get-tuple-element.49), channel_id=1, source_target_pairs={{0,16},{4,20},{8,24},{12,28},{16,0},{20,4},{24,8},{28,12},{1,2},{5... | collective-permute-start | bytes 1179656 | tf_op jit(solution)/shard_map/ppermute | solution.py:366
  5.0 12.0 %collective-permute-start.10 = (bf16[2,128,768]{2,1,0:T(8,128)(2,1)S(1)}, bf16[2,128,768]{2,1,0:T(8,128)(2,1)S(1)}, u32[]{:S(2)}, u32[]{:S(2)}) collective-permute-start(bf16[2,128,768]{2,1,0:T(8,128)(2,1)S(1)} %get-tuple-element.45.kv), channel_id=1, source_target_pairs={{0,12},{4,8},{8,4},{12,0},{16,28},{20,24},{24,20},{28,16},{1,29},{... | collective-permute-start | bytes 1179656 | tf_op jit(solution)/shard_map/ppermute | solution.py:366
  6.3 11.8 %collective-permute-start.11 = (bf16[2,128,768]{2,1,0:T(8,128)(2,1)S(1)}, bf16[2,128,768]{2,1,0:T(8,128)(2,1)S(1)}, u32[]{:S(2)}, u32[]{:S(2)}) collective-permute-start(bf16[2,128,768]{2,1,0:T(8,128)(2,1)S(1)} %get-tuple-element.45.kv), channel_id=1, source_target_pairs={{0,1},{4,5},{8,9},{12,13},{16,17},{20,21},{24,25},{28,29},{1,0},{5... | collective-permute-start | bytes 1179656 | tf_op jit(solution)/shard_map/ppermute | solution.py:366
  11.1 13.4 %collective-permute-start.2 = (bf16[2,128,768]{2,1,0:T(8,128)(2,1)S(1)}, bf16[2,128,768]{2,1,0:T(8,128)(2,1)S(1)}, u32[]{:S(2)}, u32[]{:S(2)}) collective-permute-start(bf16[2,128,768]{2,1,0:T(8,128)(2,1)S(1)} %get-tuple-element.50.kv), channel_id=1, source_target_pairs={{0,12},{4,8},{8,4},{12,0},{16,28},{20,24},{24,20},{28,16},{1,29},{... | collective-permute-start | bytes 1179656 | tf_op jit(solution)/shard_map/ppermute | solution.py:366
  11.3 13.2 %collective-permute-start.1 = (bf16[2,128,768]{2,1,0:T(8,128)(2,1)S(1)}, bf16[2,128,768]{2,1,0:T(8,128)(2,1)S(1)}, u32[]{:S(2)}, u32[]{:S(2)}) collective-permute-start(bf16[2,128,768]{2,1,0:T(8,128)(2,1)S(1)} %get-tuple-element.46), channel_id=1, source_target_pairs={{0,16},{4,20},{8,24},{12,28},{16,0},{20,4},{24,8},{28,12},{1,2},{5... | collective-permute-start | bytes 1179656 | tf_op jit(solution)/shard_map/ppermute | solution.py:366
  15.0 11.1 %collective-permute-start.4 = (bf16[2,128,768]{2,1,0:T(8,128)(2,1)S(1)}, bf16[2,128,768]{2,1,0:T(8,128)(2,1)S(1)}, u32[]{:S(2)}, u32[]{:S(2)}) collective-permute-start(bf16[2,128,768]{2,1,0:T(8,128)(2,1)S(1)} %get-tuple-element.50.kv), channel_id=1, source_target_pairs={{0,1},{4,5},{8,9},{12,13},{16,17},{20,21},{24,25},{28,29},{1,0},{5... | collective-permute-start | bytes 1179656 | tf_op jit(solution)/shard_map/ppermute | solution.py:366
  17.0 9.1 %collective-permute-start.5 = (bf16[2,128,768]{2,1,0:T(8,128)(2,1)S(1)}, bf16[2,128,768]{2,1,0:T(8,128)(2,1)S(1)}, u32[]{:S(2)}, u32[]{:S(2)}) collective-permute-start(bf16[2,128,768]{2,1,0:T(8,128)(2,1)S(1)} %get-tuple-element.50.kv), channel_id=1, source_target_pairs={{0,4},{4,0},{8,12},{12,8},{16,20},{20,16},{24,28},{28,24},{1,5},{5... | collective-permute-start | bytes 1179656 | tf_op jit(solution)/shard_map/ppermute | solution.py:366
  20.0 9.5 %collective-permute-start.12 = (f32[24,256]{1,0:T(8,128)S(1)}, f32[24,256]{1,0:T(8,128)S(1)}, u32[]{:S(2)}, u32[]{:S(2)}) collective-permute-start(f32[24,256]{1,0:T(8,128)S(1)} %stats.3.mine), channel_id=1, source_target_pairs={{0,16},{4,20},{8,24},{12,28},{16,0},{20,4},{24,8},{28,12},{1,2},{5... | collective-permute-start | bytes 73736 | tf_op jit(solution)/shard_map/ppermute | solution.py:382
  28.0 4.4 %collective-permute-start.6 = (f32[24,256]{1,0:T(8,128)S(1)}, f32[24,256]{1,0:T(8,128)S(1)}, u32[]{:S(2)}, u32[]{:S(2)}) collective-permute-start(f32[24,256]{1,0:T(8,128)S(1)} %stats.2.mine), channel_id=1, source_target_pairs={{0,16},{4,20},{8,24},{12,28},{16,0},{20,4},{24,8},{28,12},{1,2},{5... | collective-permute-start | bytes 73736 | tf_op jit(solution)/shard_map/ppermute | solution.py:382
  32.4 9.4 %collective-permute-start.13 = (bf16[2,128,768]{2,1,0:T(8,128)(2,1)S(1)}, bf16[2,128,768]{2,1,0:T(8,128)(2,1)S(1)}, u32[]{:S(2)}, u32[]{:S(2)}) collective-permute-start(bf16[2,128,768]{2,1,0:T(8,128)(2,1)S(1)} %get-tuple-element.59), channel_id=1, source_target_pairs={{0,1},{4,5},{8,9},{12,13},{16,17},{20,21},{24,25},{28,29},{1,0},{5... | collective-permute-start | bytes 1179656 | tf_op jit(solution)/shard_map/ppermute | solution.py:366
  33.5 9.3 %collective-permute-start.15 = (bf16[2,128,768]{2,1,0:T(8,128)(2,1)S(1)}, bf16[2,128,768]{2,1,0:T(8,128)(2,1)S(1)}, u32[]{:S(2)}, u32[]{:S(2)}) collective-permute-start(bf16[2,128,768]{2,1,0:T(8,128)(2,1)S(1)} %get-tuple-element.65), channel_id=1, source_target_pairs={{0,16},{4,20},{8,24},{12,28},{16,0},{20,4},{24,8},{28,12},{1,2},{5... | collective-permute-start | bytes 1179656 | tf_op jit(solution)/shard_map/ppermute | solution.py:366
  34.8 9.6 %collective-permute-start.17 = (bf16[2,128,768]{2,1,0:T(8,128)(2,1)S(1)}, bf16[2,128,768]{2,1,0:T(8,128)(2,1)S(1)}, u32[]{:S(2)}, u32[]{:S(2)}) collective-permute-start(bf16[2,128,768]{2,1,0:T(8,128)(2,1)S(1)} %get-tuple-element.69), channel_id=1, source_target_pairs={{0,4},{4,0},{8,12},{12,8},{16,20},{20,16},{24,28},{28,24},{1,5},{5... | collective-permute-start | bytes 1179656 | tf_op jit(solution)/shard_map/ppermute | solution.py:366
  34.8 11.1 %collective-permute-start.16 = (bf16[2,128,768]{2,1,0:T(8,128)(2,1)S(1)}, bf16[2,128,768]{2,1,0:T(8,128)(2,1)S(1)}, u32[]{:S(2)}, u32[]{:S(2)}) collective-permute-start(bf16[2,128,768]{2,1,0:T(8,128)(2,1)S(1)} %get-tuple-element.67), channel_id=1, source_target_pairs={{0,12},{4,8},{8,4},{12,0},{16,28},{20,24},{24,20},{28,16},{1,29},{... | collective-permute-start | bytes 1179656 | tf_op jit(solution)/shard_map/ppermute | solution.py:366
  39.4 11.5 %collective-permute-start.7 = (bf16[2,128,768]{2,1,0:T(8,128)(2,1)S(1)}, bf16[2,128,768]{2,1,0:T(8,128)(2,1)S(1)}, u32[]{:S(2)}, u32[]{:S(2)}) collective-permute-start(bf16[2,128,768]{2,1,0:T(8,128)(2,1)S(1)} %get-tuple-element.52), channel_id=1, source_target_pairs={{0,16},{4,20},{8,24},{12,28},{16,0},{20,4},{24,8},{28,12},{1,2},{5... | collective-permute-start | bytes 1179656 | tf_op jit(solution)/shard_map/ppermute | solution.py:366
  41.8 12.2 %collective-permute-start.8 = (bf16[2,128,768]{2,1,0:T(8,128)(2,1)S(1)}, bf16[2,128,768]{2,1,0:T(8,128)(2,1)S(1)}, u32[]{:S(2)}, u32[]{:S(2)}) collective-permute-start(bf16[2,128,768]{2,1,0:T(8,128)(2,1)S(1)} %get-tuple-element.53), channel_id=1, source_target_pairs={{0,12},{4,8},{8,4},{12,0},{16,28},{20,24},{24,20},{28,16},{1,29},{... | collective-permute-start | bytes 1179656 | tf_op jit(solution)/shard_map/ppermute | solution.py:366
  42.8 11.1 %collective-permute-start.9 = (bf16[2,128,768]{2,1,0:T(8,128)(2,1)S(1)}, bf16[2,128,768]{2,1,0:T(8,128)(2,1)S(1)}, u32[]{:S(2)}, u32[]{:S(2)}) collective-permute-start(bf16[2,128,768]{2,1,0:T(8,128)(2,1)S(1)} %get-tuple-element.54), channel_id=1, source_target_pairs={{0,1},{4,5},{8,9},{12,13},{16,17},{20,21},{24,25},{28,29},{1,0},{5... | collective-permute-start | bytes 1179656 | tf_op jit(solution)/shard_map/ppermute | solution.py:366
  44.3 9.6 %collective-permute-start.14 = (bf16[2,128,768]{2,1,0:T(8,128)(2,1)S(1)}, bf16[2,128,768]{2,1,0:T(8,128)(2,1)S(1)}, u32[]{:S(2)}, u32[]{:S(2)}) collective-permute-start(bf16[2,128,768]{2,1,0:T(8,128)(2,1)S(1)} %get-tuple-element.60), channel_id=1, source_target_pairs={{0,4},{4,0},{8,12},{12,8},{16,20},{20,16},{24,28},{28,24},{1,5},{5... | collective-permute-start | bytes 1179656 | tf_op jit(solution)/shard_map/ppermute | solution.py:366

commit v3 on v2

--- a/solution.py
+++ b/solution.py
@@ -10,11 +10,12 @@
 
 DH = 128
 SHARES = (0, 6, 12)
-FINISH_WIDTH = 0
-AHEAD = True
+FINISH_HEADS = 3
 ORDER = (3, 1, 2, 0)
 TIES = ((3,), (0,), (3,), (0,))
-LATE = (0, 1, 2)
+LATE = (1, 1, 1, 1)
+FIRST = (0, 0, 0, 0)
+PIECES = 1
 LAST = ((2,), (), (), ())
 VMEM_BYTES = 16 * 1024 * 1024
 SCALE = DH**-0.5
@@ -40,15 +41,6 @@
     return jnp.concatenate(parts, axis=0)
 
 
-def block_bias(flags, slot, tokens, both):
-    own = jnp.where(flags[slot] > 0, 0.0, LOW).astype(F32)
-    if not both:
-        return jnp.full((1, tokens), own, F32)
-    other = jnp.where(flags[8 + slot] > 0, 0.0, LOW).astype(F32)
-    lane = lax.broadcasted_iota(jnp.int32, (1, 2 * tokens), 1)
-    return jnp.where(lane < tokens, own, other)
-
-
 def gathered(j, polar, qg, kv, near):
     cols = pl.ds(j * DH, DH)
     slots = (kv,) + (near[:3] if polar else near)
@@ -57,26 +49,41 @@
     return qq, gg, kk, vv
 
 
-def stats_kernel(heads, tokens, flags, n4, n2, n3, n1, qg, kv, out):
+def is_polar(lat_count):
+    b = lax.axis_index("lat")
+    return (b == 0) | (b == lat_count - 1)
+
+
+def by_band(lat_count, work):
+    polar = is_polar(lat_count)
+    pl.when(polar)(lambda: work(True))
+    pl.when(jnp.logical_not(polar))(lambda: work(False))
+
+
+def stats_kernel(lat_count, heads, tokens, bias_rows, n4, n2, n3, n1, qg, kv, out):
     near = (n1, n2, n3, n4)
 
     def work(polar):
         width = 2 * tokens if polar else tokens
         count = 4 if polar else 5
-        bias = [block_bias(flags, b, tokens, polar) for b in range(count)]
+        bias = [bias_rows[b : b + 1, :width] for b in range(count)]
         tops, sums, deltas = [], [], []
         for j in range(heads):
             qq, gg, kk, vv = gathered(j, polar, qg, kv, near)
             s = dot_nt(kk, qq)
             dp = dot_nt(vv, gg)
-            parts = [s[b * tokens : (b + 1) * tokens] * FACTOR + bias[b] for b in range(count)]
-            top = functools.reduce(jnp.maximum, [jnp.max(x, axis=0, keepdims=True) for x in parts])
-            total = jnp.zeros((1, width), F32)
-            delta = jnp.zeros((1, width), F32)
             for b in range(count):
-                e = jnp.exp2(parts[b] - top)
-                total += jnp.sum(e, axis=0, keepdims=True)
-                delta += jnp.sum(e * dp[b * tokens : (b + 1) * tokens], axis=0, keepdims=True)
+                part = s[b * tokens : (b + 1) * tokens]
+                high = jnp.max(part, axis=0, keepdims=True) * FACTOR + bias[b]
+                if b:
+                    high = jnp.maximum(top, high)
+                e = jnp.exp2((part * FACTOR + bias[b]) - high)
+                one = jnp.sum(e, axis=0, keepdims=True)
+                two = jnp.sum(e * dp[b * tokens : (b + 1) * tokens], axis=0, keepdims=True)
+                if b:
+                    fade = jnp.exp2(top - high)
+                    one, two = total * fade + one, delta * fade + two
+                top, total, delta = high, one, two
             tops.append(top)
             sums.append(total)
             deltas.append(delta)
@@ -88,18 +95,17 @@
         if not polar:
             out[: 3 * heads, tokens:] = jnp.zeros((3 * heads, tokens), F32)
 
-    pl.when(flags[7] > 0)(lambda: work(True))
-    pl.when(flags[7] == 0)(lambda: work(False))
-
-
-def grads_kernel(heads, tokens, flags, n4, n2, n3, n1, mine, theirs, qg, kv, att, dq, dk, dv, r1, r2, r3, r4):
+    by_band(lat_count, work)
+
+
+def grads_kernel(lat_count, heads, tokens, bias_rows, n4, n2, n3, n1, mine, theirs, qg, kv, att, dq, dk, dv, r1, r2, r3, r4):
     near = (n1, n2, n3, n4)
     back = (r1, r2, r3, r4)
 
     def work(polar):
         width = 2 * tokens if polar else tokens
         count = 4 if polar else 5
-        bias = [block_bias(flags, b, tokens, polar) for b in range(count)]
+        bias = [bias_rows[b : b + 1, :width] for b in range(count)]
         for j in range(heads):
             cols = pl.ds(j * DH, DH)
             top, total, delta = [mine[r * heads + j : r * heads + j + 1, :width] for r in range(3)]
@@ -145,8 +151,7 @@
                 r4[0, :, cols] = o[tokens:].astype(BF16)
                 r4[1, :, cols] = dqq[tokens:].astype(BF16)
 
-    pl.when(flags[7] > 0)(lambda: work(True))
-    pl.when(flags[7] == 0)(lambda: work(False))
+    by_band(lat_count, work)
 
 
 def exchange_plan(lon_count, lat_count):
@@ -184,15 +189,14 @@
 
 def call(kernel, name, outs, *operands):
     whole = pl.BlockSpec(memory_space=pltpu.VMEM)
-    flags = pl.BlockSpec(memory_space=pltpu.SMEM)
     return pl.pallas_call(
         kernel,
-        in_specs=[flags] + [whole] * (len(operands) - 1),
+        in_specs=[whole] * len(operands),
         out_specs=[whole] * len(outs),
         out_shape=[pltpu.VMEM(shape, dtype) for shape, dtype in outs],
         compiler_params=pltpu.CompilerParams(vmem_limit_bytes=VMEM_BYTES),
         name=name,
-    )(operands[0], *[held(x) for x in operands[1:]])
+    )(*[held(x) for x in operands])
 
 
 def start_all(copies):
@@ -207,7 +211,13 @@
 
 def cut_copies(first, one, two, out, sem, at):
     cut = pl.ds(first, out.shape[2])
-    return [pltpu.make_async_copy(x.at[:, cut], out.at[i], sem.at[at + i]) for i, x in enumerate((one, two))]
+    tall = out.shape[1] // PIECES
+    parts = [pl.ds(i * tall, tall) for i in range(PIECES)]
+    return [
+        pltpu.make_async_copy(x.at[part, cut], out.at[i, part], sem.at[at + i])
+        for i, x in enumerate((one, two))
+        for part in parts
+    ]
 
 
 def start_sends(first, polar, q, k, v, g, kv, chosen, sem):
@@ -217,16 +227,11 @@
     return cut_copies(first, k, v, kv, sem, 0) + cut_copies(first, k, v, chosen, sem, 2)
 
 
-def is_polar(lat_count):
-    b = lax.axis_index("lat")
-    return (b == 0) | (b == lat_count - 1)
-
-
 def first_pack_kernel(lat_count, q, k, v, g, kv, chosen, sem):
     wait_all(start_sends(0, is_polar(lat_count), q, k, v, g, kv, chosen, sem))
 
 
-def later_pack_kernel(firsts, lat_count, lon_count, neighbours_in, partner_in, q, k, v, g, flags, *rest):
+def later_pack_kernel(firsts, lat_count, lon_count, neighbours_in, partner_in, q, k, v, g, bias, *rest):
     *outs, sem, neighbours, partner = rest
     b, s = lax.axis_index("lat"), lax.axis_index("lon")
     polar = is_polar(lat_count)
@@ -265,25 +270,25 @@
     across = jnp.where(s >= half, s - half, s + half)
     pole = jnp.where(b == 0, 0, 1)
 
-    def mark(strip, at, tiles):
+    def linked(strip, tiles):
         tile = b * lon_count + strip
         links = [neighbours[i, tile] for i in range(neighbours.shape[0])]
         links.append(jnp.where(polar, b * lon_count + partner[pole, strip], -9))
-        for i, one in enumerate(tiles):
-            flags[at + i] = functools.reduce(jnp.logical_or, [one == link for link in links]).astype(jnp.int32)
-
-    mark(s, 0, slots)
-    mark(across, 8, slots[:3])
-    flags[7] = polar.astype(jnp.int32)
-    for i in (5, 6, 11, 12, 13, 14, 15):
-        flags[i] = 0
+        found = [functools.reduce(jnp.logical_or, [one == link for link in links]) for one in tiles]
+        return [jnp.where(x, 0.0, LOW).astype(F32) for x in found]
+
+    own, other = linked(s, slots), linked(across, slots[:3])
+    lane = lax.broadcasted_iota(jnp.int32, (1, bias.shape[1]), 1)
+    for i in range(bias.shape[0]):
+        row = [x[i] if i < len(x) else jnp.float32(LOW) for x in (own, other)]
+        bias[i : i + 1, :] = jnp.where(lane < bias.shape[1] // 2, row[0], row[1])
     wait_all(copies)
 
 
 def pack(firsts, widths, lat_count, lon_count, neighbours, partner, q, k, v, g):
     tokens = q.shape[0]
     pairs = [pltpu.VMEM((2, tokens, wide), BF16) for wide in widths]
-    smem, vmem, anywhere = [pl.BlockSpec(memory_space=m) for m in (pltpu.SMEM, pltpu.VMEM, pl.ANY)]
+    vmem, anywhere = [pl.BlockSpec(memory_space=m) for m in (pltpu.VMEM, pl.ANY)]
     far = [pltpu.with_memory_space_constraint(x, pltpu.HBM) for x in (neighbours, partner, q, k, v, g)]
     params = pltpu.CompilerParams(vmem_limit_bytes=VMEM_BYTES)
     kv, chosen = pl.pallas_call(
@@ -297,11 +302,11 @@
     )(*far[2:])
     count = len(widths)
     later = [pair for pair in pairs[1:] for _ in range(2)]
-    flags, *outs = pl.pallas_call(
+    bias, *outs = pl.pallas_call(
         functools.partial(later_pack_kernel, firsts, lat_count, lon_count),
         in_specs=[anywhere] * 6,
-        out_specs=[smem] + [vmem] * (count + len(later)),
-        out_shape=[jax.ShapeDtypeStruct((16,), jnp.int32)] + pairs + later,
+        out_specs=[vmem] * (1 + count + len(later)),
+        out_shape=[pltpu.VMEM((8, 2 * tokens), F32)] + pairs + later,
         scratch_shapes=[
             pltpu.SemaphoreType.DMA((count, 8)),
             pltpu.SMEM(neighbours.shape, jnp.int32),
@@ -311,41 +316,48 @@
         name="later_pack",
     )(*far)
     sends = [(kv, chosen)] + [outs[count + 2 * c - 2 : count + 2 * c] for c in range(1, count)]
-    return flags, [(sends[c][0], outs[c], sends[c][1]) for c in range(count)]
+    return bias, [(sends[c][0], outs[c], sends[c][1]) for c in range(count)]
 
 
 def after(x, *others):
     return lax.optimization_barrier((x, *others))[0]
 
 
-def finish_kernel(flags, b4, b2, b3, b1, att, dq, dk, dv, *rest):
-    o_att, o_dq, o_dk, o_dv = rest[-4:]
-    inner = jnp.where(flags[7] > 0, 0.0, 1.0).astype(F32)
-    fourth = [b4[i].astype(F32) for i in range(2)]
-    o_att[...] = (att[...] + (1.0 - inner) * fourth[0]).astype(BF16)
-    o_dq[...] = (SCALE * (dq[...] + (1.0 - inner) * fourth[1])).astype(BF16)
-    terms = [b1[i].astype(F32) + b2[i].astype(F32) + b3[i].astype(F32) + inner * fourth[i] for i in range(2)]
-    o_dk[...] = (SCALE * (dk[...] + terms[0])).astype(BF16)
-    o_dv[...] = (dv[...] + terms[1]).astype(BF16)
-
-
-def finish(first, features, flags, parts, returned, before):
+def finish_kernel(lat_count, first, step, b4, b2, b3, b1, att, dq, dk, dv, *rest):
+    outs, (made, sem) = rest[-6:-2], rest[-2:]
+    inner = jnp.where(is_polar(lat_count), 0.0, 1.0).astype(F32)
+    wide = att.shape[1]
+    copies = []
+    for i in range(wide // step):
+        cols = pl.ds(i * step, step)
+        fourth = [b4[j, :, cols].astype(F32) for j in range(2)]
+        terms = [sum(b[j, :, cols].astype(F32) for b in (b1, b2, b3)) + inner * fourth[j] for j in range(2)]
+        made[0, :, cols] = (att[:, cols] + (1.0 - inner) * fourth[0]).astype(BF16)
+        made[1, :, cols] = (SCALE * (dq[:, cols] + (1.0 - inner) * fourth[1])).astype(BF16)
+        made[2, :, cols] = (SCALE * (dk[:, cols] + terms[0])).astype(BF16)
+        made[3, :, cols] = (dv[:, cols] + terms[1]).astype(BF16)
+        for j in range(4):
+            place = outs[j].at[:, pl.ds(first + i * step, step)]
+            copies.append(pltpu.make_async_copy(made.at[j, :, cols], place, sem.at[i, j]))
+            copies[-1].start()
+    wait_all(copies)
+
+
+def finish(lat_count, first, features, parts, returned, before):
     tokens, wide = parts[0].shape
-    block = math.gcd(first, wide) if FINISH_WIDTH == 0 else math.gcd(FINISH_WIDTH * DH, math.gcd(first, wide))
-    flat = pl.BlockSpec((tokens, block), lambda i: (0, i))
-    pair = pl.BlockSpec((2, tokens, block), lambda i: (0, 0, i))
-    place = pl.BlockSpec((tokens, block), lambda i: (0, first // block + i))
-    kept = [pl.BlockSpec(memory_space=pl.ANY)] * len(before)
+    step = DH * math.gcd(wide // DH, FINISH_HEADS)
+    vmem, anywhere = [pl.BlockSpec(memory_space=m) for m in (pltpu.VMEM, pl.ANY)]
+    near = [held(x) for x in (*[returned[i] for i in (3, 1, 2, 0)], *parts)]
     return pl.pallas_call(
-        finish_kernel,
-        grid=(wide // block,),
-        in_specs=[pl.BlockSpec(memory_space=pltpu.SMEM)] + [pair] * 4 + [flat] * 4 + kept,
-        out_specs=[place] * 4,
+        functools.partial(finish_kernel, lat_count, first, step),
+        in_specs=[vmem] * 8 + [anywhere] * len(before),
+        out_specs=[anywhere] * 4,
         out_shape=[jax.ShapeDtypeStruct((tokens, features), BF16)] * 4,
-        input_output_aliases={9 + i: i for i in range(len(before))},
+        input_output_aliases={8 + i: i for i in range(len(before))},
+        scratch_shapes=[pltpu.VMEM((4, tokens, wide), BF16), pltpu.SemaphoreType.DMA((wide // step, 4))],
         compiler_params=pltpu.CompilerParams(vmem_limit_bytes=VMEM_BYTES),
         name="finish",
-    )(flags, *[returned[i] for i in (3, 1, 2, 0)], *parts, *before)
+    )(*near, *before)
 
 
 def body(queries, keys, values, out_grad, neighbours, partner):
@@ -366,35 +378,41 @@
             out[i] = lax.ppermute(after(operands[i], *ties[i]) if ties[i] else operands[i], axes, plan[i])
         return out
 
-    flags, packed = pack(firsts, widths, lat_count, lon_count, neighbours.T, partner, q, k, v, g)
+    bias, packed = pack(firsts, widths, lat_count, lon_count, neighbours.T, partner, q, k, v, g)
 
     near = []
     for c in range(chunks):
         kv, qg, chosen = packed[c]
-        ties = [[]] * 4 if c == 0 else [[near[-1][i] for i in tie] for tie in TIES]
+        ties = [[bias] * i for i in FIRST] if c == 0 else [[near[-1][i] for i in tie] for tie in TIES]
         near.append(exchange((kv, kv, kv, chosen), ties))
 
-    mine, theirs = [], []
+    def statistics(c, ties=()):
+        kv, qg, chosen = packed[c]
+        kernel = functools.partial(stats_kernel, lat_count, counts[c], tokens)
+        outs = [((-(-3 * counts[c] // 8) * 8, 2 * tokens), F32)]
+        mine.extend(call(kernel, "stats", outs, after(bias, *ties), *[near[c][i] for i in (3, 1, 2, 0)], qg, kv))
+        theirs.append(lax.ppermute(mine[c], axes, plan[3]))
+
+    def gradients(c):
+        kv, qg, chosen = packed[c]
+        kernel = functools.partial(grads_kernel, lat_count, counts[c], tokens)
+        outs = [((tokens, widths[c]), F32)] * 4 + [((2, tokens, widths[c]), BF16)] * 4
+        return call(kernel, "grads", outs, bias, *[near[c][i] for i in (3, 1, 2, 0)], mine[c], theirs[c], qg, kv)
+
+    mine, theirs, done = [], [], []
+    statistics(0)
     for c in range(chunks):
-        kv, qg, chosen = packed[c]
-        kernel = functools.partial(stats_kernel, counts[c], tokens)
-        mine += call(kernel, "stats", [((-(-3 * counts[c] // 8) * 8, 2 * tokens), F32)], flags, *[near[c][i] for i in (3, 1, 2, 0)], qg, kv)
-        theirs.append(lax.ppermute(mine[c], axes, plan[3]))
-    done = []
-    for c in range(chunks):
-        kv, qg, chosen = packed[c]
-        other = after(theirs[c], mine[c + 1]) if AHEAD and c + 1 < chunks else theirs[c]
-        kernel = functools.partial(grads_kernel, counts[c], tokens)
-        outs = [((tokens, widths[c]), F32)] * 4 + [((2, tokens, widths[c]), BF16)] * 4
-        results = call(kernel, "grads", outs, flags, *[near[c][i] for i in (3, 1, 2, 0)], mine[c], other, qg, kv)
+        results = gradients(c)
+        ties = [[]] * 4
         if c + 1 < chunks:
-            ties = [[theirs[c + 1]] if i in LATE else [] for i in range(4)]
-        else:
-            ties = [[done[-1][1][i] for i in tie] for tie in LAST]
+            statistics(c + 1, results[:1])
+            ties = [[mine[c + 1]] * (LATE[i] == 1) + [theirs[c + 1]] * (LATE[i] == 2) for i in range(4)]
+        if c > 0:
+            ties = [ties[i] + [done[-1][1][j] for j in LAST[i]] for i in range(4)]
         done.append((results[:4], exchange(results[4:], ties)))
     outs = []
     for c in range(chunks):
-        outs = finish(firsts[c], features, flags, *done[c], outs)
+        outs = finish(lat_count, firsts[c], features, *done[c], outs)
     return tuple(x.reshape(tile_rows, tile_cols, features) for x in outs)
 
 

time: 56.2 us -> 52.6 us (0.936)
  Pallas kernels: 16.4 us -> 12.7 us
  starting transfers between devices: 18.6 us -> 21.1 us
  waiting for transfers between devices: 19.8 us -> 17.8 us
    ppermute x16, waiting for transfers between devices: 19.8 us -> 13.1 us  [exchange(): lax.ppermute(after(operands[i], *ties[i]) if ties[i] else operands[i], ax...]
    ppermute x2, waiting for transfers between devices: 0.01 us -> 4.72 us  [statistics(): theirs.append(lax.ppermute(mine[c], axes, plan[3]))]
    pallas_call x6, Pallas kernels: 13 us -> 9.81 us  [the longest x4 7.41 us: call(): pl.pallas_call(kernel, in_specs=[whole] * len(operands), out_specs=[whole...]
    ppermute x16, starting transfers between devices: 15.8 us -> 18.2 us  [exchange(): lax.ppermute(after(operands[i], *ties[i]) if ties[i] else operands[i], ax...]
    pallas_call x1, Pallas kernels: 2.19 us -> 1.6 us  [pack(): pl.pallas_call(functools.partial(later_pack_kernel, firsts, lat_count, lo...]
  transfers between devices with their start and end apart: 18 -> 18, of which waited for: 9 -> 6; matrix products, arithmetic and copies ran while one was open for 0% -> 0% of each run, Pallas kernels for 24% -> 17%
where the time goes in v3:
time: 52.6 us; the launch traced here: 52.4 us
  starting transfers between devices  21.1 us (40%)
  waiting for transfers between devices  17.8 us (34%)
  Pallas kernels  12.7 us (24%)
  between operations  0.88 us (2%)
    ppermute x16, starting transfers between devices, exchange(): lax.ppermute(after(operands[i], *ties[i]) if ties[i] else operands[i], ax...  18.2 us
    ppermute x16, waiting for transfers between devices, exchange(): lax.ppermute(after(operands[i], *ties[i]) if ties[i] else operands[i], ax...  13.1 us
    pallas_call x4, Pallas kernels, call(): pl.pallas_call(kernel, in_specs=[whole] * len(operands), out_specs=[whole...  7.41 us
    ppermute x2, waiting for transfers between devices, statistics(): theirs.append(lax.ppermute(mine[c], axes, plan[3]))  4.72 us
    ppermute x2, starting transfers between devices, statistics(): theirs.append(lax.ppermute(mine[c], axes, plan[3]))  2.87 us
    pallas_call x2, Pallas kernels, finish(): pl.pallas_call(functools.partial(finish_kernel, lat_count, first, step),...  2.41 us
    pallas_call x1, Pallas kernels, pack(): pl.pallas_call(functools.partial(later_pack_kernel, firsts, lat_count, lo...  1.6 us
    pallas_call x1, Pallas kernels, pack(): pl.pallas_call(functools.partial(first_pack_kernel, lat_count), in_specs=...  1.26 us
  transfers between devices with their start and end apart: 18, of which 6 were waited for; matrix products, arithmetic and copies ran while one was open for 0% of the time, Pallas kernels for 17%

profile of v3, /device:TPU:0, one launch (start us, length us, event | category | flops | bytes accessed | tf_op | source)
XLA Modules:
  0.0 52.4 jit_solution(10991596286278149751)
XLA Ops:
  0.6 1.3 %first_pack.1 = (bf16[2,128,768]{2,1,0:T(8,128)(2,1)S(1)}, bf16[2,128,768]{2,1,0:T(8,128)(2,1)S(1)}) custom-call(bf16[128,1536]{1,0:T(8,128)(2,1)} %bitcast.9, bf16[128,1536]{1,0:T(8,128)(2,1)} %bitcast.11, bf16[128,1536]{1,0:T(8,128)(2,1)} %bitcast.13, bf16[128,1536]{1,0:T(8,128)(2,1)} %bitcast.15), custom_call_target="tpu_custom_call" | custom-call | tf_op jit(solution)/shard_map/first_pack/pallas_call | solution.py:294
  1.9 0.5 collective-permute-start
  2.4 2.6 %collective-permute-start.3 = (bf16[2,128,768]{2,1,0:T(8,128)(2,1)S(1)}, bf16[2,128,768]{2,1,0:T(8,128)(2,1)S(1)}, u32[]{:S(2)}, u32[]{:S(2)}) collective-permute-start(bf16[2,128,768]{2,1,0:T(8,128)(2,1)S(1)} %get-tuple-element.50), channel_id=1, source_target_pairs={{0,16},{4,20},{8,24},{12,28},{16,0},{20,4},{24,8},{28,12},{1,2},{5... | collective-permute-start | bytes 1179656 | tf_op jit(solution)/shard_map/ppermute | solution.py:378
  5.0 1.3 %collective-permute-start.6 = (bf16[2,128,768]{2,1,0:T(8,128)(2,1)S(1)}, bf16[2,128,768]{2,1,0:T(8,128)(2,1)S(1)}, u32[]{:S(2)}, u32[]{:S(2)}) collective-permute-start(bf16[2,128,768]{2,1,0:T(8,128)(2,1)S(1)} %get-tuple-element.46.kv), channel_id=1, source_target_pairs={{0,12},{4,8},{8,4},{12,0},{16,28},{20,24},{24,20},{28,16},{1,29},{... | collective-permute-start | bytes 1179656 | tf_op jit(solution)/shard_map/ppermute | solution.py:378
  6.3 2.6 %collective-permute-start.7 = (bf16[2,128,768]{2,1,0:T(8,128)(2,1)S(1)}, bf16[2,128,768]{2,1,0:T(8,128)(2,1)S(1)}, u32[]{:S(2)}, u32[]{:S(2)}) collective-permute-start(bf16[2,128,768]{2,1,0:T(8,128)(2,1)S(1)} %get-tuple-element.46.kv), channel_id=1, source_target_pairs={{0,1},{4,5},{8,9},{12,13},{16,17},{20,21},{24,25},{28,29},{1,0},{5... | collective-permute-start | bytes 1179656 | tf_op jit(solution)/shard_map/ppermute | solution.py:378
  8.9 1.6 %later_pack.1 = (f32[8,256]{1,0:T(8,128)S(1)}, bf16[2,128,768]{2,1,0:T(8,128)(2,1)S(1)}, bf16[2,128,768]{2,1,0:T(8,128)(2,1)S(1)}, bf16[2,128,768]{2,1,0:T(8,128)(2,1)S(1)}, bf16[2,128,768]{2,1,0:T(8,128)(2,1)S(1)}) custom-call(s32[5,32]{1,0:T(8,128)} %bitcast.21, s32[2,8]{1,0:T(2,128)} %partner_in.1, bf16[128,1536]{1,0:T(8,128)(2,1)} %bitcast.10, ...), custom_call_target="tpu_custom_call" | custom-call | tf_op jit(solution)/shard_map/later_pack/pallas_call | solution.py:305
  10.5 0.0 collective-permute-done.n1
  10.5 0.3 collective-permute-start.2
  10.7 0.5 collective-permute-start.1
  11.3 3.7 %collective-permute-done.3.n4 = bf16[2,128,768]{2,1,0:T(8,128)(2,1)S(1)} collective-permute-done((bf16[2,128,768]{2,1,0:T(8,128)(2,1)S(1)}, bf16[2,128,768]{2,1,0:T(8,128)(2,1)S(1)}, u32[]{:S(2)}, u32[]{:S(2)}) %collective-permute-start.3) | collective-permute-done | bytes 393248 | tf_op jit(solution)/shard_map/ppermute | solution.py:378
  15.0 2.0 %collective-permute-start.4 = (bf16[2,128,768]{2,1,0:T(8,128)(2,1)S(1)}, bf16[2,128,768]{2,1,0:T(8,128)(2,1)S(1)}, u32[]{:S(2)}, u32[]{:S(2)}) collective-permute-start(bf16[2,128,768]{2,1,0:T(8,128)(2,1)S(1)} %get-tuple-element.51.kv), channel_id=1, source_target_pairs={{0,1},{4,5},{8,9},{12,13},{16,17},{20,21},{24,25},{28,29},{1,0},{5... | collective-permute-start | bytes 1179656 | tf_op jit(solution)/shard_map/ppermute | solution.py:378
  17.0 0.0 collective-permute-done.6.n2
  17.0 0.0 collective-permute-start.5
  17.0 1.1 %collective-permute-done.7.n3 = bf16[2,128,768]{2,1,0:T(8,128)(2,1)S(1)} collective-permute-done((bf16[2,128,768]{2,1,0:T(8,128)(2,1)S(1)}, bf16[2,128,768]{2,1,0:T(8,128)(2,1)S(1)}, u32[]{:S(2)}, u32[]{:S(2)}) %collective-permute-start.7) | collective-permute-done | bytes 393248 | tf_op jit(solution)/shard_map/ppermute | solution.py:378
  18.0 1.3 %stats.2.mine = f32[24,256]{1,0:T(8,128)S(1)} custom-call(f32[8,256]{1,0:T(8,128)S(1)} %get-tuple-element.54.bias_rows, bf16[2,128,768]{2,1,0:T(8,128)(2,1)S(1)} %collective-permute-done.3.n4, bf16[2,128,768]{2,1,0:T(8,128)(2,1)S(1)} %collective-permute-done.6.n2, bf16[2,128,768]{2,1,0:T(8,128)(2,1)S(1)} %collective-permute-done.7.n3, ...), custom_call_target="tpu_custom_call" | custom-call | tf_op jit(solution)/shard_map/stats/pallas_call | solution.py:192
  19.4 1.4 %collective-permute-start.8 = (f32[24,256]{1,0:T(8,128)S(1)}, f32[24,256]{1,0:T(8,128)S(1)}, u32[]{:S(2)}, u32[]{:S(2)}) collective-permute-start(f32[24,256]{1,0:T(8,128)S(1)} %stats.2.mine), channel_id=1, source_target_pairs={{0,16},{4,20},{8,24},{12,28},{16,0},{20,4},{24,8},{28,12},{1,2},{5... | collective-permute-start | bytes 73736 | tf_op jit(solution)/shard_map/ppermute | solution.py:394
  20.7 2.9 %collective-permute-done.8.theirs = f32[24,256]{1,0:T(8,128)S(1)} collective-permute-done((f32[24,256]{1,0:T(8,128)S(1)}, f32[24,256]{1,0:T(8,128)S(1)}, u32[]{:S(2)}, u32[]{:S(2)}) %collective-permute-start.8) | collective-permute-done | bytes 24608 | tf_op jit(solution)/shard_map/ppermute | solution.py:394
  23.7 2.4 %grads.2 = (f32[128,768]{1,0:T(8,128)S(1)}, f32[128,768]{1,0:T(8,128)S(1)}, f32[128,768]{1,0:T(8,128)S(1)}, f32[128,768]{1,0:T(8,128)S(1)}, bf16[2,128,768]{2,1,...) custom-call(f32[8,256]{1,0:T(8,128)S(1)} %get-tuple-element.54.bias_, ...), custom_call_target="tpu_custom_call" | custom-call | tf_op jit(solution)/shard_map/grads/pallas_call | solution.py:192
  26.0 0.0 collective-permute-done.2.n2
  26.0 0.0 collective-permute-done.1.n4
  26.0 0.0 collective-permute-done.4.n3
  26.1 0.0 collective-permute-done.5.n1
  26.1 1.4 %stats.3.mine = f32[24,256]{1,0:T(8,128)S(1)} custom-call(f32[8,256]{1,0:T(8,128)S(1)} %get-tuple-element.54.bias_rows, bf16[2,128,768]{2,1,0:T(8,128)(2,1)S(1)} %collective-permute-done.1.n4, bf16[2,128,768]{2,1,0:T(8,128)(2,1)S(1)} %collective-permute-done.2.n2, bf16[2,128,768]{2,1,0:T(8,128)(2,1)S(1)} %collective-permute-done.4.n3, ...), custom_call_target="tpu_custom_call" | custom-call | tf_op jit(solution)/shard_map/stats/pallas_call | solution.py:192
  27.4 1.3 %collective-permute-start.13 = (bf16[2,128,768]{2,1,0:T(8,128)(2,1)S(1)}, bf16[2,128,768]{2,1,0:T(8,128)(2,1)S(1)}, u32[]{:S(2)}, u32[]{:S(2)}) collective-permute-start(bf16[2,128,768]{2,1,0:T(8,128)(2,1)S(1)} %get-tuple-element.61), channel_id=1, source_target_pairs={{0,1},{4,5},{8,9},{12,13},{16,17},{20,21},{24,25},{28,29},{1,0},{5... | collective-permute-start | bytes 1179656 | tf_op jit(solution)/shard_map/ppermute | solution.py:378
  28.7 0.0 collective-permute-start.17
  28.7 1.6 %collective-permute-start.16 = (bf16[2,128,768]{2,1,0:T(8,128)(2,1)S(1)}, bf16[2,128,768]{2,1,0:T(8,128)(2,1)S(1)}, u32[]{:S(2)}, u32[]{:S(2)}) collective-permute-start(bf16[2,128,768]{2,1,0:T(8,128)(2,1)S(1)} %get-tuple-element.70), channel_id=1, source_target_pairs={{0,12},{4,8},{8,4},{12,0},{16,28},{20,24},{24,20},{28,16},{1,29},{... | collective-permute-start | bytes 1179656 | tf_op jit(solution)/shard_map/ppermute | solution.py:378
  30.3 1.5 %collective-permute-start.9 = (f32[24,256]{1,0:T(8,128)S(1)}, f32[24,256]{1,0:T(8,128)S(1)}, u32[]{:S(2)}, u32[]{:S(2)}) collective-permute-start(f32[24,256]{1,0:T(8,128)S(1)} %stats.3.mine), channel_id=1, source_target_pairs={{0,16},{4,20},{8,24},{12,28},{16,0},{20,4},{24,8},{28,12},{1,2},{5... | collective-permute-start | bytes 73736 | tf_op jit(solution)/shard_map/ppermute | solution.py:394
  31.9 0.5 collective-permute-start.15
  32.4 1.8 %collective-permute-done.9.theirs = f32[24,256]{1,0:T(8,128)S(1)} collective-permute-done((f32[24,256]{1,0:T(8,128)S(1)}, f32[24,256]{1,0:T(8,128)S(1)}, u32[]{:S(2)}, u32[]{:S(2)}) %collective-permute-start.9) | collective-permute-done | bytes 24608 | tf_op jit(solution)/shard_map/ppermute | solution.py:394
  34.2 2.4 %grads.3 = (f32[128,768]{1,0:T(8,128)S(1)}, f32[128,768]{1,0:T(8,128)S(1)}, f32[128,768]{1,0:T(8,128)S(1)}, f32[128,768]{1,0:T(8,128)S(1)}, bf16[2,128,768]{2,1,...) custom-call(f32[8,256]{1,0:T(8,128)S(1)} %get-tuple-element.54.bias_, ...), custom_call_target="tpu_custom_call" | custom-call | tf_op jit(solution)/shard_map/grads/pallas_call | solution.py:192
  36.5 1.8 %collective-permute-start.10 = (bf16[2,128,768]{2,1,0:T(8,128)(2,1)S(1)}, bf16[2,128,768]{2,1,0:T(8,128)(2,1)S(1)}, u32[]{:S(2)}, u32[]{:S(2)}) collective-permute-start(bf16[2,128,768]{2,1,0:T(8,128)(2,1)S(1)} %get-tuple-element.56), channel_id=1, source_target_pairs={{0,16},{4,20},{8,24},{12,28},{16,0},{20,4},{24,8},{28,12},{1,2},{5... | collective-permute-start | bytes 1179656 | tf_op jit(solution)/shard_map/ppermute | solution.py:378
  38.4 0.0 collective-permute-done.13.b3
  38.4 0.0 collective-permute-start.11
  38.4 0.0 collective-permute-done.17.b1
  38.4 3.2 %collective-permute-start.12 = (bf16[2,128,768]{2,1,0:T(8,128)(2,1)S(1)}, bf16[2,128,768]{2,1,0:T(8,128)(2,1)S(1)}, u32[]{:S(2)}, u32[]{:S(2)}) collective-permute-start(bf16[2,128,768]{2,1,0:T(8,128)(2,1)S(1)} %get-tuple-element.58), channel_id=1, source_target_pairs={{0,1},{4,5},{8,9},{12,13},{16,17},{20,21},{24,25},{28,29},{1,0},{5... | collective-permute-start | bytes 1179656 | tf_op jit(solution)/shard_map/ppermute | solution.py:378
  41.6 0.0 collective-permute-done.16.b2
  41.6 0.0 collective-permute-start.14
  41.6 2.3 %collective-permute-done.15.b4 = bf16[2,128,768]{2,1,0:T(8,128)(2,1)S(1)} collective-permute-done((bf16[2,128,768]{2,1,0:T(8,128)(2,1)S(1)}, bf16[2,128,768]{2,1,0:T(8,128)(2,1)S(1)}, u32[]{:S(2)}, u32[]{:S(2)}) %collective-permute-start.15) | collective-permute-done | bytes 393248 | tf_op jit(solution)/shard_map/ppermute | solution.py:378
  43.9 1.2 %finish.2 = (bf16[128,1536]{1,0:T(8,128)(2,1)}, bf16[128,1536]{1,0:T(8,128)(2,1)}, bf16[128,1536]{1,0:T(8,128)(2,1)}, bf16[128,1536]{1,0:T(8,128)(2,1)}) custom-call(bf16[2,128,768]{2,1,0:T(8,128)(2,1)S(1)} %collective-permute-done.15.b4, bf16[2,128,768]{2,1,0:T(8,128)(2,1)S(1)} %collective-permute-done.16.b2, ...), custom_call_target="tpu_custom_call" | custom-call | tf_op jit(solution)/shard_map/finish/pallas_call | solution.py:351
  45.1 5.9 %collective-permute-done.10.b4 = bf16[2,128,768]{2,1,0:T(8,128)(2,1)S(1)} collective-permute-done((bf16[2,128,768]{2,1,0:T(8,128)(2,1)S(1)}, bf16[2,128,768]{2,1,0:T(8,128)(2,1)S(1)}, u32[]{:S(2)}, u32[]{:S(2)}) %collective-permute-start.10) | collective-permute-done | bytes 393248 | tf_op jit(solution)/shard_map/ppermute | solution.py:378
  51.0 0.0 collective-permute-done.11.b2
  51.0 0.0 collective-permute-done.12.b3
  51.0 0.0 collective-permute-done.14.b1
  51.0 1.2 %finish.3 = (bf16[128,1536]{1,0:T(8,128)(2,1)}, bf16[128,1536]{1,0:T(8,128)(2,1)}, bf16[128,1536]{1,0:T(8,128)(2,1)}, bf16[128,1536]{1,0:T(8,128)(2,1)}) custom-call(bf16[2,128,768]{2,1,0:T(8,128)(2,1)S(1)} %collective-permute-done.10.b4, ...), custom_call_target="tpu_custom_call", output_to_operand_aliasing={{0}: (8, {}), {1}: (9, {}), {2}: (10, {}), {3}: (11, {})} | custom-call | tf_op jit(solution)/shard_map/finish/pallas_call | solution.py:351
Async XLA Ops:
  1.9 8.6 %collective-permute-start = (bf16[2,128,768]{2,1,0:T(8,128)(2,1)S(1)}, bf16[2,128,768]{2,1,0:T(8,128)(2,1)S(1)}, u32[]{:S(2)}, u32[]{:S(2)}) collective-permute-start(bf16[2,128,768]{2,1,0:T(8,128)(2,1)S(1)} %get-tuple-element.46.kv), channel_id=1, source_target_pairs={{0,4},{4,0},{8,12},{12,8},{16,20},{20,16},{24,28},{28,24},{1,5},{5... | collective-permute-start | bytes 1179656 | tf_op jit(solution)/shard_map/ppermute | solution.py:378
  2.4 12.6 %collective-permute-start.3 = (bf16[2,128,768]{2,1,0:T(8,128)(2,1)S(1)}, bf16[2,128,768]{2,1,0:T(8,128)(2,1)S(1)}, u32[]{:S(2)}, u32[]{:S(2)}) collective-permute-start(bf16[2,128,768]{2,1,0:T(8,128)(2,1)S(1)} %get-tuple-element.50), channel_id=1, source_target_pairs={{0,16},{4,20},{8,24},{12,28},{16,0},{20,4},{24,8},{28,12},{1,2},{5... | collective-permute-start | bytes 1179656 | tf_op jit(solution)/shard_map/ppermute | solution.py:378
  5.0 12.0 %collective-permute-start.6 = (bf16[2,128,768]{2,1,0:T(8,128)(2,1)S(1)}, bf16[2,128,768]{2,1,0:T(8,128)(2,1)S(1)}, u32[]{:S(2)}, u32[]{:S(2)}) collective-permute-start(bf16[2,128,768]{2,1,0:T(8,128)(2,1)S(1)} %get-tuple-element.46.kv), channel_id=1, source_target_pairs={{0,12},{4,8},{8,4},{12,0},{16,28},{20,24},{24,20},{28,16},{1,29},{... | collective-permute-start | bytes 1179656 | tf_op jit(solution)/shard_map/ppermute | solution.py:378
  6.3 11.8 %collective-permute-start.7 = (bf16[2,128,768]{2,1,0:T(8,128)(2,1)S(1)}, bf16[2,128,768]{2,1,0:T(8,128)(2,1)S(1)}, u32[]{:S(2)}, u32[]{:S(2)}) collective-permute-start(bf16[2,128,768]{2,1,0:T(8,128)(2,1)S(1)} %get-tuple-element.46.kv), channel_id=1, source_target_pairs={{0,1},{4,5},{8,9},{12,13},{16,17},{20,21},{24,25},{28,29},{1,0},{5... | collective-permute-start | bytes 1179656 | tf_op jit(solution)/shard_map/ppermute | solution.py:378
  10.5 15.6 %collective-permute-start.2 = (bf16[2,128,768]{2,1,0:T(8,128)(2,1)S(1)}, bf16[2,128,768]{2,1,0:T(8,128)(2,1)S(1)}, u32[]{:S(2)}, u32[]{:S(2)}) collective-permute-start(bf16[2,128,768]{2,1,0:T(8,128)(2,1)S(1)} %get-tuple-element.51.kv), channel_id=1, source_target_pairs={{0,12},{4,8},{8,4},{12,0},{16,28},{20,24},{24,20},{28,16},{1,29},{... | collective-permute-start | bytes 1179656 | tf_op jit(solution)/shard_map/ppermute | solution.py:378
  10.7 15.3 %collective-permute-start.1 = (bf16[2,128,768]{2,1,0:T(8,128)(2,1)S(1)}, bf16[2,128,768]{2,1,0:T(8,128)(2,1)S(1)}, u32[]{:S(2)}, u32[]{:S(2)}) collective-permute-start(bf16[2,128,768]{2,1,0:T(8,128)(2,1)S(1)} %get-tuple-element.47), channel_id=1, source_target_pairs={{0,16},{4,20},{8,24},{12,28},{16,0},{20,4},{24,8},{28,12},{1,2},{5... | collective-permute-start | bytes 1179656 | tf_op jit(solution)/shard_map/ppermute | solution.py:378
  15.0 11.1 %collective-permute-start.4 = (bf16[2,128,768]{2,1,0:T(8,128)(2,1)S(1)}, bf16[2,128,768]{2,1,0:T(8,128)(2,1)S(1)}, u32[]{:S(2)}, u32[]{:S(2)}) collective-permute-start(bf16[2,128,768]{2,1,0:T(8,128)(2,1)S(1)} %get-tuple-element.51.kv), channel_id=1, source_target_pairs={{0,1},{4,5},{8,9},{12,13},{16,17},{20,21},{24,25},{28,29},{1,0},{5... | collective-permute-start | bytes 1179656 | tf_op jit(solution)/shard_map/ppermute | solution.py:378
  17.0 9.1 %collective-permute-start.5 = (bf16[2,128,768]{2,1,0:T(8,128)(2,1)S(1)}, bf16[2,128,768]{2,1,0:T(8,128)(2,1)S(1)}, u32[]{:S(2)}, u32[]{:S(2)}) collective-permute-start(bf16[2,128,768]{2,1,0:T(8,128)(2,1)S(1)} %get-tuple-element.51.kv), channel_id=1, source_target_pairs={{0,4},{4,0},{8,12},{12,8},{16,20},{20,16},{24,28},{28,24},{1,5},{5... | collective-permute-start | bytes 1179656 | tf_op jit(solution)/shard_map/ppermute | solution.py:378
  19.4 4.3 %collective-permute-start.8 = (f32[24,256]{1,0:T(8,128)S(1)}, f32[24,256]{1,0:T(8,128)S(1)}, u32[]{:S(2)}, u32[]{:S(2)}) collective-permute-start(f32[24,256]{1,0:T(8,128)S(1)} %stats.2.mine), channel_id=1, source_target_pairs={{0,16},{4,20},{8,24},{12,28},{16,0},{20,4},{24,8},{28,12},{1,2},{5... | collective-permute-start | bytes 73736 | tf_op jit(solution)/shard_map/ppermute | solution.py:394
  27.4 10.9 %collective-permute-start.13 = (bf16[2,128,768]{2,1,0:T(8,128)(2,1)S(1)}, bf16[2,128,768]{2,1,0:T(8,128)(2,1)S(1)}, u32[]{:S(2)}, u32[]{:S(2)}) collective-permute-start(bf16[2,128,768]{2,1,0:T(8,128)(2,1)S(1)} %get-tuple-element.61), channel_id=1, source_target_pairs={{0,1},{4,5},{8,9},{12,13},{16,17},{20,21},{24,25},{28,29},{1,0},{5... | collective-permute-start | bytes 1179656 | tf_op jit(solution)/shard_map/ppermute | solution.py:378
  28.7 9.6 %collective-permute-start.17 = (bf16[2,128,768]{2,1,0:T(8,128)(2,1)S(1)}, bf16[2,128,768]{2,1,0:T(8,128)(2,1)S(1)}, u32[]{:S(2)}, u32[]{:S(2)}) collective-permute-start(bf16[2,128,768]{2,1,0:T(8,128)(2,1)S(1)} %get-tuple-element.72), channel_id=1, source_target_pairs={{0,4},{4,0},{8,12},{12,8},{16,20},{20,16},{24,28},{28,24},{1,5},{5... | collective-permute-start | bytes 1179656 | tf_op jit(solution)/shard_map/ppermute | solution.py:378
  28.7 12.9 %collective-permute-start.16 = (bf16[2,128,768]{2,1,0:T(8,128)(2,1)S(1)}, bf16[2,128,768]{2,1,0:T(8,128)(2,1)S(1)}, u32[]{:S(2)}, u32[]{:S(2)}) collective-permute-start(bf16[2,128,768]{2,1,0:T(8,128)(2,1)S(1)} %get-tuple-element.70), channel_id=1, source_target_pairs={{0,12},{4,8},{8,4},{12,0},{16,28},{20,24},{24,20},{28,16},{1,29},{... | collective-permute-start | bytes 1179656 | tf_op jit(solution)/shard_map/ppermute | solution.py:378
  30.3 3.8 %collective-permute-start.9 = (f32[24,256]{1,0:T(8,128)S(1)}, f32[24,256]{1,0:T(8,128)S(1)}, u32[]{:S(2)}, u32[]{:S(2)}) collective-permute-start(f32[24,256]{1,0:T(8,128)S(1)} %stats.3.mine), channel_id=1, source_target_pairs={{0,16},{4,20},{8,24},{12,28},{16,0},{20,4},{24,8},{28,12},{1,2},{5... | collective-permute-start | bytes 73736 | tf_op jit(solution)/shard_map/ppermute | solution.py:394
  31.9 12.0 %collective-permute-start.15 = (bf16[2,128,768]{2,1,0:T(8,128)(2,1)S(1)}, bf16[2,128,768]{2,1,0:T(8,128)(2,1)S(1)}, u32[]{:S(2)}, u32[]{:S(2)}) collective-permute-start(bf16[2,128,768]{2,1,0:T(8,128)(2,1)S(1)} %get-tuple-element.68), channel_id=1, source_target_pairs={{0,16},{4,20},{8,24},{12,28},{16,0},{20,4},{24,8},{28,12},{1,2},{5... | collective-permute-start | bytes 1179656 | tf_op jit(solution)/shard_map/ppermute | solution.py:378
  36.5 14.5 %collective-permute-start.10 = (bf16[2,128,768]{2,1,0:T(8,128)(2,1)S(1)}, bf16[2,128,768]{2,1,0:T(8,128)(2,1)S(1)}, u32[]{:S(2)}, u32[]{:S(2)}) collective-permute-start(bf16[2,128,768]{2,1,0:T(8,128)(2,1)S(1)} %get-tuple-element.56), channel_id=1, source_target_pairs={{0,16},{4,20},{8,24},{12,28},{16,0},{20,4},{24,8},{28,12},{1,2},{5... | collective-permute-start | bytes 1179656 | tf_op jit(solution)/shard_map/ppermute | solution.py:378
  38.4 12.7 %collective-permute-start.11 = (bf16[2,128,768]{2,1,0:T(8,128)(2,1)S(1)}, bf16[2,128,768]{2,1,0:T(8,128)(2,1)S(1)}, u32[]{:S(2)}, u32[]{:S(2)}) collective-permute-start(bf16[2,128,768]{2,1,0:T(8,128)(2,1)S(1)} %get-tuple-element.57), channel_id=1, source_target_pairs={{0,12},{4,8},{8,4},{12,0},{16,28},{20,24},{24,20},{28,16},{1,29},{... | collective-permute-start | bytes 1179656 | tf_op jit(solution)/shard_map/ppermute | solution.py:378
  38.4 12.7 %collective-permute-start.12 = (bf16[2,128,768]{2,1,0:T(8,128)(2,1)S(1)}, bf16[2,128,768]{2,1,0:T(8,128)(2,1)S(1)}, u32[]{:S(2)}, u32[]{:S(2)}) collective-permute-start(bf16[2,128,768]{2,1,0:T(8,128)(2,1)S(1)} %get-tuple-element.58), channel_id=1, source_target_pairs={{0,1},{4,5},{8,9},{12,13},{16,17},{20,21},{24,25},{28,29},{1,0},{5... | collective-permute-start | bytes 1179656 | tf_op jit(solution)/shard_map/ppermute | solution.py:378
  41.6 9.4 %collective-permute-start.14 = (bf16[2,128,768]{2,1,0:T(8,128)(2,1)S(1)}, bf16[2,128,768]{2,1,0:T(8,128)(2,1)S(1)}, u32[]{:S(2)}, u32[]{:S(2)}) collective-permute-start(bf16[2,128,768]{2,1,0:T(8,128)(2,1)S(1)} %get-tuple-element.62), channel_id=1, source_target_pairs={{0,4},{4,0},{8,12},{12,8},{16,20},{20,16},{24,28},{28,24},{1,5},{5... | collective-permute-start | bytes 1179656 | tf_op jit(solution)/shard_map/ppermute | solution.py:378

commit v4 on v3

--- a/solution.py
+++ b/solution.py
@@ -10,7 +10,6 @@
 
 DH = 128
 SHARES = (0, 6, 12)
-FINISH_HEADS = 3
 ORDER = (3, 1, 2, 0)
 TIES = ((3,), (0,), (3,), (0,))
 LATE = (1, 1, 1, 1)
@@ -323,41 +322,65 @@
     return lax.optimization_barrier((x, *others))[0]
 
 
-def finish_kernel(lat_count, first, step, b4, b2, b3, b1, att, dq, dk, dv, *rest):
+def send_out(made, values, outs, cut, sem):
+    for j, value in enumerate(values):
+        made[j] = value.astype(BF16)
+        pltpu.make_async_copy(made.at[j], outs[j].at[:, cut], sem.at[j]).start()
+    for j in range(2):
+        pltpu.make_async_copy(made.at[j], outs[j].at[:, cut], sem.at[j]).wait()
+
+
+def early_finish_kernel(lat_count, first, b2, b3, b1, att, dq, dk, dv, *rest):
+    outs, (kept, made, sem) = rest[-7:-3], rest[-3:]
+    cut = pl.ds(first, att.shape[1])
+    terms = [sum(b[j].astype(F32) for b in (b1, b2, b3)) for j in range(2)]
+    keys, vals = dk[...] + terms[0], dv[...] + terms[1]
+
+    def work(polar):
+        if polar:
+            kept[0], kept[1] = att[...], dq[...]
+            send_out(made, (SCALE * keys, vals), outs[2:], cut, sem)
+        else:
+            kept[0], kept[1] = keys, vals
+            send_out(made, (att[...], SCALE * dq[...]), outs[:2], cut, sem)
+
+    by_band(lat_count, work)
+
+
+def late_finish_kernel(lat_count, first, b4, kept, *rest):
     outs, (made, sem) = rest[-6:-2], rest[-2:]
-    inner = jnp.where(is_polar(lat_count), 0.0, 1.0).astype(F32)
-    wide = att.shape[1]
-    copies = []
-    for i in range(wide // step):
-        cols = pl.ds(i * step, step)
-        fourth = [b4[j, :, cols].astype(F32) for j in range(2)]
-        terms = [sum(b[j, :, cols].astype(F32) for b in (b1, b2, b3)) + inner * fourth[j] for j in range(2)]
-        made[0, :, cols] = (att[:, cols] + (1.0 - inner) * fourth[0]).astype(BF16)
-        made[1, :, cols] = (SCALE * (dq[:, cols] + (1.0 - inner) * fourth[1])).astype(BF16)
-        made[2, :, cols] = (SCALE * (dk[:, cols] + terms[0])).astype(BF16)
-        made[3, :, cols] = (dv[:, cols] + terms[1]).astype(BF16)
-        for j in range(4):
-            place = outs[j].at[:, pl.ds(first + i * step, step)]
-            copies.append(pltpu.make_async_copy(made.at[j, :, cols], place, sem.at[i, j]))
-            copies[-1].start()
-    wait_all(copies)
+    cut = pl.ds(first, b4.shape[2])
+    one, two = [kept[j] + b4[j].astype(F32) for j in range(2)]
+
+    def work(polar):
+        if polar:
+            send_out(made, (one, SCALE * two), outs[:2], cut, sem)
+        else:
+            send_out(made, (SCALE * one, two), outs[2:], cut, sem)
+
+    by_band(lat_count, work)
 
 
 def finish(lat_count, first, features, parts, returned, before):
     tokens, wide = parts[0].shape
-    step = DH * math.gcd(wide // DH, FINISH_HEADS)
     vmem, anywhere = [pl.BlockSpec(memory_space=m) for m in (pltpu.VMEM, pl.ANY)]
-    near = [held(x) for x in (*[returned[i] for i in (3, 1, 2, 0)], *parts)]
-    return pl.pallas_call(
-        functools.partial(finish_kernel, lat_count, first, step),
-        in_specs=[vmem] * 8 + [anywhere] * len(before),
-        out_specs=[anywhere] * 4,
-        out_shape=[jax.ShapeDtypeStruct((tokens, features), BF16)] * 4,
-        input_output_aliases={8 + i: i for i in range(len(before))},
-        scratch_shapes=[pltpu.VMEM((4, tokens, wide), BF16), pltpu.SemaphoreType.DMA((wide // step, 4))],
-        compiler_params=pltpu.CompilerParams(vmem_limit_bytes=VMEM_BYTES),
-        name="finish",
-    )(*near, *before)
+    whole = jax.ShapeDtypeStruct((tokens, features), BF16)
+
+    def run(kernel, name, near, before, extra):
+        return pl.pallas_call(
+            functools.partial(kernel, lat_count, first),
+            in_specs=[vmem] * len(near) + [anywhere] * len(before),
+            out_specs=[anywhere] * 4 + [vmem] * len(extra),
+            out_shape=[whole] * 4 + extra,
+            input_output_aliases={len(near) + i: i for i in range(len(before))},
+            scratch_shapes=[pltpu.VMEM((2, tokens, wide), BF16), pltpu.SemaphoreType.DMA((2,))],
+            compiler_params=pltpu.CompilerParams(vmem_limit_bytes=VMEM_BYTES),
+            name=name,
+        )(*[held(x) for x in near], *before)
+
+    near = [returned[i] for i in (1, 2, 0)] + list(parts)
+    *outs, kept = run(early_finish_kernel, "early_finish", near, before, [pltpu.VMEM((2, tokens, wide), F32)])
+    return run(late_finish_kernel, "late_finish", [returned[3], kept], outs, [])
 
 
 def body(queries, keys, values, out_grad, neighbours, partner):

time: 52.6 us -> 53 us (level)
  starting transfers between devices: 21.1 us -> 18.8 us
  Pallas kernels: 12.7 us -> 14.1 us
  waiting for transfers between devices: 17.8 us -> 19 us
    ppermute x16, starting transfers between devices: 18.2 us -> 15.9 us  [exchange(): lax.ppermute(after(operands[i], *ties[i]) if ties[i] else operands[i], ax...]
    pallas_call x2 -> x4, Pallas kernels: 2.41 us -> 3.89 us  [run(): pl.pallas_call(functools.partial(kernel, lat_count, first), in_specs=[vme...]
    ppermute x16, waiting for transfers between devices: 13.1 us -> 14.3 us  [exchange(): lax.ppermute(after(operands[i], *ties[i]) if ties[i] else operands[i], ax...]
  transfers between devices with their start and end apart: 18 -> 18, of which waited for: 6 -> 10; matrix products, arithmetic and copies ran while one was open for 0% -> 0% of each run, Pallas kernels for 17% -> 20%
where the time goes in v4:
time: 53 us; the launch traced here: 52.8 us
  waiting for transfers between devices  19 us (36%)
  starting transfers between devices  18.8 us (35%)
  Pallas kernels  14.1 us (27%)
  between operations  0.9 us (2%)
    ppermute x16, starting transfers between devices, exchange(): lax.ppermute(after(operands[i], *ties[i]) if ties[i] else operands[i], ax...  15.9 us
    ppermute x16, waiting for transfers between devices, exchange(): lax.ppermute(after(operands[i], *ties[i]) if ties[i] else operands[i], ax...  14.3 us
    pallas_call x4, Pallas kernels, call(): pl.pallas_call(kernel, in_specs=[whole] * len(operands), out_specs=[whole...  7.41 us
    ppermute x2, waiting for transfers between devices, statistics(): theirs.append(lax.ppermute(mine[c], axes, plan[3]))  4.72 us
    pallas_call x4, Pallas kernels, run(): pl.pallas_call(functools.partial(kernel, lat_count, first), in_specs=[vme...  3.89 us
    ppermute x2, starting transfers between devices, statistics(): theirs.append(lax.ppermute(mine[c], axes, plan[3]))  2.87 us
    pallas_call x1, Pallas kernels, pack(): pl.pallas_call(functools.partial(later_pack_kernel, firsts, lat_count, lo...  1.6 us
    pallas_call x1, Pallas kernels, pack(): pl.pallas_call(functools.partial(first_pack_kernel, lat_count), in_specs=...  1.26 us
  transfers between devices with their start and end apart: 18, of which 10 were waited for; matrix products, arithmetic and copies ran while one was open for 0% of the time, Pallas kernels for 20%

profile of v4, /device:TPU:0, one launch (start us, length us, event | category | flops | bytes accessed | tf_op | source)
XLA Modules:
  0.0 52.8 jit_solution(11307484015483023830)
XLA Ops:
  0.6 1.3 %first_pack.1 = (bf16[2,128,768]{2,1,0:T(8,128)(2,1)S(1)}, bf16[2,128,768]{2,1,0:T(8,128)(2,1)S(1)}) custom-call(bf16[128,1536]{1,0:T(8,128)(2,1)} %bitcast.13, bf16[128,1536]{1,0:T(8,128)(2,1)} %bitcast.15, bf16[128,1536]{1,0:T(8,128)(2,1)} %bitcast.17, bf16[128,1536]{1,0:T(8,128)(2,1)} %bitcast.19), custom_call_target="tpu_custom_call" | custom-call | tf_op jit(solution)/shard_map/first_pack/pallas_call | solution.py:293
  1.9 0.5 collective-permute-start
  2.4 2.6 %collective-permute-start.3 = (bf16[2,128,768]{2,1,0:T(8,128)(2,1)S(1)}, bf16[2,128,768]{2,1,0:T(8,128)(2,1)S(1)}, u32[]{:S(2)}, u32[]{:S(2)}) collective-permute-start(bf16[2,128,768]{2,1,0:T(8,128)(2,1)S(1)} %get-tuple-element.60), channel_id=1, source_target_pairs={{0,16},{4,20},{8,24},{12,28},{16,0},{20,4},{24,8},{28,12},{1,2},{5... | collective-permute-start | bytes 1179656 | tf_op jit(solution)/shard_map/ppermute | solution.py:401
  5.0 1.3 %collective-permute-start.6 = (bf16[2,128,768]{2,1,0:T(8,128)(2,1)S(1)}, bf16[2,128,768]{2,1,0:T(8,128)(2,1)S(1)}, u32[]{:S(2)}, u32[]{:S(2)}) collective-permute-start(bf16[2,128,768]{2,1,0:T(8,128)(2,1)S(1)} %get-tuple-element.56.kv), channel_id=1, source_target_pairs={{0,12},{4,8},{8,4},{12,0},{16,28},{20,24},{24,20},{28,16},{1,29},{... | collective-permute-start | bytes 1179656 | tf_op jit(solution)/shard_map/ppermute | solution.py:401
  6.3 2.6 %collective-permute-start.7 = (bf16[2,128,768]{2,1,0:T(8,128)(2,1)S(1)}, bf16[2,128,768]{2,1,0:T(8,128)(2,1)S(1)}, u32[]{:S(2)}, u32[]{:S(2)}) collective-permute-start(bf16[2,128,768]{2,1,0:T(8,128)(2,1)S(1)} %get-tuple-element.56.kv), channel_id=1, source_target_pairs={{0,1},{4,5},{8,9},{12,13},{16,17},{20,21},{24,25},{28,29},{1,0},{5... | collective-permute-start | bytes 1179656 | tf_op jit(solution)/shard_map/ppermute | solution.py:401
  8.9 1.6 %later_pack.1 = (f32[8,256]{1,0:T(8,128)S(1)}, bf16[2,128,768]{2,1,0:T(8,128)(2,1)S(1)}, bf16[2,128,768]{2,1,0:T(8,128)(2,1)S(1)}, bf16[2,128,768]{2,1,0:T(8,128)(2,1)S(1)}, bf16[2,128,768]{2,1,0:T(8,128)(2,1)S(1)}) custom-call(s32[5,32]{1,0:T(8,128)} %bitcast.21, s32[2,8]{1,0:T(2,128)} %partner_in.1, bf16[128,1536]{1,0:T(8,128)(2,1)} %bitcast.14, ...), custom_call_target="tpu_custom_call" | custom-call | tf_op jit(solution)/shard_map/later_pack/pallas_call | solution.py:304
  10.5 0.0 collective-permute-done.n1
  10.5 0.3 collective-permute-start.2
  10.7 0.5 collective-permute-start.1
  11.3 3.7 %collective-permute-done.3.n4 = bf16[2,128,768]{2,1,0:T(8,128)(2,1)S(1)} collective-permute-done((bf16[2,128,768]{2,1,0:T(8,128)(2,1)S(1)}, bf16[2,128,768]{2,1,0:T(8,128)(2,1)S(1)}, u32[]{:S(2)}, u32[]{:S(2)}) %collective-permute-start.3) | collective-permute-done | bytes 393248 | tf_op jit(solution)/shard_map/ppermute | solution.py:401
  15.0 2.0 %collective-permute-start.4 = (bf16[2,128,768]{2,1,0:T(8,128)(2,1)S(1)}, bf16[2,128,768]{2,1,0:T(8,128)(2,1)S(1)}, u32[]{:S(2)}, u32[]{:S(2)}) collective-permute-start(bf16[2,128,768]{2,1,0:T(8,128)(2,1)S(1)} %get-tuple-element.61.kv), channel_id=1, source_target_pairs={{0,1},{4,5},{8,9},{12,13},{16,17},{20,21},{24,25},{28,29},{1,0},{5... | collective-permute-start | bytes 1179656 | tf_op jit(solution)/shard_map/ppermute | solution.py:401
  17.0 0.0 collective-permute-done.6.n2
  17.0 0.0 collective-permute-start.5
  17.0 1.1 %collective-permute-done.7.n3 = bf16[2,128,768]{2,1,0:T(8,128)(2,1)S(1)} collective-permute-done((bf16[2,128,768]{2,1,0:T(8,128)(2,1)S(1)}, bf16[2,128,768]{2,1,0:T(8,128)(2,1)S(1)}, u32[]{:S(2)}, u32[]{:S(2)}) %collective-permute-start.7) | collective-permute-done | bytes 393248 | tf_op jit(solution)/shard_map/ppermute | solution.py:401
  18.0 1.3 %stats.2.mine = f32[24,256]{1,0:T(8,128)S(1)} custom-call(f32[8,256]{1,0:T(8,128)S(1)} %get-tuple-element.64.bias_rows, bf16[2,128,768]{2,1,0:T(8,128)(2,1)S(1)} %collective-permute-done.3.n4, bf16[2,128,768]{2,1,0:T(8,128)(2,1)S(1)} %collective-permute-done.6.n2, bf16[2,128,768]{2,1,0:T(8,128)(2,1)S(1)} %collective-permute-done.7.n3, ...), custom_call_target="tpu_custom_call" | custom-call | tf_op jit(solution)/shard_map/stats/pallas_call | solution.py:191
  19.4 1.4 %collective-permute-start.8 = (f32[24,256]{1,0:T(8,128)S(1)}, f32[24,256]{1,0:T(8,128)S(1)}, u32[]{:S(2)}, u32[]{:S(2)}) collective-permute-start(f32[24,256]{1,0:T(8,128)S(1)} %stats.2.mine), channel_id=1, source_target_pairs={{0,16},{4,20},{8,24},{12,28},{16,0},{20,4},{24,8},{28,12},{1,2},{5... | collective-permute-start | bytes 73736 | tf_op jit(solution)/shard_map/ppermute | solution.py:417
  20.7 2.9 %collective-permute-done.8.theirs = f32[24,256]{1,0:T(8,128)S(1)} collective-permute-done((f32[24,256]{1,0:T(8,128)S(1)}, f32[24,256]{1,0:T(8,128)S(1)}, u32[]{:S(2)}, u32[]{:S(2)}) %collective-permute-start.8) | collective-permute-done | bytes 24608 | tf_op jit(solution)/shard_map/ppermute | solution.py:417
  23.7 2.4 %grads.2 = (f32[128,768]{1,0:T(8,128)S(1)}, f32[128,768]{1,0:T(8,128)S(1)}, f32[128,768]{1,0:T(8,128)S(1)}, f32[128,768]{1,0:T(8,128)S(1)}, bf16[2,128,768]{2,1,...) custom-call(f32[8,256]{1,0:T(8,128)S(1)} %get-tuple-element.64.bias_, ...), custom_call_target="tpu_custom_call" | custom-call | tf_op jit(solution)/shard_map/grads/pallas_call | solution.py:191
  26.0 0.0 collective-permute-done.2.n2
  26.0 0.0 collective-permute-done.1.n4
  26.0 0.0 collective-permute-done.4.n3
  26.1 0.0 collective-permute-done.5.n1
  26.1 1.4 %stats.3.mine = f32[24,256]{1,0:T(8,128)S(1)} custom-call(f32[8,256]{1,0:T(8,128)S(1)} %get-tuple-element.64.bias_rows, bf16[2,128,768]{2,1,0:T(8,128)(2,1)S(1)} %collective-permute-done.1.n4, bf16[2,128,768]{2,1,0:T(8,128)(2,1)S(1)} %collective-permute-done.2.n2, bf16[2,128,768]{2,1,0:T(8,128)(2,1)S(1)} %collective-permute-done.4.n3, ...), custom_call_target="tpu_custom_call" | custom-call | tf_op jit(solution)/shard_map/stats/pallas_call | solution.py:191
  27.4 1.3 %collective-permute-start.13 = (bf16[2,128,768]{2,1,0:T(8,128)(2,1)S(1)}, bf16[2,128,768]{2,1,0:T(8,128)(2,1)S(1)}, u32[]{:S(2)}, u32[]{:S(2)}) collective-permute-start(bf16[2,128,768]{2,1,0:T(8,128)(2,1)S(1)} %get-tuple-element.71), channel_id=1, source_target_pairs={{0,1},{4,5},{8,9},{12,13},{16,17},{20,21},{24,25},{28,29},{1,0},{5... | collective-permute-start | bytes 1179656 | tf_op jit(solution)/shard_map/ppermute | solution.py:401
  28.7 0.0 collective-permute-start.17
  28.7 1.6 %collective-permute-start.16 = (bf16[2,128,768]{2,1,0:T(8,128)(2,1)S(1)}, bf16[2,128,768]{2,1,0:T(8,128)(2,1)S(1)}, u32[]{:S(2)}, u32[]{:S(2)}) collective-permute-start(bf16[2,128,768]{2,1,0:T(8,128)(2,1)S(1)} %get-tuple-element.80), channel_id=1, source_target_pairs={{0,12},{4,8},{8,4},{12,0},{16,28},{20,24},{24,20},{28,16},{1,29},{... | collective-permute-start | bytes 1179656 | tf_op jit(solution)/shard_map/ppermute | solution.py:401
  30.3 1.5 %collective-permute-start.9 = (f32[24,256]{1,0:T(8,128)S(1)}, f32[24,256]{1,0:T(8,128)S(1)}, u32[]{:S(2)}, u32[]{:S(2)}) collective-permute-start(f32[24,256]{1,0:T(8,128)S(1)} %stats.3.mine), channel_id=1, source_target_pairs={{0,16},{4,20},{8,24},{12,28},{16,0},{20,4},{24,8},{28,12},{1,2},{5... | collective-permute-start | bytes 73736 | tf_op jit(solution)/shard_map/ppermute | solution.py:417
  31.9 0.5 collective-permute-start.15
  32.4 1.8 %collective-permute-done.9.theirs = f32[24,256]{1,0:T(8,128)S(1)} collective-permute-done((f32[24,256]{1,0:T(8,128)S(1)}, f32[24,256]{1,0:T(8,128)S(1)}, u32[]{:S(2)}, u32[]{:S(2)}) %collective-permute-start.9) | collective-permute-done | bytes 24608 | tf_op jit(solution)/shard_map/ppermute | solution.py:417
  34.2 2.4 %grads.3 = (f32[128,768]{1,0:T(8,128)S(1)}, f32[128,768]{1,0:T(8,128)S(1)}, f32[128,768]{1,0:T(8,128)S(1)}, f32[128,768]{1,0:T(8,128)S(1)}, bf16[2,128,768]{2,1,...) custom-call(f32[8,256]{1,0:T(8,128)S(1)} %get-tuple-element.64.bias_, ...), custom_call_target="tpu_custom_call" | custom-call | tf_op jit(solution)/shard_map/grads/pallas_call | solution.py:191
  36.5 0.1 collective-permute-start.11
  36.6 1.8 %collective-permute-done.13.b3 = bf16[2,128,768]{2,1,0:T(8,128)(2,1)S(1)} collective-permute-done((bf16[2,128,768]{2,1,0:T(8,128)(2,1)S(1)}, bf16[2,128,768]{2,1,0:T(8,128)(2,1)S(1)}, u32[]{:S(2)}, u32[]{:S(2)}) %collective-permute-start.13) | collective-permute-done | bytes 393248 | tf_op jit(solution)/shard_map/ppermute | solution.py:401
  38.4 1.1 %collective-permute-start.12 = (bf16[2,128,768]{2,1,0:T(8,128)(2,1)S(1)}, bf16[2,128,768]{2,1,0:T(8,128)(2,1)S(1)}, u32[]{:S(2)}, u32[]{:S(2)}) collective-permute-start(bf16[2,128,768]{2,1,0:T(8,128)(2,1)S(1)} %get-tuple-element.68), channel_id=1, source_target_pairs={{0,1},{4,5},{8,9},{12,13},{16,17},{20,21},{24,25},{28,29},{1,0},{5... | collective-permute-start | bytes 1179656 | tf_op jit(solution)/shard_map/ppermute | solution.py:401
  39.5 0.0 collective-permute-done.17.b1
  39.5 0.0 collective-permute-start.14
  39.5 0.3 collective-permute-done.16.b2
  39.8 1.5 %collective-permute-start.10 = (bf16[2,128,768]{2,1,0:T(8,128)(2,1)S(1)}, bf16[2,128,768]{2,1,0:T(8,128)(2,1)S(1)}, u32[]{:S(2)}, u32[]{:S(2)}) collective-permute-start(bf16[2,128,768]{2,1,0:T(8,128)(2,1)S(1)} %get-tuple-element.66), channel_id=1, source_target_pairs={{0,16},{4,20},{8,24},{12,28},{16,0},{20,4},{24,8},{28,12},{1,2},{5... | collective-permute-start | bytes 1179656 | tf_op jit(solution)/shard_map/ppermute | solution.py:401
  41.3 1.1 %early_finish.2 = (bf16[128,1536]{1,0:T(8,128)(2,1)}, bf16[128,1536]{1,0:T(8,128)(2,1)}, bf16[128,1536]{1,0:T(8,128)(2,1)}, bf16[128,1536]{1,0:T(8,128)(2,1)}, f32[2,128,768]{2,1,0:T(8,128)S(1)}) custom-call(bf16[2,128,768]{2,1,0:T(8,128)(2,1)S(1)} %collective-permute-done.16.b2, bf16[2,128,768]{2,1,0:T(8,128)(2,1)S(1)} %collective-permute-done.13.b3, ...), custom_call_target="tpu_custom_call" | custom-call | tf_op jit(solution)/shard_map/early_finish/pallas_call | solution.py:370
  42.4 0.2 collective-permute-done.15.b4
  42.6 0.9 %late_finish.2 = (bf16[128,1536]{1,0:T(8,128)(2,1)}, bf16[128,1536]{1,0:T(8,128)(2,1)}, bf16[128,1536]{1,0:T(8,128)(2,1)}, bf16[128,1536]{1,0:T(8,128)(2,1)}) custom-call(bf16[2,128,768]{2,1,0:T(8,128)(2,1)S(1)} %collective-permute-done.15.b4, ...), custom_call_target="tpu_custom_call", output_to_operand_aliasing={{0}: (2, {}), {1}: (3, {}), {2}: (4, {}), {3}: (5, {})} | custom-call | tf_op jit(solution)/shard_map/late_finish/pallas_call | solution.py:370
  43.5 4.6 %collective-permute-done.11.b2 = bf16[2,128,768]{2,1,0:T(8,128)(2,1)S(1)} collective-permute-done((bf16[2,128,768]{2,1,0:T(8,128)(2,1)S(1)}, bf16[2,128,768]{2,1,0:T(8,128)(2,1)S(1)}, u32[]{:S(2)}, u32[]{:S(2)}) %collective-permute-start.11) | collective-permute-done | bytes 393248 | tf_op jit(solution)/shard_map/ppermute | solution.py:401
  48.1 0.3 collective-permute-done.12.b3
  48.4 0.0 collective-permute-done.14.b1
  48.4 1.1 %early_finish.3 = (bf16[128,1536]{1,0:T(8,128)(2,1)}, bf16[128,1536]{1,0:T(8,128)(2,1)}, bf16[128,1536]{1,0:T(8,128)(2,1)}, bf16[128,1536]{1,0:T(8,128)(2,1)}, f32[2,128,768]{2,1,0:T(8,128)S(1)}) custom-call(bf16[2,128,768]{2,1,0:T(8,128)(2,1)S(1)} %collective-permute-done.11.b2, ...), custom_call_target="tpu_custom_call", output_to_operand_aliasing={{0}: (7, {}), {1}: (8, {}), {2}: (9, {}), {3}: (10, {})} | custom-call | tf_op jit(solution)/shard_map/early_finish/pallas_call | solution.py:370
  49.5 2.3 %collective-permute-done.10.b4 = bf16[2,128,768]{2,1,0:T(8,128)(2,1)S(1)} collective-permute-done((bf16[2,128,768]{2,1,0:T(8,128)(2,1)S(1)}, bf16[2,128,768]{2,1,0:T(8,128)(2,1)S(1)}, u32[]{:S(2)}, u32[]{:S(2)}) %collective-permute-start.10) | collective-permute-done | bytes 393248 | tf_op jit(solution)/shard_map/ppermute | solution.py:401
  51.8 0.9 %late_finish.3 = (bf16[128,1536]{1,0:T(8,128)(2,1)}, bf16[128,1536]{1,0:T(8,128)(2,1)}, bf16[128,1536]{1,0:T(8,128)(2,1)}, bf16[128,1536]{1,0:T(8,128)(2,1)}) custom-call(bf16[2,128,768]{2,1,0:T(8,128)(2,1)S(1)} %collective-permute-done.10.b4, ...), custom_call_target="tpu_custom_call", output_to_operand_aliasing={{0}: (2, {}), {1}: (3, {}), {2}: (4, {}), {3}: (5, {})} | custom-call | tf_op jit(solution)/shard_map/late_finish/pallas_call | solution.py:370
Async XLA Ops:
  1.9 8.6 %collective-permute-start = (bf16[2,128,768]{2,1,0:T(8,128)(2,1)S(1)}, bf16[2,128,768]{2,1,0:T(8,128)(2,1)S(1)}, u32[]{:S(2)}, u32[]{:S(2)}) collective-permute-start(bf16[2,128,768]{2,1,0:T(8,128)(2,1)S(1)} %get-tuple-element.56.kv), channel_id=1, source_target_pairs={{0,4},{4,0},{8,12},{12,8},{16,20},{20,16},{24,28},{28,24},{1,5},{5... | collective-permute-start | bytes 1179656 | tf_op jit(solution)/shard_map/ppermute | solution.py:401
  2.4 12.6 %collective-permute-start.3 = (bf16[2,128,768]{2,1,0:T(8,128)(2,1)S(1)}, bf16[2,128,768]{2,1,0:T(8,128)(2,1)S(1)}, u32[]{:S(2)}, u32[]{:S(2)}) collective-permute-start(bf16[2,128,768]{2,1,0:T(8,128)(2,1)S(1)} %get-tuple-element.60), channel_id=1, source_target_pairs={{0,16},{4,20},{8,24},{12,28},{16,0},{20,4},{24,8},{28,12},{1,2},{5... | collective-permute-start | bytes 1179656 | tf_op jit(solution)/shard_map/ppermute | solution.py:401
  5.0 12.0 %collective-permute-start.6 = (bf16[2,128,768]{2,1,0:T(8,128)(2,1)S(1)}, bf16[2,128,768]{2,1,0:T(8,128)(2,1)S(1)}, u32[]{:S(2)}, u32[]{:S(2)}) collective-permute-start(bf16[2,128,768]{2,1,0:T(8,128)(2,1)S(1)} %get-tuple-element.56.kv), channel_id=1, source_target_pairs={{0,12},{4,8},{8,4},{12,0},{16,28},{20,24},{24,20},{28,16},{1,29},{... | collective-permute-start | bytes 1179656 | tf_op jit(solution)/shard_map/ppermute | solution.py:401
  6.3 11.8 %collective-permute-start.7 = (bf16[2,128,768]{2,1,0:T(8,128)(2,1)S(1)}, bf16[2,128,768]{2,1,0:T(8,128)(2,1)S(1)}, u32[]{:S(2)}, u32[]{:S(2)}) collective-permute-start(bf16[2,128,768]{2,1,0:T(8,128)(2,1)S(1)} %get-tuple-element.56.kv), channel_id=1, source_target_pairs={{0,1},{4,5},{8,9},{12,13},{16,17},{20,21},{24,25},{28,29},{1,0},{5... | collective-permute-start | bytes 1179656 | tf_op jit(solution)/shard_map/ppermute | solution.py:401
  10.5 15.6 %collective-permute-start.2 = (bf16[2,128,768]{2,1,0:T(8,128)(2,1)S(1)}, bf16[2,128,768]{2,1,0:T(8,128)(2,1)S(1)}, u32[]{:S(2)}, u32[]{:S(2)}) collective-permute-start(bf16[2,128,768]{2,1,0:T(8,128)(2,1)S(1)} %get-tuple-element.61.kv), channel_id=1, source_target_pairs={{0,12},{4,8},{8,4},{12,0},{16,28},{20,24},{24,20},{28,16},{1,29},{... | collective-permute-start | bytes 1179656 | tf_op jit(solution)/shard_map/ppermute | solution.py:401
  10.7 15.3 %collective-permute-start.1 = (bf16[2,128,768]{2,1,0:T(8,128)(2,1)S(1)}, bf16[2,128,768]{2,1,0:T(8,128)(2,1)S(1)}, u32[]{:S(2)}, u32[]{:S(2)}) collective-permute-start(bf16[2,128,768]{2,1,0:T(8,128)(2,1)S(1)} %get-tuple-element.57), channel_id=1, source_target_pairs={{0,16},{4,20},{8,24},{12,28},{16,0},{20,4},{24,8},{28,12},{1,2},{5... | collective-permute-start | bytes 1179656 | tf_op jit(solution)/shard_map/ppermute | solution.py:401
  15.0 11.1 %collective-permute-start.4 = (bf16[2,128,768]{2,1,0:T(8,128)(2,1)S(1)}, bf16[2,128,768]{2,1,0:T(8,128)(2,1)S(1)}, u32[]{:S(2)}, u32[]{:S(2)}) collective-permute-start(bf16[2,128,768]{2,1,0:T(8,128)(2,1)S(1)} %get-tuple-element.61.kv), channel_id=1, source_target_pairs={{0,1},{4,5},{8,9},{12,13},{16,17},{20,21},{24,25},{28,29},{1,0},{5... | collective-permute-start | bytes 1179656 | tf_op jit(solution)/shard_map/ppermute | solution.py:401
  17.0 9.1 %collective-permute-start.5 = (bf16[2,128,768]{2,1,0:T(8,128)(2,1)S(1)}, bf16[2,128,768]{2,1,0:T(8,128)(2,1)S(1)}, u32[]{:S(2)}, u32[]{:S(2)}) collective-permute-start(bf16[2,128,768]{2,1,0:T(8,128)(2,1)S(1)} %get-tuple-element.61.kv), channel_id=1, source_target_pairs={{0,4},{4,0},{8,12},{12,8},{16,20},{20,16},{24,28},{28,24},{1,5},{5... | collective-permute-start | bytes 1179656 | tf_op jit(solution)/shard_map/ppermute | solution.py:401
  19.4 4.3 %collective-permute-start.8 = (f32[24,256]{1,0:T(8,128)S(1)}, f32[24,256]{1,0:T(8,128)S(1)}, u32[]{:S(2)}, u32[]{:S(2)}) collective-permute-start(f32[24,256]{1,0:T(8,128)S(1)} %stats.2.mine), channel_id=1, source_target_pairs={{0,16},{4,20},{8,24},{12,28},{16,0},{20,4},{24,8},{28,12},{1,2},{5... | collective-permute-start | bytes 73736 | tf_op jit(solution)/shard_map/ppermute | solution.py:417
  27.4 10.9 %collective-permute-start.13 = (bf16[2,128,768]{2,1,0:T(8,128)(2,1)S(1)}, bf16[2,128,768]{2,1,0:T(8,128)(2,1)S(1)}, u32[]{:S(2)}, u32[]{:S(2)}) collective-permute-start(bf16[2,128,768]{2,1,0:T(8,128)(2,1)S(1)} %get-tuple-element.71), channel_id=1, source_target_pairs={{0,1},{4,5},{8,9},{12,13},{16,17},{20,21},{24,25},{28,29},{1,0},{5... | collective-permute-start | bytes 1179656 | tf_op jit(solution)/shard_map/ppermute | solution.py:401
  28.7 10.8 %collective-permute-start.17 = (bf16[2,128,768]{2,1,0:T(8,128)(2,1)S(1)}, bf16[2,128,768]{2,1,0:T(8,128)(2,1)S(1)}, u32[]{:S(2)}, u32[]{:S(2)}) collective-permute-start(bf16[2,128,768]{2,1,0:T(8,128)(2,1)S(1)} %get-tuple-element.82), channel_id=1, source_target_pairs={{0,4},{4,0},{8,12},{12,8},{16,20},{20,16},{24,28},{28,24},{1,5},{5... | collective-permute-start | bytes 1179656 | tf_op jit(solution)/shard_map/ppermute | solution.py:401
  28.7 11.1 %collective-permute-start.16 = (bf16[2,128,768]{2,1,0:T(8,128)(2,1)S(1)}, bf16[2,128,768]{2,1,0:T(8,128)(2,1)S(1)}, u32[]{:S(2)}, u32[]{:S(2)}) collective-permute-start(bf16[2,128,768]{2,1,0:T(8,128)(2,1)S(1)} %get-tuple-element.80), channel_id=1, source_target_pairs={{0,12},{4,8},{8,4},{12,0},{16,28},{20,24},{24,20},{28,16},{1,29},{... | collective-permute-start | bytes 1179656 | tf_op jit(solution)/shard_map/ppermute | solution.py:401
  30.3 3.8 %collective-permute-start.9 = (f32[24,256]{1,0:T(8,128)S(1)}, f32[24,256]{1,0:T(8,128)S(1)}, u32[]{:S(2)}, u32[]{:S(2)}) collective-permute-start(f32[24,256]{1,0:T(8,128)S(1)} %stats.3.mine), channel_id=1, source_target_pairs={{0,16},{4,20},{8,24},{12,28},{16,0},{20,4},{24,8},{28,12},{1,2},{5... | collective-permute-start | bytes 73736 | tf_op jit(solution)/shard_map/ppermute | solution.py:417
  31.9 10.7 %collective-permute-start.15 = (bf16[2,128,768]{2,1,0:T(8,128)(2,1)S(1)}, bf16[2,128,768]{2,1,0:T(8,128)(2,1)S(1)}, u32[]{:S(2)}, u32[]{:S(2)}) collective-permute-start(bf16[2,128,768]{2,1,0:T(8,128)(2,1)S(1)} %get-tuple-element.78), channel_id=1, source_target_pairs={{0,16},{4,20},{8,24},{12,28},{16,0},{20,4},{24,8},{28,12},{1,2},{5... | collective-permute-start | bytes 1179656 | tf_op jit(solution)/shard_map/ppermute | solution.py:401
  36.5 11.5 %collective-permute-start.11 = (bf16[2,128,768]{2,1,0:T(8,128)(2,1)S(1)}, bf16[2,128,768]{2,1,0:T(8,128)(2,1)S(1)}, u32[]{:S(2)}, u32[]{:S(2)}) collective-permute-start(bf16[2,128,768]{2,1,0:T(8,128)(2,1)S(1)} %get-tuple-element.67), channel_id=1, source_target_pairs={{0,12},{4,8},{8,4},{12,0},{16,28},{20,24},{24,20},{28,16},{1,29},{... | collective-permute-start | bytes 1179656 | tf_op jit(solution)/shard_map/ppermute | solution.py:401
  38.4 10.0 %collective-permute-start.12 = (bf16[2,128,768]{2,1,0:T(8,128)(2,1)S(1)}, bf16[2,128,768]{2,1,0:T(8,128)(2,1)S(1)}, u32[]{:S(2)}, u32[]{:S(2)}) collective-permute-start(bf16[2,128,768]{2,1,0:T(8,128)(2,1)S(1)} %get-tuple-element.68), channel_id=1, source_target_pairs={{0,1},{4,5},{8,9},{12,13},{16,17},{20,21},{24,25},{28,29},{1,0},{5... | collective-permute-start | bytes 1179656 | tf_op jit(solution)/shard_map/ppermute | solution.py:401
  39.5 8.9 %collective-permute-start.14 = (bf16[2,128,768]{2,1,0:T(8,128)(2,1)S(1)}, bf16[2,128,768]{2,1,0:T(8,128)(2,1)S(1)}, u32[]{:S(2)}, u32[]{:S(2)}) collective-permute-start(bf16[2,128,768]{2,1,0:T(8,128)(2,1)S(1)} %get-tuple-element.72), channel_id=1, source_target_pairs={{0,4},{4,0},{8,12},{12,8},{16,20},{20,16},{24,28},{28,24},{1,5},{5... | collective-permute-start | bytes 1179656 | tf_op jit(solution)/shard_map/ppermute | solution.py:401
  39.8 12.0 %collective-permute-start.10 = (bf16[2,128,768]{2,1,0:T(8,128)(2,1)S(1)}, bf16[2,128,768]{2,1,0:T(8,128)(2,1)S(1)}, u32[]{:S(2)}, u32[]{:S(2)}) collective-permute-start(bf16[2,128,768]{2,1,0:T(8,128)(2,1)S(1)} %get-tuple-element.66), channel_id=1, source_target_pairs={{0,16},{4,20},{8,24},{12,28},{16,0},{20,4},{24,8},{28,12},{1,2},{5... | collective-permute-start | bytes 1179656 | tf_op jit(solution)/shard_map/ppermute | solution.py:401
